TPU v7x, 32 devices: a whole 2x2x4 slice. The times are simulated.
32 devices in a mesh: gy: 4 (over x, core), gz: 8 (over z, y).
Axes of the slice: x: 2, y: 2, z: 4, core: 2. Of those that a mesh axis runs over, the one named last changes fastest.
Arguments:
- offsets: float32 [3, 262144], P(None, ('gy', 'gz')), may hold values from 0 to 1
- masses: float32 [262144], P(('gy', 'gz')), may hold values from 0.25 to 4
- velocities: float32 [3, 262144], P(None, ('gy', 'gz')), may hold values from -5 to 5
- destination: int32 [262144, 1], P(('gy', 'gz')), may hold values from 0 to 31; in each aligned block of 8192 rows (0 to 8191, 8192 to 16383, ...) at most 512 rows name the same one
- first_weight: bfloat16 [16, 4, 3, 3, 3], replicated, may hold values from -0.625 to 0.625
- first_bias: float32 [16], replicated, may hold values from -3 to 3
- second_weight: bfloat16 [16, 16, 3, 3, 3], replicated, may hold values from -0.3125 to 0.3125
- second_bias: float32 [16], replicated, may hold values from -3 to 3
- cotangent: bfloat16 [16, 32, 64, 128], P(None, 'gy', 'gz'), may hold values from -6 to 6
Outputs:
- refined: bfloat16 [16, 32, 64, 128], P(None, 'gy', 'gz')
- grad_field: float32 [4, 32, 64, 128], P(None, 'gy', 'gz')
- grad_first_weight: float32 [16, 4, 3, 3, 3], replicated
- grad_first_bias: float32 [16], replicated
- grad_second_weight: float32 [16, 16, 3, 3, 3], replicated
- grad_second_bias: float32 [16], replicated
Inputs may be any that keep to these rules, and one draw needn't show every extreme that they name: `destination`: in the rows of one device (aligned blocks of 8192 rows) no block number is named by more than 512 rows, and some block number is named by exactly 512.
All inputs are finite; a program needn't handle non-finite values.
Results may differ from a plain program's by a relative error of at most 0.009.
Values may be sent and summed in bfloat16 or wider, within the bound.
No kernel may reach another device: no remote copies, remote signals or barrier semaphores. Data moves between devices by JAX's collectives and lax.ppermute only.
A program may use at most 192 MiB of HBM per device.

v0:
```python
import math

import jax
import jax.numpy as jnp
from jax import lax
from jax.sharding import PartitionSpec as P


def extended_2(cells, sides, width):
    for axis, dim in sides:
        count = lax.axis_size(axis)
        ends = count - 1
        head = lax.slice_in_dim(cells, 0, width, axis=dim)
        tail = lax.slice_in_dim(cells, cells.shape[dim] - width, cells.shape[dim], axis=dim)
        cells = jnp.concatenate(
            [
                lax.ppermute(tail, axis, [(i, (i + 1) % count) for i in range(ends)]),
                cells,
                lax.ppermute(head, axis, [((i + 1) % count, i) for i in range(ends)]),
            ],
            axis=dim,
        )
    return cells


def cell_split(coord, span):
    position = coord * span
    cell = jnp.minimum(jnp.floor(position).astype(jnp.int32), span - 1)
    frac = position - cell.astype(position.dtype)
    return (cell, frac)


def deposit_local(arrived, span_y, span_z, span_x):
    cell_y, frac_y = cell_split(arrived[0], span_y)
    cell_z, frac_z = cell_split(arrived[1], span_z)
    cell_x, frac_x = cell_split(arrived[2], span_x)
    charges = jnp.concatenate([arrived[3:4], arrived[3:4] * arrived[4:7]], axis=0)
    grid_y, grid_z, grid_x = (span_y + 1, span_z + 1, span_x + 1)
    total = jnp.zeros((charges.shape[0], grid_y * grid_z * grid_x), jnp.float32)
    for step_y in range(2):
        weight_y = frac_y if step_y else 1.0 - frac_y
        for step_z in range(2):
            weight_z = frac_z if step_z else 1.0 - frac_z
            for step_x in range(2):
                weight_x = frac_x if step_x else 1.0 - frac_x
                index = ((cell_y + step_y) * grid_z + (cell_z + step_z)) * grid_x + cell_x + step_x
                total = total.at[:, index].add(charges * (weight_y * weight_z * weight_x)[None, :])
    return total.reshape(charges.shape[0], grid_y, grid_z, grid_x)[:, :, :, :span_x]


def fold_rims(wide, axis_dim, span):

    def window_of(start, stop):
        return lax.slice_in_dim(wide, start, stop, axis=axis_dim)

    return jnp.concatenate(
        [
            window_of(0, 1),
            window_of(1, 2) + window_of(2, 3),
            window_of(3, span + 2),
            window_of(span + 2, span + 3) + window_of(span + 3, span + 4),
        ],
        axis=axis_dim,
    )


def conv_rims(field):
    return extended_2(field, (("gy", 1), ("gz", 2)), 1)


def pad_depth(field):
    return jnp.pad(field, ((0, 0), (0, 0), (0, 0), (1, 1)))


def conv_valid(source_ext, kernel):
    source_pad = pad_depth(source_ext)
    out_y = source_pad.shape[1] - 2
    out_z = source_pad.shape[2] - 2
    out_x = source_pad.shape[3] - 2
    result = jnp.zeros((kernel.shape[0], out_y, out_z, out_x), jnp.float32)
    for shift_y in range(3):
        for shift_z in range(3):
            for shift_x in range(3):
                window = source_pad[
                    :,
                    shift_y : shift_y + out_y,
                    shift_z : shift_z + out_z,
                    shift_x : shift_x + out_x,
                ]
                result = result + jnp.einsum(
                    "oc,cyzx->oyzx",
                    kernel[:, :, shift_y, shift_z, shift_x],
                    window,
                    preferred_element_type=jnp.float32,
                )
    return result


def flipped(kernel):
    return jnp.flip(kernel, (2, 3, 4)).transpose(1, 0, 2, 3, 4)


def dsilu(value):
    sig = jax.nn.sigmoid(value)
    return sig * (1.0 + value * (1.0 - sig))


def tap_products(delta, source_ext):
    source_pad = pad_depth(source_ext)
    span_y, span_z, span_x = (delta.shape[1], delta.shape[2], delta.shape[3])
    planes = []
    for shift_y in range(3):
        rows_out = []
        for shift_z in range(3):
            cols_out = []
            for shift_x in range(3):
                window = source_pad[
                    :,
                    shift_y : shift_y + span_y,
                    shift_z : shift_z + span_z,
                    shift_x : shift_x + span_x,
                ]
                cols_out.append(
                    jnp.einsum("oyzx,cyzx->oc", delta, window, preferred_element_type=jnp.float32)
                )
            rows_out.append(jnp.stack(cols_out, axis=-1))
        planes.append(jnp.stack(rows_out, axis=-2))
    return jnp.stack(planes, axis=-3)


def local(
    offsets,
    masses,
    velocities,
    destination,
    first_weight,
    first_bias,
    second_weight,
    second_bias,
    cotangent,
):
    count_y = lax.axis_size("gy")
    count_z = lax.axis_size("gz")
    devices = count_y * count_z
    particle_count = masses.shape[0]
    capacity = 2 * particle_count // devices
    span_y, span_z, span_x = (cotangent.shape[1], cotangent.shape[2], cotangent.shape[3])
    target = destination[:, 0]
    order = jnp.argsort(target, stable=True)
    sorted_target = target[order]
    starts = jnp.searchsorted(sorted_target, jnp.arange(devices, dtype=jnp.int32))
    ranked = jnp.arange(particle_count, dtype=jnp.int32) - starts[sorted_target]
    column = sorted_target * capacity + ranked
    filler = jnp.zeros((1, particle_count), jnp.float32)
    payload = jnp.concatenate([offsets, masses[None, :], velocities, filler], axis=0)[:, order]
    outgoing = jnp.zeros((8, devices * capacity), jnp.float32).at[:, column].set(payload)
    arrived = lax.all_to_all(
        outgoing.reshape(8, devices, capacity),
        ("gy", "gz"),
        split_axis=1,
        concat_axis=1,
        tiled=True,
    )
    arrived = arrived.reshape(8, devices * capacity)
    extended = deposit_local(arrived, span_y, span_z, span_x)
    wide = extended_2(extended, (("gy", 1), ("gz", 2)), 2)
    folded = fold_rims(fold_rims(wide, 1, span_y), 2, span_z)
    keep_y = (lax.axis_index("gy") < count_y - 1).astype(jnp.float32)
    keep_z = (lax.axis_index("gz") < count_z - 1).astype(jnp.float32)
    folded = jnp.concatenate([folded[:, : span_y + 1], folded[:, span_y + 1 :] * keep_y], axis=1)
    folded = jnp.concatenate(
        [folded[:, :, : span_z + 1], folded[:, :, span_z + 1 :] * keep_z], axis=2
    )
    folded_ext = folded.astype(jnp.bfloat16)
    pre_one = conv_valid(folded_ext, first_weight) + first_bias[:, None, None, None]
    active = jax.nn.silu(pre_one).astype(jnp.bfloat16)
    active_ext = conv_rims(active)
    pre_two = conv_valid(active_ext, second_weight) + second_bias[:, None, None, None]
    refined = jax.nn.silu(pre_two).astype(jnp.bfloat16)
    delta_two = (cotangent.astype(jnp.float32) * dsilu(pre_two)).astype(jnp.bfloat16)
    delta_two_ext = conv_rims(delta_two)
    back_one = conv_valid(delta_two_ext, flipped(second_weight))
    delta_one = (back_one * dsilu(pre_one)).astype(jnp.bfloat16)
    delta_one_ext = conv_rims(delta_one)
    grad_field = conv_valid(delta_one_ext, flipped(first_weight))
    second_terms = tap_products(delta_two, active_ext)
    second_bias_terms = jnp.sum(delta_two, axis=(1, 2, 3), dtype=jnp.float32)
    first_terms = tap_products(delta_one, folded_ext)
    first_bias_terms = jnp.sum(delta_one, axis=(1, 2, 3), dtype=jnp.float32)
    totals = lax.psum(
        (first_terms, first_bias_terms, second_terms, second_bias_terms), ("gy", "gz")
    )
    scale = 1.0 / math.sqrt(span_y * span_z * span_x * devices)
    return (
        refined,
        grad_field,
        totals[0] * scale,
        totals[1] * scale,
        totals[2] * scale,
        totals[3] * scale,
    )


def solution(mesh):
    placed = (
        P(None, ("gy", "gz")),
        P(("gy", "gz")),
        P(None, ("gy", "gz")),
        P(("gy", "gz"), None),
        P(),
        P(),
        P(),
        P(),
        P(None, "gy", "gz", None),
    )
    return jax.shard_map(
        local,
        mesh=mesh,
        in_specs=placed,
        out_specs=(P(None, "gy", "gz", None), P(None, "gy", "gz", None), P(), P(), P(), P()),
        check_vma=False,
    )
```

profile of v0, /device:TPU:0, one launch (start us, length us, event | category | flops | bytes accessed | tf_op | source)
XLA Modules:
  0.0 1246.3 jit_solution(1879208767363110317)
XLA Ops:
  0.7 7.6 sort.17
  8.3 45.5 %gather_fusion.1 = s32[8192]{0:T(1024)S(1)} fusion(s32[8192]{0:T(1024)S(1)} %bitcast.1453, s32[8192]{0:T(1024)S(1)} %fusion.215), kind=kCustom, calls=%fused_computation.1 | custom fusion | bytes 98304 | tf_op jit(solution)/shard_map/gather | solution.py:150
  53.8 10.5 while.24
  72.9 15.7 %select_select_fusion = s32[8192]{0:T(1024)S(1)} fusion(pred[8192]{0:T(1024)(128)(4,1)S(1)} %get-tuple-element.133, pred[8192]{0:T(1024)(128)(4,1)S(1)} %get-tuple-element.132, pred[8192]{0:T(1024)(128)(4,1)S(1)} %get-tuple-element.131, pred[8192]{0:T(1024)(128)(4,1)S(1)} %get-tuple-element.130, pred[8192]{0:T(1024)(128)(4,1)S(1)} %get-tuple-element.129, ...), kind=kLoop, calls=%fused_computation.519 | loop fusion | flops 204800 | bytes 270436 | tf_op jit(solution)/shard_map/gather | solution.py:152
  91.5 70.3 %scatter_custom_fusion = f32[8,16384]{0,1:T(8,128)} fusion(s32[8192]{0:T(1024)S(1)} %bitcast.1479, f32[8,8192]{0,1:T(8,128)} %copy.35, s32[8192]{0:T(1024)S(1)} %fusion.215, f32[]{:T(128)} %constant.32.clone.1), kind=kCustom, calls=%fused_computation.20 | custom fusion | bytes 524800 | tf_op jit(solution)/shard_map/scatter | solution.py:156
  161.8 5.2 copy.36
  167.0 23.5 %all_to_all.5 = f32[8,32,512]{2,0,1:T(8,128)S(1)} all-to-all(f32[8,32,512]{2,0,1:T(8,128)S(1)} %copy.36), channel_id=1, replica_groups=mesh['gy'=4,'gz'=8] {'gy','gz'}, dimensions={1} | all-to-all | bytes 1048576 | tf_op jit(solution)/shard_map/all_to_all | solution.py:157
  191.1 5.0 copy.37
  211.5 5.1 copy.41
  216.6 5.0 copy.42
  221.6 5.1 copy.43
  226.7 5.0 copy.44
  232.8 106.5 %scatter_custom_fusion.1 = f32[4,10449]{0,1:T(8,128)} fusion(s32[16384]{0:T(1024)S(1)} %bitcast.1477, f32[16384,4]{1,0:T(8,128)} %copy.37, f32[]{:T(128)} %constant.32.clone.1), kind=kCustom, calls=%fused_computation.23 | custom fusion | flops 65536 | bytes 167696 | tf_op jit(solution)/shard_map/scatter-add | solution.py:47
  339.4 105.8 %scatter_fusion = f32[4,10449]{0,1:T(8,128)} fusion(f32[4,10449]{0,1:T(8,128)} %scatter_custom_fusion.1, s32[16384]{0:T(1024)S(1)} %bitcast.1464, f32[16384,4]{1,0:T(8,128)} %copy.38), kind=kCustom, calls=%fused_computation.5 | custom fusion | flops 65536 | bytes 851968 | tf_op jit(solution)/shard_map/scatter-add | solution.py:47
  445.3 105.5 %scatter_fusion.1 = f32[4,10449]{0,1:T(8,128)} fusion(f32[4,10449]{0,1:T(8,128)} %scatter_fusion, s32[16384]{0:T(1024)S(1)} %bitcast.1467, f32[16384,4]{1,0:T(8,128)} %copy.39), kind=kCustom, calls=%fused_computation.6 | custom fusion | flops 65536 | bytes 851968 | tf_op jit(solution)/shard_map/scatter-add | solution.py:47
  550.7 105.5 %scatter_fusion.2 = f32[4,10449]{0,1:T(8,128)} fusion(f32[4,10449]{0,1:T(8,128)} %scatter_fusion.1, s32[16384]{0:T(1024)S(1)} %bitcast.1463, f32[16384,4]{1,0:T(8,128)} %copy.40), kind=kCustom, calls=%fused_computation.7 | custom fusion | flops 65536 | bytes 851968 | tf_op jit(solution)/shard_map/scatter-add | solution.py:47
  656.2 105.5 %scatter_fusion.3 = f32[4,10449]{0,1:T(8,128)} fusion(f32[4,10449]{0,1:T(8,128)} %scatter_fusion.2, s32[16384]{0:T(1024)S(1)} %bitcast.1466, f32[16384,4]{1,0:T(8,128)} %copy.41), kind=kCustom, calls=%fused_computation.8 | custom fusion | flops 65536 | bytes 851968 | tf_op jit(solution)/shard_map/scatter-add | solution.py:47
  761.6 105.5 %scatter_fusion.4 = f32[4,10449]{0,1:T(8,128)} fusion(f32[4,10449]{0,1:T(8,128)} %scatter_fusion.3, s32[16384]{0:T(1024)S(1)} %bitcast.1462, f32[16384,4]{1,0:T(8,128)} %copy.42), kind=kCustom, calls=%fused_computation.9 | custom fusion | flops 65536 | bytes 851968 | tf_op jit(solution)/shard_map/scatter-add | solution.py:47
  867.1 105.6 %scatter_fusion.5 = f32[4,10449]{0,1:T(8,128)} fusion(f32[4,10449]{0,1:T(8,128)} %scatter_fusion.4, s32[16384]{0:T(1024)S(1)} %bitcast.1465, f32[16384,4]{1,0:T(8,128)} %copy.43), kind=kCustom, calls=%fused_computation.10 | custom fusion | flops 65536 | bytes 851968 | tf_op jit(solution)/shard_map/scatter-add | solution.py:47
  972.7 105.5 %scatter_fusion.6 = f32[4,10449]{0,1:T(8,128)} fusion(f32[4,10449]{0,1:T(8,128)} %scatter_fusion.5, s32[16384]{0:T(1024)S(1)} %bitcast.1461, f32[16384,4]{1,0:T(8,128)} %copy.44), kind=kCustom, calls=%fused_computation.11 | custom fusion | flops 65536 | bytes 851968 | tf_op jit(solution)/shard_map/scatter-add | solution.py:47
  1082.1 16.0 %collective-permute-start = (f32[4,2,9,128]{3,0,2,1:T(4,128)S(1)}, f32[4,2,9,128]{3,0,2,1:T(4,128)S(1)}, u32[]{:S(2)}, u32[]{:S(2)}) collective-permute-start(f32[4,2,9,128]{3,0,2,1:T(4,128)S(1)} %copy.215), channel_id=1, source_target_pairs={{0,8},{8,16},{16,24},{1,9},{9,17},{17,25},{2,10},{10,18},{18,26},{... | collective-permute-start | bytes 110600 | tf_op jit(solution)/shard_map/ppermute | solution.py:17
  1151.3 5.4 collective-permute-start.10
  1173.0 5.3 collective-permute-start.12
  1178.6 51.4 %all-reduce.4 = (f32[16,4,3,3,3]{0,1,4,3,2:T(4,128)S(1)}, f32[16]{0:T(128)S(1)}, f32[16,16,3,3,3]{1,0,4,3,2:T(8,128)S(1)}, f32[16]{0:T(128)S(1)}) all-reduce(f32[16,4,3,3,3]{0,1,4,3,2:T(4,128)S(1)} %pad_maximum_fusion.19, f32[16]{0:T(128)S(1)} %get-tuple-element.252, ...), channel_id=1, replica_groups=mesh['gy'=4,'gz'=8] {'gy','gz'}, use_global_device_ids=true, to_apply=%region_12.13 | all-reduce | flops 8672 | bytes 69376 | tf_op jit(solution)/shard_map/psum | solution.py:190
  (360 shorter events, 126.9 us)
Async XLA Ops:
  0.6 7.6 copy-start
  8.2 80.5 %copy-start.2 = (f32[3,8192]{1,0:T(4,128)S(1)}, f32[3,8192]{1,0:T(4,128)}, u32[]{:S(2)}) copy-start(f32[3,8192]{1,0:T(4,128)} %param.13) | copy-start | bytes 294916
  8.3 80.5 %copy-start.3 = (f32[3,8192]{1,0:T(4,128)S(1)}, f32[3,8192]{1,0:T(4,128)}, u32[]{:S(2)}) copy-start(f32[3,8192]{1,0:T(4,128)} %param.11) | copy-start | bytes 294916
  8.3 80.5 %copy-start.5 = (f32[8192]{0:T(1024)S(1)}, f32[8192]{0:T(1024)}, u32[]{:S(2)}) copy-start(f32[8192]{0:T(1024)} %param.12) | copy-start | bytes 98308
  972.7 134.4 %copy-start.1 = (bf16[16,16,3,3,3]{1,0,4,3,2:T(8,128)(2,1)S(1)}, bf16[16,16,3,3,3]{1,0,4,3,2:T(8,128)(2,1)}, u32[]{:S(2)}) copy-start(bf16[16,16,3,3,3]{1,0,4,3,2:T(8,128)(2,1)} %param.17) | copy-start | bytes 41476
  1078.2 31.1 %copy-start.4 = (bf16[16,4,3,3,3]{0,1,4,3,2:T(4,128)(2,1)S(1)}, bf16[16,4,3,3,3]{0,1,4,3,2:T(4,128)(2,1)}, u32[]{:S(2)}) copy-start(bf16[16,4,3,3,3]{0,1,4,3,2:T(4,128)(2,1)} %param.15) | copy-start | bytes 10372
  1082.1 17.4 %collective-permute-start = (f32[4,2,9,128]{3,0,2,1:T(4,128)S(1)}, f32[4,2,9,128]{3,0,2,1:T(4,128)S(1)}, u32[]{:S(2)}, u32[]{:S(2)}) collective-permute-start(f32[4,2,9,128]{3,0,2,1:T(4,128)S(1)} %copy.215), channel_id=1, source_target_pairs={{0,8},{8,16},{16,24},{1,9},{9,17},{17,25},{2,10},{10,18},{18,26},{... | collective-permute-start | bytes 110600 | tf_op jit(solution)/shard_map/ppermute | solution.py:17
  1098.2 3.1 collective-permute-start.1
  1101.3 6.0 collective-permute-start.3
  1102.6 6.3 collective-permute-start.2
  1114.9 2.1 copy-start.7
  1117.3 4.9 collective-permute-start.5
  1118.6 4.4 collective-permute-start.4
  1123.1 6.1 collective-permute-start.7
  1124.4 6.5 collective-permute-start.6
  1135.6 1.8 copy-start.6
  1144.5 5.3 collective-permute-start.9
  1145.8 4.2 collective-permute-start.8
  1150.0 7.5 collective-permute-start.11
  1151.3 6.8 collective-permute-start.10
  1171.7 60.2 %collective-permute-start.13 = (bf16[16,1,8,128]{3,0,2,1:T(8,128)(2,1)S(1)}, bf16[16,1,8,128]{3,0,2,1:T(8,128)(2,1)S(1)}, u32[]{:S(2)}, u32[]{:S(2)}) collective-permute-start(bf16[16,1,8,128]{3,0,2,1:T(8,128)(2,1)S(1)} %get-tuple-element.195), channel_id=1, source_target_pairs={{8,0},{16,8},{24,16},{9,1},{17,9},{25,17},{10,2},{18,10},{26,18},{... | collective-permute-start | bytes 98312 | tf_op jit(solution)/shard_map/ppermute | solution.py:19
  1173.0 58.9 %collective-permute-start.12 = (bf16[16,1,8,128]{3,0,2,1:T(8,128)(2,1)S(1)}, bf16[16,1,8,128]{3,0,2,1:T(8,128)(2,1)S(1)}, u32[]{:S(2)}, u32[]{:S(2)}) collective-permute-start(bf16[16,1,8,128]{3,0,2,1:T(8,128)(2,1)S(1)} %get-tuple-element.194), channel_id=1, source_target_pairs={{0,8},{8,16},{16,24},{1,9},{9,17},{17,25},{2,10},{10,18},{18,26},{... | collective-permute-start | bytes 98312 | tf_op jit(solution)/shard_map/ppermute | solution.py:17
  1231.9 6.7 collective-permute-start.15
  1233.2 6.2 collective-permute-start.14
  (1 other events, 1.8 us)
where the time goes:
time: 1260 us; the launch traced here: 1250 us
  other arithmetic  883 us (70%)
  local copies, waits for them, and re-layouts  181 us (14%)
  blocking collectives  74.9 us (6%)
  starting transfers between devices  58.2 us (5%)
  matrix products  39 us (3%)
    scatter-add x8, other arithmetic, deposit_local(): total.at[:, index].add(charges * (weight_y * weight_z * weight_x)[None, :])  845 us
    scatter x1, local copies, waits for them, and re-layouts, local(): jnp.zeros((8, devices * capacity), jnp.float32).at[:, column].set(payload)  70.3 us
    psum x1, blocking collectives, local(): lax.psum((first_terms, first_bias_terms, second_terms, second_bias_terms)...  51.4 us
    ppermute x8, starting transfers between devices, extended_2(): lax.ppermute(tail, axis, [(i, (i + 1) % count) for i in range(ends)])  47.9 us
    gather x1, local copies, waits for them, and re-layouts, local(): sorted_target = target[order]  45.5 us
    mul x8, local copies, waits for them, and re-layouts, deposit_local(): charges * (weight_y * weight_z * weight_x)[None, :]  40.2 us
    dot_general x108, matrix products, conv_valid(): jnp.einsum('oc,cyzx->oyzx', kernel[:, :, shift_y, shift_z, shift_x], wind...  25.6 us
  transfers between devices with their start and end apart: 16, of which 7 were waited for; matrix products, arithmetic and copies ran while one was open for 0% of the time, Pallas kernels for 0%

commit v1 on v0

v1 whole, which is shorter than its diff:
```python
import functools
import math

import jax
import jax.numpy as jnp
from jax import lax
from jax.experimental import pallas as pl
from jax.experimental.pallas import tpu as pltpu
from jax.sharding import PartitionSpec as P

BF = jnp.bfloat16
F32 = jnp.float32
LANES = 128
VALUES = 10
VMEM_LIMIT = 48 * 1024 * 1024


def _iota(shape, dim):
    return lax.broadcasted_iota(jnp.int32, shape, dim)


def _dot(a, b):
    return jnp.dot(a, b, preferred_element_type=F32)


def _dot_lanes(a, b):
    return lax.dot_general(a, b, (((1,), (1,)), ((), ())), preferred_element_type=F32)


def _call(kernel, out_shape, scratch=(), flops=0, moved=0):
    return pl.pallas_call(
        kernel,
        out_shape=out_shape,
        scratch_shapes=list(scratch),
        compiler_params=pltpu.CompilerParams(vmem_limit_bytes=VMEM_LIMIT),
        cost_estimate=pl.CostEstimate(flops=flops, bytes_accessed=moved, transcendentals=0),
    )


def _route_kernel(devices, spans, off_ref, mass_ref, vel_ref, dest_ref, out_ref, acc_ref, base_ref):
    particles = dest_ref.shape[1]
    capacity = 2 * particles // devices
    pieces = capacity // LANES
    width = 512
    lo_count = 2 * LANES
    hi_count = 2 * particles // lo_count
    acc_ref[...] = jnp.zeros_like(acc_ref)
    base_ref[...] = jnp.zeros_like(base_ref)
    row, col = _iota((LANES, 2 * LANES), 0), _iota((LANES, 2 * LANES), 1)
    prefix = jnp.where((row <= col) | (col >= LANES), 1.0, 0.0).astype(BF)

    def step(i, carry):
        lanes = pl.ds(pl.multiple_of(i * width, width), width)
        dest = dest_ref[:, lanes]
        chosen = jnp.where(_iota((devices, width), 0) == dest, 1.0, 0.0)
        base = base_ref[...]
        ranks = []
        for j in range(width // LANES):
            mine = chosen[:, j * LANES : (j + 1) * LANES]
            counts = _dot(mine.astype(BF), prefix)
            ranks.append(jnp.sum(mine * (counts[:, :LANES] + base), axis=0, keepdims=True))
            base = base + counts[:, LANES:]
        base_ref[...] = base
        rank = jnp.concatenate(ranks, axis=1).astype(jnp.int32) - 1
        if pieces >= 2:
            hi = (rank >> 8) * devices + dest
            lo = rank & 255
        else:
            half = devices // 2
            upper = dest >= half
            hi = jnp.where(upper, dest - half, dest)
            lo = rank + jnp.where(upper, LANES, 0)
        rows = []
        for axis in range(3):
            position = off_ref[axis : axis + 1, lanes] * spans[axis]
            coarse = position.astype(BF)
            rows.append(coarse)
            rows.append((position - coarse.astype(F32)).astype(BF))
        mass = mass_ref[:, lanes]
        rows.append(mass.astype(BF))
        for axis in range(3):
            rows.append((mass * vel_ref[axis : axis + 1, lanes]).astype(BF))
        at_hi = jnp.where(_iota((hi_count, width), 0) == hi, 1.0, 0.0).astype(BF)
        at_lo = jnp.where(_iota((lo_count, width), 0) == lo, 1.0, 0.0).astype(BF)
        spread = jnp.concatenate([at_hi * value for value in rows], axis=0)
        acc_ref[...] += _dot_lanes(spread, at_lo)
        return carry

    lax.fori_loop(0, particles // width, step, 0)
    halves = []
    for half in range(2):
        part = acc_ref[:, half * LANES : (half + 1) * LANES]
        if pieces >= 2:
            halves.append(part.reshape(VALUES * pieces // 2, devices, LANES))
        else:
            halves.append(part.reshape(VALUES, devices // 2, LANES))
    whole = jnp.concatenate(halves, axis=0 if pieces >= 2 else 1)
    out_ref[...] = jnp.transpose(whole, (1, 0, 2)).astype(BF)


def _route(offsets, masses, velocities, destination, devices, spans):
    particles = masses.shape[0]
    capacity = 2 * particles // devices
    rows = VALUES * capacity // LANES
    return _call(
        functools.partial(_route_kernel, devices, spans),
        jax.ShapeDtypeStruct((devices, rows, LANES), BF),
        [
            pltpu.VMEM((VALUES * 2 * particles // 256, 256), F32),
            pltpu.VMEM((devices, LANES), F32),
        ],
        flops=4_000_000_000,
        moved=1_000_000,
    )(offsets, masses.reshape(1, particles), velocities, destination.reshape(1, particles))


def _deposit_kernel(span_y, arrived_ref, cot_ref, own_ref, next_ref, prev_ref, acc_ref):
    sources, height, _ = arrived_ref.shape
    pieces = height // VALUES
    group = max(1, 4 // pieces)
    width = group * pieces * LANES
    span_x = LANES
    acc_ref[...] = jnp.zeros_like(acc_ref)

    def value_rows(blocks, value):
        parts = []
        for block in blocks:
            for piece in range(pieces):
                if pieces >= 2:
                    half = pieces // 2
                    at = (piece % 2) * VALUES * half + value * half + piece // 2
                else:
                    at = value
                parts.append(block[at : at + 1, :])
        return jnp.concatenate(parts, axis=1)

    def step(i, carry):
        blocks = [arrived_ref[i * group + g].astype(F32) for g in range(group)]
        pos_y = value_rows(blocks, 0) + value_rows(blocks, 1)
        pos_z = value_rows(blocks, 2) + value_rows(blocks, 3)
        pos_x = value_rows(blocks, 4) + value_rows(blocks, 5)
        charges = jnp.concatenate([value_rows(blocks, 6 + c) for c in range(4)] * 2, axis=0)
        cell_x = _iota((span_x, width), 0).astype(F32)
        hat_x = jnp.maximum(1.0 - jnp.abs(cell_x - pos_x), 0.0).astype(BF)
        cell_z = (_iota((40, width), 0) >> 2).astype(F32)
        hat_z = jnp.maximum(1.0 - jnp.abs(cell_z - pos_z), 0.0)
        planes = hat_z * jnp.concatenate([charges] * 5, axis=0)
        shares = [
            planes * jnp.maximum(1.0 - jnp.abs(y - pos_y), 0.0) for y in range(span_y + 1)
        ]
        acc_ref[...] += _dot_lanes(jnp.concatenate(shares, axis=0).astype(BF), hat_x)
        return carry

    lax.fori_loop(0, sources // group, step, 0)
    own = jnp.concatenate([acc_ref[y * 40 : (y + 1) * 40, :] for y in range(span_y + 1)], axis=1)
    own_ref[...] = own
    lanes = own.shape[1]
    next_ref[0:32, :] = jnp.concatenate([own[16:40], jnp.zeros((8, lanes), F32)], axis=0).astype(BF)
    next_ref[32:64, 0 : lanes - LANES] = cot_ref[96:128, :]
    next_ref[32:64, lanes - LANES :] = jnp.zeros((32, LANES), BF)
    prev_ref[0:16, :] = own[0:16].astype(BF)
    prev_ref[16:48, 0 : lanes - LANES] = cot_ref[0:32, :]
    prev_ref[16:48, lanes - LANES :] = jnp.zeros((32, LANES), BF)


def _turn_kernel(cot_ref, out_ref):
    channels, span_y, span_z, _ = cot_ref.shape
    size = channels * span_z
    strips = [
        jnp.concatenate([cot_ref[o, y].astype(F32) for o in range(channels)], axis=0)
        for y in range(span_y)
    ]
    field = jnp.concatenate(strips, axis=1).astype(BF)
    row, col = _iota((size, size), 0), _iota((size, size), 1)
    order = (row % channels) * span_z + row // channels
    out_ref[...] = _dot(jnp.where(col == order, 1.0, 0.0).astype(BF), field).astype(BF)


def _merge_kernel(count_z, own_ref, cot_ref, left_ref, right_ref, wide_ref, cotw_ref, first_ref, second_ref):
    keep = jnp.where(lax.axis_index("gz") < count_z - 1, 1.0, 0.0)
    even = lax.axis_index("gy") % 2 == 0
    left = left_ref[0:32, :].astype(F32)
    right = right_ref[0:16, :].astype(F32)
    own = own_ref[...]
    wide = jnp.concatenate(
        [
            left[0:16],
            own[0:8] + left[16:24],
            own[8:32],
            own[32:40] * keep + right[0:8],
            right[8:16],
        ],
        axis=0,
    )
    wide_ref[...] = wide
    cells = cot_ref.shape[1]
    cotw_ref[0:32, :] = left_ref[32:64, 0:cells]
    cotw_ref[32:160, :] = cot_ref[...]
    cotw_ref[160:192, :] = right_ref[16:48, 0:cells]

    def to_next(out):
        out[:, 0:640] = wide[:, 512:1152].astype(BF)
        for i in range(3):
            out[:, 640 + 256 * i : 896 + 256 * i] = cotw_ref[64 * i : 64 * (i + 1), cells - 256 : cells]

    def to_prev(out):
        out[:, 0:512] = wide[:, 0:512].astype(BF)
        out[:, 512:640] = jnp.zeros((64, 128), BF)
        for i in range(3):
            out[:, 640 + 256 * i : 896 + 256 * i] = cotw_ref[64 * i : 64 * (i + 1), 0:256]

    @pl.when(even)
    def _():
        to_next(first_ref)
        to_prev(second_ref)

    @pl.when(jnp.logical_not(even))
    def _():
        to_prev(first_ref)
        to_next(second_ref)


def _weights_kernel(k1_ref, k2_ref, w1_ref, w2_ref, wb_ref, wf_ref, scr_ref):
    def wide(x):
        rows, cols = x.shape
        return jnp.concatenate([x, jnp.zeros((rows, LANES - cols), F32)], axis=1)

    def base(block, stride, step, total):
        out = None
        for tx in range(3):
            for tz in range(3):
                x = wide(block(tz, tx))
                x = jnp.concatenate([x, jnp.zeros((x.shape[0], total - LANES), F32)], axis=1)
                at = tx * stride + tz * step
                x = pltpu.roll(x, at, 1) if at else x
                out = x if out is None else out + x
        return out

    for ty in range(3):
        def tap(tz, tx):
            return (ty * 3 + tz) * 3 + tx

        def back(tz, tx):
            return 26 - tap(tz, tx)

        b = base(lambda tz, tx: jnp.swapaxes(wide(k1_ref[tap(tz, tx)].astype(F32)), 0, 1)[0:16, :], 64, 4, 256)
        for z in range(14):
            w1_ref[ty, z * 16 : (z + 1) * 16, :] = (pltpu.roll(b, 4 * z, 1) if z else b).astype(BF)
        b = base(lambda tz, tx: k2_ref[tap(tz, tx)].astype(F32), 256, 16, 768)
        for z in range(12):
            w2_ref[ty, z * 16 : (z + 1) * 16, :] = (pltpu.roll(b, 16 * z, 1) if z else b).astype(BF)
        b = base(lambda tz, tx: jnp.swapaxes(wide(k2_ref[back(tz, tx)].astype(F32)), 0, 1)[0:16, :], 192, 16, 640)
        for z in range(10):
            wb_ref[ty, z * 16 : (z + 1) * 16, :] = (pltpu.roll(b, 16 * z, 1) if z else b).astype(BF)
        b = base(lambda tz, tx: k1_ref[back(tz, tx)].astype(F32), 160, 16, 512)
        for z in range(8):
            moved = pltpu.roll(b, 16 * z, 1) if z else b
            for c in range(4):
                scr_ref[c * 8 + z : c * 8 + z + 1, :] = moved[c : c + 1, :]
        wf_ref[ty] = scr_ref[...].astype(BF)


def _net_kernel(
    count_y, count_z, wide_ref, cotw_ref, ra_ref, rb_ref, w1_ref, w2_ref, wb_ref, wf_ref,
    b1_ref, b2_ref, refined_ref, field_ref, sums_ref,
    msg_ref, dens_ref, act_ref, del_ref, one_ref, ds_ref, ref_ref,
):
    me_y, me_z = lax.axis_index("gy"), lax.axis_index("gz")
    even = me_y % 2 == 0

    @pl.when(even)
    def _():
        msg_ref[0] = rb_ref[...]
        msg_ref[1] = ra_ref[...]

    @pl.when(jnp.logical_not(even))
    def _():
        msg_ref[0] = ra_ref[...]
        msg_ref[1] = rb_ref[...]

    edge = _iota((1, LANES), 1)
    first_lane, last_lane = edge == 0, edge == LANES - 1

    def shifted(value, dst, row0, stride, lane0):
        rows, lanes = value.shape
        for y in range(lanes // LANES):
            block = value[:, y * LANES : (y + 1) * LANES]
            at = slice(lane0 + y * LANES, lane0 + (y + 1) * LANES)
            left = jnp.where(first_lane, 0.0, pltpu.roll(block, 1, 1))
            right = jnp.where(last_lane, 0.0, pltpu.roll(block, LANES - 1, 1))
            dst[row0 : row0 + rows, at] = left.astype(BF)
            dst[row0 + stride : row0 + stride + rows, at] = block.astype(BF)
            dst[row0 + 2 * stride : row0 + 2 * stride + rows, at] = right.astype(BF)

    keep_y = jnp.where(me_y < count_y - 1, 1.0, 0.0)
    up = msg_ref[0, :, 0:640].astype(F32)
    down = msg_ref[1, :, 0:512].astype(F32)
    shifted(up[:, 0:512], dens_ref, 0, 64, 0)
    shifted(wide_ref[:, 0:128] + up[:, 512:640], dens_ref, 0, 64, 512)
    shifted(wide_ref[:, 128:1024], dens_ref, 0, 64, 640)
    shifted(wide_ref[:, 1024:1152] * keep_y + down[:, 0:128], dens_ref, 0, 64, 1536)
    shifted(down[:, 128:512], dens_ref, 0, 64, 1664)

    eye = _iota((16, 16), 0) == _iota((16, 16), 1)

    def column(bias_ref, count):
        one = jnp.sum(jnp.where(eye, bias_ref[...], 0.0), axis=1, keepdims=True)
        return jnp.concatenate([one] * count, axis=0)

    def inside_z(rows, halo):
        z = me_z * 8 - halo + (_iota((rows, 1), 0) >> 4)
        return jnp.where((z >= 0) & (z < count_z * 8), 1.0, 0.0)

    def inside_y(first, halo):
        y = me_y * 8 - halo + first + (_iota((1, 256), 1) >> 7)
        return jnp.where((y >= 0) & (y < count_y * 8), 1.0, 0.0)

    bias = column(b1_ref, 14)
    mask_z = inside_z(224, 3)
    for tx in range(3):
        act_ref[tx * 256 + 224 : (tx + 1) * 256, :] = jnp.zeros((32, act_ref.shape[1]), BF)
    for n in range(7):
        pre = bias
        for ty in range(3):
            at = (2 * n + ty) * LANES
            pre = pre + _dot(w1_ref[ty, :, 0:192], dens_ref[:, at : at + 256])
        sig = 0.5 * jnp.tanh(0.5 * pre) + 0.5
        act = pre * sig
        if 1 <= n <= 5:
            mid = slice(32, 192)
            ds_ref[:, (n - 1) * 256 : n * 256] = sig[mid] * (1.0 + pre[mid] - act[mid])
        shifted(act * (mask_z * inside_y(2 * n, 3)), act_ref, 0, 256, n * 256)

    bias = column(b2_ref, 12)
    for n in range(6):
        pre = bias
        for ty in range(3):
            at = (2 * n + ty) * LANES
            pre = pre + _dot(w2_ref[ty], act_ref[:, at : at + 256])
        sig = 0.5 * jnp.tanh(0.5 * pre) + 0.5
        act = pre * sig
        if n == 0 or n == 5:
            side = 0 if n == 0 else 1
            cot = jnp.concatenate(
                [msg_ref[side, :, 640 + 256 * i : 896 + 256 * i] for i in range(3)], axis=0
            )
        else:
            cot = cotw_ref[:, (n - 1) * 256 : n * 256]
            ref_ref[:, (n - 1) * 256 : n * 256] = act[32:160].astype(BF)
        shifted(cot.astype(F32) * (sig * (1.0 + pre - act)), del_ref, 0, 192, n * 256)

    mask_z = inside_z(160, 1)
    for n in range(5):
        back = None
        for ty in range(3):
            at = (2 * n + ty) * LANES
            term = _dot(wb_ref[ty, :, 0:576], del_ref[:, at : at + 256])
            back = term if back is None else back + term
        back = back * ds_ref[:, n * 256 : (n + 1) * 256] * (mask_z * inside_y(2 * n, 1))
        shifted(back, one_ref, 0, 160, n * 256)

    for n in range(4):
        grad = None
        for ty in range(3):
            at = (2 * n + ty) * LANES
            term = _dot(wf_ref[ty, :, 0:480], one_ref[:, at : at + 256])
            grad = term if grad is None else grad + term
        for y in range(2):
            for c in range(4):
                field_ref[c, 2 * n + y] = grad[c * 8 : (c + 1) * 8, y * LANES : (y + 1) * LANES]

    row, col = _iota((128, 128), 0), _iota((128, 128), 1)
    order = jnp.where(col == (row % 8) * 16 + row // 8, 1.0, 0.0).astype(BF)
    for n in range(4):
        turned = _dot(order, ref_ref[:, n * 256 : (n + 1) * 256]).astype(BF)
        for y in range(2):
            for o in range(16):
                refined_ref[o, 2 * n + y] = turned[o * 8 : (o + 1) * 8, y * LANES : (y + 1) * LANES]

    lane_z = _iota((1, LANES), 1) >> 4
    own_two = del_ref[224:352, 256:1280]
    own_one = one_ref[176:304, 128:1152]

    def folded(value):
        for step in (64, 32, 16):
            value = value + pltpu.roll(value, step, 1)
        return value

    def packed(taps, rows):
        groups = []
        for g in range(4):
            out = jnp.zeros((rows, LANES), F32)
            for t in range(8 * g, min(8 * g + 8, len(taps))):
                out = jnp.where(lane_z == t % 8, taps[t], out)
            groups.append(out)
        return groups

    taps = [None] * 27
    for ty in range(3):
        for tx in range(3):
            lanes = slice((2 + ty) * LANES, (2 + ty) * LANES + 1024)
            pairs = _dot_lanes(act_ref[tx * 256 + 32 : tx * 256 + 192, lanes], own_two)
            for tz in range(3):
                total = jnp.zeros((16, LANES), F32)
                for z in range(tz, tz + 8):
                    total = total + jnp.where(lane_z == z - tz, pairs[z * 16 : (z + 1) * 16], 0.0)
                taps[(ty * 3 + tz) * 3 + tx] = folded(total)
    ones = jnp.ones((16, 1024), BF)
    taps.append(folded(_dot_lanes(ones, own_two)))
    taps.append(folded(_dot_lanes(ones, own_one)))
    for g, group in enumerate(packed(taps, 16)):
        sums_ref[g * 16 : (g + 1) * 16, :] = group

    taps = [None] * 27
    row_z = (_iota((64, LANES), 0) >> 2) - (_iota((64, LANES), 1) >> 4) - 3
    for ty in range(3):
        for tx in range(3):
            lanes = slice((3 + ty) * LANES, (3 + ty) * LANES + 1024)
            pairs = _dot_lanes(dens_ref[tx * 64 : (tx + 1) * 64, lanes], own_one)
            for tz in range(3):
                chosen = jnp.where(row_z == tz, pairs, 0.0)
                total = chosen[0:8]
                for i in range(1, 8):
                    total = total + chosen[i * 8 : (i + 1) * 8]
                total = total + pltpu.roll(total, 4, 0)
                taps[(ty * 3 + tz) * 3 + tx] = folded(total)
    upper = _iota((8, LANES), 0) < 4
    groups = packed(taps, 8)
    sums_ref[64:72, :] = jnp.where(upper, groups[0], groups[1])
    sums_ref[72:80, :] = jnp.where(upper, groups[2], groups[3])


def _finish_kernel(scale, a_ref, b_ref, c_ref, d_ref, k1_ref, b1_ref, k2_ref, b2_ref):
    total = ((a_ref[...] + b_ref[...]) + (c_ref[...] + d_ref[...])) * scale
    for g in range(4):
        block = jnp.swapaxes(total[g * 16 : (g + 1) * 16, :], 0, 1)
        for j in range(8):
            t = g * 8 + j
            if t < 27:
                k2_ref[t] = block[j * 16 : (j + 1) * 16, :]
    tail = total[48:49, :]
    b2_ref[...] = tail[:, 48:64]
    b1_ref[...] = tail[:, 64:80]
    for t in range(27):
        g = t // 8
        rows = 64 + 8 * (g // 2) + 4 * (g % 2)
        k1_ref[t] = total[rows : rows + 4, (t % 8) * 16 : (t % 8) * 16 + 16]


def _local(
    offsets,
    masses,
    velocities,
    destination,
    first_weight,
    first_bias,
    second_weight,
    second_bias,
    cotangent,
):
    count_y = lax.axis_size("gy")
    count_z = lax.axis_size("gz")
    devices = count_y * count_z
    channels, span_y, span_z, span_x = cotangent.shape
    spans = (float(span_y), float(span_z), float(span_x))
    lanes = span_y * span_x
    both = ("gy", "gz")

    outgoing = _route(offsets, masses, velocities, destination, devices, spans)
    arrived = lax.all_to_all(outgoing, both, split_axis=0, concat_axis=0, tiled=True)

    turned = _call(
        _turn_kernel, jax.ShapeDtypeStruct((channels * span_z, lanes), BF), flops=10**8, moved=10**6
    )(cotangent)
    own, to_next, to_prev = _call(
        functools.partial(_deposit_kernel, span_y),
        (
            jax.ShapeDtypeStruct((40, lanes + span_x), F32),
            jax.ShapeDtypeStruct((64, lanes + span_x), BF),
            jax.ShapeDtypeStruct((48, lanes + span_x), BF),
        ),
        [pltpu.VMEM((40 * (span_y + 1), span_x), F32)],
        flops=4 * 10**9,
        moved=10**6,
    )(arrived, turned)
    left = lax.ppermute(to_next, "gz", [(i, i + 1) for i in range(count_z - 1)])
    right = lax.ppermute(to_prev, "gz", [(i + 1, i) for i in range(count_z - 1)])
    k1 = first_weight.transpose(2, 3, 4, 1, 0).reshape(27, 4, 16)
    k2 = second_weight.transpose(2, 3, 4, 0, 1).reshape(27, 16, 16)
    banded = _call(
        _weights_kernel,
        (
            jax.ShapeDtypeStruct((3, 224, 256), BF),
            jax.ShapeDtypeStruct((3, 192, 768), BF),
            jax.ShapeDtypeStruct((3, 160, 640), BF),
            jax.ShapeDtypeStruct((3, 32, 512), BF),
        ),
        [pltpu.VMEM((32, 512), F32)],
        flops=2 * 10**9,
        moved=2 * 10**6,
    )(k1, k2)
    wide, cot_wide, first, second = _call(
        functools.partial(_merge_kernel, count_z),
        (
            jax.ShapeDtypeStruct((64, lanes + span_x), F32),
            jax.ShapeDtypeStruct((192, lanes), BF),
            jax.ShapeDtypeStruct((64, 1408), BF),
            jax.ShapeDtypeStruct((64, 1408), BF),
        ),
        flops=10**6,
        moved=10**6,
    )(own, turned, left, right)
    inner = [(i, i ^ 1) for i in range(count_y)]
    outer = [(i, i + 1) for i in range(1, count_y - 1, 2)]
    outer = outer + [(j, i) for i, j in outer]
    got_first = lax.ppermute(first, "gy", inner)
    got_second = lax.ppermute(second, "gy", outer)
    refined, grad_field, sums = _call(
        functools.partial(_net_kernel, count_y, count_z),
        (
            jax.ShapeDtypeStruct(cotangent.shape, BF),
            jax.ShapeDtypeStruct((4,) + cotangent.shape[1:], F32),
            jax.ShapeDtypeStruct((80, LANES), F32),
        ),
        [
            pltpu.VMEM((2, 64, 1408), BF),
            pltpu.VMEM((192, 2048), BF),
            pltpu.VMEM((768, 1792), BF),
            pltpu.VMEM((576, 1536), BF),
            pltpu.VMEM((480, 1280), BF),
            pltpu.VMEM((160, 1280), F32),
            pltpu.VMEM((128, 1024), BF),
        ],
        flops=6 * 10**9,
        moved=2 * 10**6,
    )(
        wide, cot_wide, got_first, got_second, *banded,
        first_bias.reshape(1, 16), second_bias.reshape(1, 16),
    )

    def swapped(value, bit):
        return lax.ppermute(value, both, [(i, i ^ bit) for i in range(devices)])

    bits = [1 << i for i in range((devices - 1).bit_length())]
    inner_bit = count_z
    rest = [b for b in bits if b != inner_bit]
    total = sums + swapped(sums, inner_bit)
    while len(rest) > 2:
        a = rest.pop()
        if len(rest) > 2:
            b = rest.pop(0)
            total = (total + swapped(total, a)) + (swapped(total, b) + swapped(total, a ^ b))
        else:
            total = total + swapped(total, a)
    a, b = rest
    parts = (total, swapped(total, a), swapped(total, b), swapped(total, a ^ b))
    scale = 1.0 / math.sqrt(span_y * span_z * span_x * devices)
    g1, gb1, g2, gb2 = _call(
        functools.partial(_finish_kernel, scale),
        (
            jax.ShapeDtypeStruct((27, 4, 16), F32),
            jax.ShapeDtypeStruct((1, 16), F32),
            jax.ShapeDtypeStruct((27, 16, 16), F32),
            jax.ShapeDtypeStruct((1, 16), F32),
        ),
        flops=10**5,
        moved=10**5,
    )(*parts)
    return (
        refined,
        grad_field,
        g1.reshape(3, 3, 3, 4, 16).transpose(4, 3, 0, 1, 2),
        gb1.reshape(16),
        g2.reshape(3, 3, 3, 16, 16).transpose(3, 4, 0, 1, 2),
        gb2.reshape(16),
    )


def solution(mesh):
    placed = (
        P(None, ("gy", "gz")),
        P(("gy", "gz")),
        P(None, ("gy", "gz")),
        P(("gy", "gz"), None),
        P(),
        P(),
        P(),
        P(),
        P(None, "gy", "gz", None),
    )
    return jax.shard_map(
        _local,
        mesh=mesh,
        in_specs=placed,
        out_specs=(P(None, "gy", "gz", None), P(None, "gy", "gz", None), P(), P(), P(), P()),
        check_vma=False,
    )
```

time: 1260 us -> 83.2 us (0.07); the launches traced: 1250 us -> 82.8 us
  other arithmetic: 883 us -> 0.02 us
  local copies, waits for them, and re-layouts: 181 us -> 4.03 us
  blocking collectives: 74.9 us -> 0 us
  matrix products: 39 us -> 0 us
  starting transfers between devices: 58.2 us -> 25.3 us
  Pallas kernels: 0 us -> 28.5 us
  waiting for transfers between devices: 7.45 us -> 24.2 us
    scatter-add x8 -> x0, other arithmetic: 845 us -> none  [deposit_local(): total.at[:, index].add(charges * (weight_y * weight_z * weight_x)[None, :])]
    scatter x1 -> x0, local copies, waits for them, and re-layouts: 70.3 us -> none  [local(): jnp.zeros((8, devices * capacity), jnp.float32).at[:, column].set(payload)]
    gather x17 -> x0, local copies, waits for them, and re-layouts: 56.8 us -> none  [the longest x1 45.5 us: local(): sorted_target = target[order]]
    psum x1 -> x0, blocking collectives: 51.4 us -> none  [local(): lax.psum((first_terms, first_bias_terms, second_terms, second_bias_terms)...]
    ppermute x16 -> x11, starting transfers between devices: 58.2 us -> 18 us  [the longest x7 13.1 us: swapped(): return lax.ppermute(value, both, [(i, i ^ bit) for i in range(devices)])]
    mul x8 -> x0, local copies, waits for them, and re-layouts: 40.2 us -> none  [deposit_local(): charges * (weight_y * weight_z * weight_x)[None, :]]
    dot_general x162 -> x0, matrix products: 39 us -> none  [the longest x108 25.6 us: conv_valid(): jnp.einsum('oc,cyzx->oyzx', kernel[:, :, shift_y, shift_z, shift_x], wind...]
    pallas_call x0 -> x7, Pallas kernels: none -> 28.5 us  [the longest x1 10.1 us: _local(): _call(functools.partial(_deposit_kernel, span_y), (jax.ShapeDtypeStruct((...]
  transfers between devices with their start and end apart: 16 -> 12, of which waited for: 7 -> 8; matrix products, arithmetic and copies ran while one was open for 0% -> 0% of each run, Pallas kernels for 0% -> 2%
where the time goes in v1:
time: 83.2 us; the launch traced here: 82.8 us
  Pallas kernels  28.5 us (34%)
  starting transfers between devices  25.3 us (30%)
  waiting for transfers between devices  24.2 us (29%)
  local copies, waits for them, and re-layouts  4.03 us (5%)
    ppermute x7, starting transfers between devices, swapped(): return lax.ppermute(value, both, [(i, i ^ bit) for i in range(devices)])  13.1 us
    all_to_all x1, waiting for transfers between devices, _local(): lax.all_to_all(outgoing, both, split_axis=0, concat_axis=0, tiled=True)  11.9 us
    pallas_call x1, Pallas kernels, _local(): _call(functools.partial(_deposit_kernel, span_y), (jax.ShapeDtypeStruct((...  10.1 us
    pallas_call x1, Pallas kernels, _route(): _call(functools.partial(_route_kernel, devices, spans), jax.ShapeDtypeStr...  9.72 us
    all_to_all x1, starting transfers between devices, _local(): lax.all_to_all(outgoing, both, split_axis=0, concat_axis=0, tiled=True)  7.3 us
    ppermute x7, waiting for transfers between devices, swapped(): return lax.ppermute(value, both, [(i, i ^ bit) for i in range(devices)])  6.86 us
    pallas_call x1, Pallas kernels, _local(): _call(functools.partial(_net_kernel, count_y, count_z), (jax.ShapeDtypeSt...  5.91 us
    ppermute x1, waiting for transfers between devices, _local(): lax.ppermute(to_prev, 'gz', [(i + 1, i) for i in range(count_z - 1)])  5.39 us
  transfers between devices with their start and end apart: 12, of which 8 were waited for; matrix products, arithmetic and copies ran while one was open for 0% of the time, Pallas kernels for 2%

profile of v1, /device:TPU:0, one launch (start us, length us, event | category | flops | bytes accessed | tf_op | source)
XLA Modules:
  0.0 82.8 jit_solution(7155920987900164740)
XLA Ops:
  0.6 0.9 %copy-done.1 = f32[3,8192]{1,0:T(4,128)S(1)} copy-done((f32[3,8192]{1,0:T(4,128)S(1)}, f32[3,8192]{1,0:T(4,128)}, u32[]{:S(2)}) %copy-start.1) | copy-done | bytes 98328
  1.5 0.9 %copy-done.2 = f32[3,8192]{1,0:T(4,128)S(1)} copy-done((f32[3,8192]{1,0:T(4,128)S(1)}, f32[3,8192]{1,0:T(4,128)}, u32[]{:S(2)}) %copy-start.2) | copy-done | bytes 98328
  2.4 0.8 copy-done.4
  3.2 0.8 copy-done.5
  4.0 9.7 %shard_map.136 = bf16[32,40,128]{2,1,0:T(8,128)(2,1)} custom-call(f32[3,8192]{1,0:T(4,128)S(1)} %copy-done.1, f32[1,8192]{1,0:T(1,128)S(1)} %bitcast.19, f32[3,8192]{1,0:T(4,128)S(1)} %copy-done.2, s32[1,8192]{1,0:T(1,128)S(1)} %bitcast.20), custom_call_target="tpu_custom_call" | custom-call | flops 4000000000 | bytes 1000000 | tf_op jit(solution)/shard_map/pallas_call | solution.py:105
  13.7 7.3 %all-to-all-start = ((bf16[32,40,128]{2,1,0:T(8,128)(2,1)}), bf16[32,40,128]{2,1,0:T(8,128)(2,1)S(1)}, u32[]{:S(2)}, u32[]{:S(2)}) async-start(bf16[32,40,128]{2,1,0:T(8,128)(2,1)} %shard_map.136), calls=%async_computation | async-start | bytes 655360 | tf_op jit(solution)/shard_map/all_to_all | solution.py:470
  21.2 11.9 %all-to-all-done.arrived_ref = bf16[32,40,128]{2,1,0:T(8,128)(2,1)S(1)} async-done(((bf16[32,40,128]{2,1,0:T(8,128)(2,1)}), bf16[32,40,128]{2,1,0:T(8,128)(2,1)S(1)}, u32[]{:S(2)}, u32[]{:S(2)}) %all-to-all-start) | async-done | bytes 327712 | tf_op jit(solution)/shard_map/all_to_all | solution.py:470
  33.1 10.1 %shard_map.138 = (f32[40,1152]{1,0:T(8,128)S(1)}, bf16[64,1152]{1,0:T(8,128)(2,1)S(1)}, bf16[48,1152]{1,0:T(8,128)(2,1)S(1)}) custom-call(bf16[32,40,128]{2,1,0:T(8,128)(2,1)S(1)} %all-to-all-done.arrived_ref, bf16[128,1024]{1,0:T(8,128)(2,1)S(1)} %shard_map.137.cot_ref), custom_call_target="tpu_custom_call" | custom-call | flops 4000000000 | bytes 1000000 | tf_op jit(solution)/shard_map/pallas_call | solution.py:475
  43.2 2.8 %collective-permute-start = (bf16[64,1152]{1,0:T(8,128)(2,1)S(1)}, bf16[64,1152]{1,0:T(8,128)(2,1)S(1)}, u32[]{:S(2)}, u32[]{:S(2)}) collective-permute-start(bf16[64,1152]{1,0:T(8,128)(2,1)S(1)} %get-tuple-element.25), channel_id=1, source_target_pairs={{0,1},{1,2},{2,3},{3,4},{4,5},{5,6},{6,7},{8,9},{9,10},{10,11},{11... | collective-permute-start | bytes 442376 | tf_op jit(solution)/shard_map/ppermute | solution.py:486
  46.0 1.3 %collective-permute-start.1 = (bf16[48,1152]{1,0:T(8,128)(2,1)S(1)}, bf16[48,1152]{1,0:T(8,128)(2,1)S(1)}, u32[]{:S(2)}, u32[]{:S(2)}) collective-permute-start(bf16[48,1152]{1,0:T(8,128)(2,1)S(1)} %get-tuple-element.26), channel_id=1, source_target_pairs={{1,0},{2,1},{3,2},{4,3},{5,4},{6,5},{7,6},{9,8},{10,9},{11,10},{12... | collective-permute-start | bytes 331784 | tf_op jit(solution)/shard_map/ppermute | solution.py:487
  47.3 5.4 %collective-permute-done.1.right_ref = bf16[48,1152]{1,0:T(8,128)(2,1)S(1)} collective-permute-done((bf16[48,1152]{1,0:T(8,128)(2,1)S(1)}, bf16[48,1152]{1,0:T(8,128)(2,1)S(1)}, u32[]{:S(2)}, u32[]{:S(2)}) %collective-permute-start.1) | collective-permute-done | bytes 110624 | tf_op jit(solution)/shard_map/ppermute | solution.py:487
  53.6 1.7 %shard_map.140 = (bf16[3,224,256]{2,1,0:T(8,128)(2,1)S(1)}, bf16[3,192,768]{2,1,0:T(8,128)(2,1)S(1)}, bf16[3,160,640]{2,1,0:T(8,128)(2,1)S(1)}, bf16[3,32,512]{2,1,0:T(8,128)(2,1)S(1)}) custom-call(bf16[27,4,16]{2,1,0:T(4,128)(2,1)S(1)} %bitcast.21, bf16[27,16,16]{2,1,0:T(8,128)(2,1)S(1)} %bitcast.18), custom_call_target="tpu_custom_call" | custom-call | flops 2000000000 | bytes 2000000 | tf_op jit(solution)/shard_map/pallas_call | solution.py:490
  56.0 5.9 %shard_map.141 = (bf16[16,8,8,128]{3,2,1,0:T(8,128)(2,1)}, f32[4,8,8,128]{3,2,1,0:T(8,128)}, f32[80,128]{1,0:T(8,128)S(1)}) custom-call(f32[64,1152]{1,0:T(8,128)S(1)} %get-tuple-element.27.wide_ref, bf16[192,1024]{1,0:T(8,128)(2,1)S(1)} %get-tuple-element.28.cotw_ref, bf16[64,1408]{1,0:T(8,128)(2,1)S(1)} %collective-permute-done.2.ra_ref, ...), custom_call_target="tpu_custom_call" | custom-call | flops 6000000000 | bytes 2000000 | tf_op jit(solution)/shard_map/pallas_call | solution.py:518
  61.9 4.9 %collective-permute-start.4 = (f32[80,128]{1,0:T(8,128)S(1)}, f32[80,128]{1,0:T(8,128)S(1)}, u32[]{:S(2)}, u32[]{:S(2)}) collective-permute-start(f32[80,128]{1,0:T(8,128)S(1)} %get-tuple-element.37), channel_id=1, source_target_pairs={{0,8},{1,9},{2,10},{3,11},{4,12},{5,13},{6,14},{7,15},{8,0},{9,1},... | collective-permute-start | bytes 122888 | tf_op jit(solution)/shard_map/ppermute | solution.py:542
  66.8 0.9 %collective-permute-done.4 = f32[80,128]{1,0:T(8,128)S(1)} collective-permute-done((f32[80,128]{1,0:T(8,128)S(1)}, f32[80,128]{1,0:T(8,128)S(1)}, u32[]{:S(2)}, u32[]{:S(2)}) %collective-permute-start.4) | collective-permute-done | bytes 40992 | tf_op jit(solution)/shard_map/ppermute | solution.py:542
  67.7 2.1 %collective-permute-start.7 = (f32[80,128]{1,0:T(8,128)S(1)}, f32[80,128]{1,0:T(8,128)S(1)}, u32[]{:S(2)}, u32[]{:S(2)}) collective-permute-start(f32[80,128]{1,0:T(8,128)S(1)} %add.12), channel_id=1, source_target_pairs={{0,17},{1,16},{2,19},{3,18},{4,21},{5,20},{6,23},{7,22},{8,25},{9,... | collective-permute-start | bytes 122888 | tf_op jit(solution)/shard_map/ppermute | solution.py:542
  70.1 1.4 %collective-permute-start.5 = (f32[80,128]{1,0:T(8,128)S(1)}, f32[80,128]{1,0:T(8,128)S(1)}, u32[]{:S(2)}, u32[]{:S(2)}) collective-permute-start(f32[80,128]{1,0:T(8,128)S(1)} %add.12), channel_id=1, source_target_pairs={{0,16},{1,17},{2,18},{3,19},{4,20},{5,21},{6,22},{7,23},{8,24},{9,... | collective-permute-start | bytes 122888 | tf_op jit(solution)/shard_map/ppermute | solution.py:542
  71.5 1.2 %collective-permute-done.7 = f32[80,128]{1,0:T(8,128)S(1)} collective-permute-done((f32[80,128]{1,0:T(8,128)S(1)}, f32[80,128]{1,0:T(8,128)S(1)}, u32[]{:S(2)}, u32[]{:S(2)}) %collective-permute-start.7) | collective-permute-done | bytes 40992 | tf_op jit(solution)/shard_map/ppermute | solution.py:542
  72.6 1.2 %collective-permute-done.6 = f32[80,128]{1,0:T(8,128)S(1)} collective-permute-done((f32[80,128]{1,0:T(8,128)S(1)}, f32[80,128]{1,0:T(8,128)S(1)}, u32[]{:S(2)}, u32[]{:S(2)}) %collective-permute-start.6) | collective-permute-done | bytes 40992 | tf_op jit(solution)/shard_map/ppermute | solution.py:542
  74.1 2.9 %collective-permute-start.10 = (f32[80,128]{1,0:T(8,128)S(1)}, f32[80,128]{1,0:T(8,128)S(1)}, u32[]{:S(2)}, u32[]{:S(2)}) collective-permute-start(f32[80,128]{1,0:T(8,128)S(1)} %add_add_fusion.a_ref), channel_id=1, source_target_pairs={{0,6},{1,7},{2,4},{3,5},{4,2},{5,3},{6,0},{7,1},{8,14},{9,15},{10,... | collective-permute-start | bytes 122888 | tf_op jit(solution)/shard_map/ppermute | solution.py:542
  77.5 1.1 %collective-permute-start.8 = (f32[80,128]{1,0:T(8,128)S(1)}, f32[80,128]{1,0:T(8,128)S(1)}, u32[]{:S(2)}, u32[]{:S(2)}) collective-permute-start(f32[80,128]{1,0:T(8,128)S(1)} %add_add_fusion.a_ref), channel_id=1, source_target_pairs={{0,2},{1,3},{2,0},{3,1},{4,6},{5,7},{6,4},{7,5},{8,10},{9,11},{10,... | collective-permute-start | bytes 122888 | tf_op jit(solution)/shard_map/ppermute | solution.py:542
  78.6 1.5 %collective-permute-done.10.d_ref = f32[80,128]{1,0:T(8,128)S(1)} collective-permute-done((f32[80,128]{1,0:T(8,128)S(1)}, f32[80,128]{1,0:T(8,128)S(1)}, u32[]{:S(2)}, u32[]{:S(2)}) %collective-permute-start.10) | collective-permute-done | bytes 40992 | tf_op jit(solution)/shard_map/ppermute | solution.py:542
  80.1 1.8 %collective-permute-done.9.c_ref = f32[80,128]{1,0:T(8,128)S(1)} collective-permute-done((f32[80,128]{1,0:T(8,128)S(1)}, f32[80,128]{1,0:T(8,128)S(1)}, u32[]{:S(2)}, u32[]{:S(2)}) %collective-permute-start.9) | collective-permute-done | bytes 40992 | tf_op jit(solution)/shard_map/ppermute | solution.py:542
  81.9 0.9 %shard_map.142 = (f32[27,4,16]{2,1,0:T(4,128)}, f32[1,16]{1,0:T(1,128)}, f32[27,16,16]{2,1,0:T(8,128)}, f32[1,16]{1,0:T(1,128)}) custom-call(f32[80,128]{1,0:T(8,128)S(1)} %add_add_fusion.a_ref, f32[80,128]{1,0:T(8,128)S(1)} %collective-permute-done.8.b_ref, f32[80,128]{1,0:T(8,128)S(1)} %collective-permute-done.9.c_ref, ...), custom_call_target="tpu_custom_call" | custom-call | flops 100000 | bytes 100000 | tf_op jit(solution)/shard_map/pallas_call | solution.py:558
  (27 shorter events, 2.8 us)
Async XLA Ops:
  0.6 0.9 %copy-start.1 = (f32[3,8192]{1,0:T(4,128)S(1)}, f32[3,8192]{1,0:T(4,128)}, u32[]{:S(2)}) copy-start(f32[3,8192]{1,0:T(4,128)} %off_ref.1) | copy-start | bytes 294916
  1.5 0.9 %copy-start.2 = (f32[3,8192]{1,0:T(4,128)S(1)}, f32[3,8192]{1,0:T(4,128)}, u32[]{:S(2)}) copy-start(f32[3,8192]{1,0:T(4,128)} %vel_ref.1) | copy-start | bytes 294916
  2.4 0.8 copy-start.4
  3.2 0.8 copy-start.5
  13.7 7.3 %copy-start = (bf16[16,8,8,128]{3,2,1,0:T(8,128)(2,1)S(1)}, bf16[16,8,8,128]{3,2,1,0:T(8,128)(2,1)}, u32[]{:S(2)}) copy-start(bf16[16,8,8,128]{3,2,1,0:T(8,128)(2,1)} %cot_ref.1) | copy-start | bytes 786436
  13.7 19.4 %all-to-all-start = ((bf16[32,40,128]{2,1,0:T(8,128)(2,1)}), bf16[32,40,128]{2,1,0:T(8,128)(2,1)S(1)}, u32[]{:S(2)}, u32[]{:S(2)}) async-start(bf16[32,40,128]{2,1,0:T(8,128)(2,1)} %shard_map.136), calls=%async_computation | async-start | bytes 655360 | tf_op jit(solution)/shard_map/all_to_all | solution.py:470
  43.2 9.5 %collective-permute-start = (bf16[64,1152]{1,0:T(8,128)(2,1)S(1)}, bf16[64,1152]{1,0:T(8,128)(2,1)S(1)}, u32[]{:S(2)}, u32[]{:S(2)}) collective-permute-start(bf16[64,1152]{1,0:T(8,128)(2,1)S(1)} %get-tuple-element.25), channel_id=1, source_target_pairs={{0,1},{1,2},{2,3},{3,4},{4,5},{5,6},{6,7},{8,9},{9,10},{10,11},{11... | collective-permute-start | bytes 442376 | tf_op jit(solution)/shard_map/ppermute | solution.py:486
  46.0 6.7 %collective-permute-start.1 = (bf16[48,1152]{1,0:T(8,128)(2,1)S(1)}, bf16[48,1152]{1,0:T(8,128)(2,1)S(1)}, u32[]{:S(2)}, u32[]{:S(2)}) collective-permute-start(bf16[48,1152]{1,0:T(8,128)(2,1)S(1)} %get-tuple-element.26), channel_id=1, source_target_pairs={{1,0},{2,1},{3,2},{4,3},{5,4},{6,5},{7,6},{9,8},{10,9},{11,10},{12... | collective-permute-start | bytes 331784 | tf_op jit(solution)/shard_map/ppermute | solution.py:487
  52.7 0.9 %copy-start.3 = (bf16[16,16,3,3,3]{1,0,4,3,2:T(8,128)(2,1)S(1)}, bf16[16,16,3,3,3]{1,0,4,3,2:T(8,128)(2,1)}, u32[]{:S(2)}) copy-start(bf16[16,16,3,3,3]{1,0,4,3,2:T(8,128)(2,1)} %param.15) | copy-start | bytes 41476
  52.7 0.9 %copy-start.6 = (bf16[16,4,3,3,3]{0,1,4,3,2:T(4,128)(2,1)S(1)}, bf16[16,4,3,3,3]{0,1,4,3,2:T(4,128)(2,1)}, u32[]{:S(2)}) copy-start(bf16[16,4,3,3,3]{0,1,4,3,2:T(4,128)(2,1)} %param.13) | copy-start | bytes 10372
  52.8 2.5 %collective-permute-start.2 = (bf16[64,1408]{1,0:T(8,128)(2,1)S(1)}, bf16[64,1408]{1,0:T(8,128)(2,1)S(1)}, u32[]{:S(2)}, u32[]{:S(2)}) collective-permute-start(bf16[64,1408]{1,0:T(8,128)(2,1)S(1)} %get-tuple-element.29), channel_id=1, source_target_pairs={{0,8},{8,0},{16,24},{24,16},{1,9},{9,1},{17,25},{25,17},{2,10},{10... | collective-permute-start | bytes 540680 | tf_op jit(solution)/shard_map/ppermute | solution.py:516
  52.9 2.4 %collective-permute-start.3 = (bf16[64,1408]{1,0:T(8,128)(2,1)S(1)}, bf16[64,1408]{1,0:T(8,128)(2,1)S(1)}, u32[]{:S(2)}, u32[]{:S(2)}) collective-permute-start(bf16[64,1408]{1,0:T(8,128)(2,1)S(1)} %get-tuple-element.30), channel_id=1, source_target_pairs={{8,16},{16,8},{9,17},{17,9},{10,18},{18,10},{11,19},{19,11},{12,20... | collective-permute-start | bytes 540680 | tf_op jit(solution)/shard_map/ppermute | solution.py:517
  55.3 0.7 copy-start.7
  55.3 0.7 copy-start.8
  61.9 5.8 %collective-permute-start.4 = (f32[80,128]{1,0:T(8,128)S(1)}, f32[80,128]{1,0:T(8,128)S(1)}, u32[]{:S(2)}, u32[]{:S(2)}) collective-permute-start(f32[80,128]{1,0:T(8,128)S(1)} %get-tuple-element.37), channel_id=1, source_target_pairs={{0,8},{1,9},{2,10},{3,11},{4,12},{5,13},{6,14},{7,15},{8,0},{9,1},... | collective-permute-start | bytes 122888 | tf_op jit(solution)/shard_map/ppermute | solution.py:542
  67.7 4.9 %collective-permute-start.7 = (f32[80,128]{1,0:T(8,128)S(1)}, f32[80,128]{1,0:T(8,128)S(1)}, u32[]{:S(2)}, u32[]{:S(2)}) collective-permute-start(f32[80,128]{1,0:T(8,128)S(1)} %add.12), channel_id=1, source_target_pairs={{0,17},{1,16},{2,19},{3,18},{4,21},{5,20},{6,23},{7,22},{8,25},{9,... | collective-permute-start | bytes 122888 | tf_op jit(solution)/shard_map/ppermute | solution.py:542
  69.8 4.0 %collective-permute-start.6 = (f32[80,128]{1,0:T(8,128)S(1)}, f32[80,128]{1,0:T(8,128)S(1)}, u32[]{:S(2)}, u32[]{:S(2)}) collective-permute-start(f32[80,128]{1,0:T(8,128)S(1)} %add.12), channel_id=1, source_target_pairs={{0,1},{1,0},{2,3},{3,2},{4,5},{5,4},{6,7},{7,6},{8,9},{9,8},{10,11... | collective-permute-start | bytes 122888 | tf_op jit(solution)/shard_map/ppermute | solution.py:542
  70.1 4.1 %collective-permute-start.5 = (f32[80,128]{1,0:T(8,128)S(1)}, f32[80,128]{1,0:T(8,128)S(1)}, u32[]{:S(2)}, u32[]{:S(2)}) collective-permute-start(f32[80,128]{1,0:T(8,128)S(1)} %add.12), channel_id=1, source_target_pairs={{0,16},{1,17},{2,18},{3,19},{4,20},{5,21},{6,22},{7,23},{8,24},{9,... | collective-permute-start | bytes 122888 | tf_op jit(solution)/shard_map/ppermute | solution.py:542
  74.1 6.0 %collective-permute-start.10 = (f32[80,128]{1,0:T(8,128)S(1)}, f32[80,128]{1,0:T(8,128)S(1)}, u32[]{:S(2)}, u32[]{:S(2)}) collective-permute-start(f32[80,128]{1,0:T(8,128)S(1)} %add_add_fusion.a_ref), channel_id=1, source_target_pairs={{0,6},{1,7},{2,4},{3,5},{4,2},{5,3},{6,0},{7,1},{8,14},{9,15},{10,... | collective-permute-start | bytes 122888 | tf_op jit(solution)/shard_map/ppermute | solution.py:542
  77.0 4.9 %collective-permute-start.9 = (f32[80,128]{1,0:T(8,128)S(1)}, f32[80,128]{1,0:T(8,128)S(1)}, u32[]{:S(2)}, u32[]{:S(2)}) collective-permute-start(f32[80,128]{1,0:T(8,128)S(1)} %add_add_fusion.a_ref), channel_id=1, source_target_pairs={{0,4},{1,5},{2,6},{3,7},{4,0},{5,1},{6,2},{7,3},{8,12},{9,13},{10,... | collective-permute-start | bytes 122888 | tf_op jit(solution)/shard_map/ppermute | solution.py:542
  77.5 4.4 %collective-permute-start.8 = (f32[80,128]{1,0:T(8,128)S(1)}, f32[80,128]{1,0:T(8,128)S(1)}, u32[]{:S(2)}, u32[]{:S(2)}) collective-permute-start(f32[80,128]{1,0:T(8,128)S(1)} %add_add_fusion.a_ref), channel_id=1, source_target_pairs={{0,2},{1,3},{2,0},{3,1},{4,6},{5,7},{6,4},{7,5},{8,10},{9,11},{10,... | collective-permute-start | bytes 122888 | tf_op jit(solution)/shard_map/ppermute | solution.py:542

commit v2 on v1

--- a/solution.py
+++ b/solution.py
@@ -13,6 +13,8 @@
 LANES = 128
 VALUES = 10
 VMEM_LIMIT = 48 * 1024 * 1024
+ROUTE_VMEM_LIMIT = 60 * 1024 * 1024
+ROUTE_WIDTH = 512
 
 
 def _iota(shape, dim):
@@ -37,31 +39,51 @@
     )
 
 
-def _route_kernel(devices, spans, off_ref, mass_ref, vel_ref, dest_ref, out_ref, acc_ref, base_ref):
+def _route_kernel(
+    devices, spans, off_hbm, mass_hbm, vel_hbm, dest_hbm, out_ref,
+    off_ref, mass_ref, vel_ref, dest_ref, acc_ref, rank_ref, sems,
+):
+    loads = [
+        pltpu.make_async_copy(src, dst, sems.at[i])
+        for i, (src, dst) in enumerate(
+            ((dest_hbm, dest_ref), (off_hbm, off_ref), (mass_hbm, mass_ref), (vel_hbm, vel_ref))
+        )
+    ]
+    for load in loads:
+        load.start()
     particles = dest_ref.shape[1]
     capacity = 2 * particles // devices
     pieces = capacity // LANES
-    width = 512
+    width = ROUTE_WIDTH
     lo_count = 2 * LANES
     hi_count = 2 * particles // lo_count
-    acc_ref[...] = jnp.zeros_like(acc_ref)
-    base_ref[...] = jnp.zeros_like(base_ref)
     row, col = _iota((LANES, 2 * LANES), 0), _iota((LANES, 2 * LANES), 1)
     prefix = jnp.where((row <= col) | (col >= LANES), 1.0, 0.0).astype(BF)
+    number = _iota((devices, LANES), 0)
+    loads[0].wait()
+
+    def count(i, base):
+        dests = [
+            dest_ref[:, pl.ds(pl.multiple_of((i * 16 + j) * LANES, LANES), LANES)] for j in range(16)
+        ]
+        chosen = [jnp.where(number == dest, 1.0, 0.0) for dest in dests]
+        counts = _dot(jnp.concatenate(chosen, axis=0).astype(BF), prefix)
+        for j in range(16):
+            mine = counts[j * devices : (j + 1) * devices]
+            rank = jnp.sum(chosen[j] * (mine[:, :LANES] + base), axis=0, keepdims=True)
+            at = pl.ds(pl.multiple_of((i * 16 + j) * LANES, LANES), LANES)
+            rank_ref[:, at] = rank.astype(jnp.int32) - 1
+            base = base + mine[:, LANES:]
+        return base
+
+    lax.fori_loop(0, particles // (16 * LANES), count, jnp.zeros((devices, LANES), F32), unroll=True)
+    for load in loads[1:]:
+        load.wait()
 
     def step(i, carry):
-        lanes = pl.ds(pl.multiple_of(i * width, width), width)
+        lanes = slice(i * width, (i + 1) * width)
         dest = dest_ref[:, lanes]
-        chosen = jnp.where(_iota((devices, width), 0) == dest, 1.0, 0.0)
-        base = base_ref[...]
-        ranks = []
-        for j in range(width // LANES):
-            mine = chosen[:, j * LANES : (j + 1) * LANES]
-            counts = _dot(mine.astype(BF), prefix)
-            ranks.append(jnp.sum(mine * (counts[:, :LANES] + base), axis=0, keepdims=True))
-            base = base + counts[:, LANES:]
-        base_ref[...] = base
-        rank = jnp.concatenate(ranks, axis=1).astype(jnp.int32) - 1
+        rank = rank_ref[:, lanes]
         if pieces >= 2:
             hi = (rank >> 8) * devices + dest
             lo = rank & 255
@@ -83,10 +105,14 @@
         at_hi = jnp.where(_iota((hi_count, width), 0) == hi, 1.0, 0.0).astype(BF)
         at_lo = jnp.where(_iota((lo_count, width), 0) == lo, 1.0, 0.0).astype(BF)
         spread = jnp.concatenate([at_hi * value for value in rows], axis=0)
-        acc_ref[...] += _dot_lanes(spread, at_lo)
-        return carry
-
-    lax.fori_loop(0, particles // width, step, 0)
+        term = _dot_lanes(spread, at_lo)
+        if i == 0:
+            acc_ref[...] = term
+        else:
+            acc_ref[...] += term
+
+    for i in range(particles // width):
+        step(i, 0)
     halves = []
     for half in range(2):
         part = acc_ref[:, half * LANES : (half + 1) * LANES]
@@ -102,19 +128,26 @@
     particles = masses.shape[0]
     capacity = 2 * particles // devices
     rows = VALUES * capacity // LANES
-    return _call(
+    return pl.pallas_call(
         functools.partial(_route_kernel, devices, spans),
-        jax.ShapeDtypeStruct((devices, rows, LANES), BF),
-        [
+        out_shape=jax.ShapeDtypeStruct((devices, rows, LANES), BF),
+        in_specs=[pl.BlockSpec(memory_space=pltpu.HBM)] * 4,
+        scratch_shapes=[
+            pltpu.VMEM((3, particles), F32),
+            pltpu.VMEM((1, particles), F32),
+            pltpu.VMEM((3, particles), F32),
+            pltpu.VMEM((1, particles), jnp.int32),
             pltpu.VMEM((VALUES * 2 * particles // 256, 256), F32),
-            pltpu.VMEM((devices, LANES), F32),
+            pltpu.VMEM((1, particles), jnp.int32),
+            pltpu.SemaphoreType.DMA((4,)),
         ],
-        flops=4_000_000_000,
-        moved=1_000_000,
+        compiler_params=pltpu.CompilerParams(vmem_limit_bytes=ROUTE_VMEM_LIMIT),
+        cost_estimate=pl.CostEstimate(flops=4 * 10**9, bytes_accessed=10**6, transcendentals=0),
     )(offsets, masses.reshape(1, particles), velocities, destination.reshape(1, particles))
 
 
-def _deposit_kernel(span_y, arrived_ref, cot_ref, own_ref, next_ref, prev_ref, acc_ref):
+def _deposit_kernel(span_y, arrived_ref, *refs):
+    own_ref, first_ref, second_ref, acc_ref = refs[-4:]
     sources, height, _ = arrived_ref.shape
     pieces = height // VALUES
     group = max(1, 4 // pieces)
@@ -145,42 +178,27 @@
         cell_z = (_iota((40, width), 0) >> 2).astype(F32)
         hat_z = jnp.maximum(1.0 - jnp.abs(cell_z - pos_z), 0.0)
         planes = hat_z * jnp.concatenate([charges] * 5, axis=0)
-        shares = [
-            planes * jnp.maximum(1.0 - jnp.abs(y - pos_y), 0.0) for y in range(span_y + 1)
-        ]
+        cell_y = _iota((16, width), 0).astype(F32)
+        hat_y = jnp.maximum(1.0 - jnp.abs(cell_y - pos_y), 0.0)
+        shares = [planes * hat_y[y : y + 1] for y in range(span_y + 1)]
         acc_ref[...] += _dot_lanes(jnp.concatenate(shares, axis=0).astype(BF), hat_x)
         return carry
 
-    lax.fori_loop(0, sources // group, step, 0)
+    lax.fori_loop(0, sources // group, step, 0, unroll=True)
     own = jnp.concatenate([acc_ref[y * 40 : (y + 1) * 40, :] for y in range(span_y + 1)], axis=1)
     own_ref[...] = own
-    lanes = own.shape[1]
-    next_ref[0:32, :] = jnp.concatenate([own[16:40], jnp.zeros((8, lanes), F32)], axis=0).astype(BF)
-    next_ref[32:64, 0 : lanes - LANES] = cot_ref[96:128, :]
-    next_ref[32:64, lanes - LANES :] = jnp.zeros((32, LANES), BF)
-    prev_ref[0:16, :] = own[0:16].astype(BF)
-    prev_ref[16:48, 0 : lanes - LANES] = cot_ref[0:32, :]
-    prev_ref[16:48, lanes - LANES :] = jnp.zeros((32, LANES), BF)
-
-
-def _turn_kernel(cot_ref, out_ref):
-    channels, span_y, span_z, _ = cot_ref.shape
-    size = channels * span_z
-    strips = [
-        jnp.concatenate([cot_ref[o, y].astype(F32) for o in range(channels)], axis=0)
-        for y in range(span_y)
-    ]
-    field = jnp.concatenate(strips, axis=1).astype(BF)
-    row, col = _iota((size, size), 0), _iota((size, size), 1)
-    order = (row % channels) * span_z + row // channels
-    out_ref[...] = _dot(jnp.where(col == order, 1.0, 0.0).astype(BF), field).astype(BF)
-
-
-def _merge_kernel(count_z, own_ref, cot_ref, left_ref, right_ref, wide_ref, cotw_ref, first_ref, second_ref):
+    even = lax.axis_index("gz") % 2 == 0
+    first_ref[...] = jnp.where(even, own[16:40], own[0:24]).astype(BF)
+    second_ref[...] = jnp.where(even, own[0:24], own[16:40]).astype(BF)
+
+
+def _merge_kernel(count_z, own_ref, fb_ref, fa_ref, wide_ref, first_ref, second_ref):
     keep = jnp.where(lax.axis_index("gz") < count_z - 1, 1.0, 0.0)
     even = lax.axis_index("gy") % 2 == 0
-    left = left_ref[0:32, :].astype(F32)
-    right = right_ref[0:16, :].astype(F32)
+    even_z = lax.axis_index("gz") % 2 == 0
+    first, second = fa_ref[...].astype(F32), fb_ref[...].astype(F32)
+    left = jnp.where(even_z, second, first)
+    right = jnp.where(even_z, first, second)
     own = own_ref[...]
     wide = jnp.concatenate(
         [
@@ -193,34 +211,47 @@
         axis=0,
     )
     wide_ref[...] = wide
-    cells = cot_ref.shape[1]
-    cotw_ref[0:32, :] = left_ref[32:64, 0:cells]
-    cotw_ref[32:160, :] = cot_ref[...]
-    cotw_ref[160:192, :] = right_ref[16:48, 0:cells]
-
-    def to_next(out):
-        out[:, 0:640] = wide[:, 512:1152].astype(BF)
-        for i in range(3):
-            out[:, 640 + 256 * i : 896 + 256 * i] = cotw_ref[64 * i : 64 * (i + 1), cells - 256 : cells]
-
-    def to_prev(out):
-        out[:, 0:512] = wide[:, 0:512].astype(BF)
-        out[:, 512:640] = jnp.zeros((64, 128), BF)
-        for i in range(3):
-            out[:, 640 + 256 * i : 896 + 256 * i] = cotw_ref[64 * i : 64 * (i + 1), 0:256]
-
-    @pl.when(even)
-    def _():
-        to_next(first_ref)
-        to_prev(second_ref)
-
-    @pl.when(jnp.logical_not(even))
-    def _():
-        to_prev(first_ref)
-        to_next(second_ref)
-
-
-def _weights_kernel(k1_ref, k2_ref, w1_ref, w2_ref, wb_ref, wf_ref, scr_ref):
+    to_next = wide[:, 512:1152]
+    to_prev = wide[:, 0:640]
+    first_ref[...] = jnp.where(even, to_next, to_prev).astype(BF)
+    second_ref[...] = jnp.where(even, to_prev, to_next).astype(BF)
+
+
+def _turn_kernel(cot_ref, out_ref, first_ref, second_ref):
+    channels, span_y, span_z, _ = cot_ref.shape
+    size = channels * span_z
+    strips = [
+        jnp.concatenate([cot_ref[o, y].astype(F32) for o in range(channels)], axis=0)
+        for y in range(span_y)
+    ]
+    field = jnp.concatenate(strips, axis=1).astype(BF)
+    row, col = _iota((size, size), 0), _iota((size, size), 1)
+    order = (row % channels) * span_z + row // channels
+    turned = _dot(jnp.where(col == order, 1.0, 0.0).astype(BF), field)
+    out_ref[...] = turned.astype(BF)
+    even = lax.axis_index("gz") % 2 == 0
+    to_next, to_prev = turned[size - 32 :], turned[0:32]
+    first_ref[...] = jnp.where(even, to_next, to_prev).astype(BF)
+    second_ref[...] = jnp.where(even, to_prev, to_next).astype(BF)
+
+
+def _rim_kernel(cot_ref, fb_ref, fa_ref, wide_ref, first_ref, second_ref):
+    even = lax.axis_index("gy") % 2 == 0
+    even_z = lax.axis_index("gz") % 2 == 0
+    first, second = fa_ref[...].astype(F32), fb_ref[...].astype(F32)
+    wide_ref[0:32, :] = jnp.where(even_z, second, first).astype(BF)
+    wide_ref[32:160, :] = cot_ref[...]
+    wide_ref[160:192, :] = jnp.where(even_z, first, second).astype(BF)
+    cells = wide_ref.shape[1]
+    to_next = wide_ref[:, cells - 256 : cells].astype(F32)
+    to_prev = wide_ref[:, 0:256].astype(F32)
+    first_ref[...] = jnp.where(even, to_next, to_prev).astype(BF)
+    second_ref[...] = jnp.where(even, to_prev, to_next).astype(BF)
+
+
+def _weights_kernel(
+    k1_ref, k2_ref, b1_ref, b2_ref, w1_ref, w2_ref, wb_ref, wf_ref, c1_ref, c2_ref, scr_ref
+):
     def wide(x):
         rows, cols = x.shape
         return jnp.concatenate([x, jnp.zeros((rows, LANES - cols), F32)], axis=1)
@@ -259,24 +290,19 @@
                 scr_ref[c * 8 + z : c * 8 + z + 1, :] = moved[c : c + 1, :]
         wf_ref[ty] = scr_ref[...].astype(BF)
 
+    eye = _iota((16, 16), 0) == _iota((16, 16), 1)
+    for bias_ref, out_ref in ((b1_ref, c1_ref), (b2_ref, c2_ref)):
+        one = jnp.sum(jnp.where(eye, bias_ref[...], 0.0), axis=1, keepdims=True)
+        out_ref[...] = jnp.broadcast_to(one, (16, 256))
+
 
 def _net_kernel(
-    count_y, count_z, wide_ref, cotw_ref, ra_ref, rb_ref, w1_ref, w2_ref, wb_ref, wf_ref,
+    count_y, count_z, wide_ref, cotw_ref, db_ref, da_ref, cb_ref, ca_ref, w1_ref, w2_ref, wb_ref, wf_ref,
     b1_ref, b2_ref, refined_ref, field_ref, sums_ref,
-    msg_ref, dens_ref, act_ref, del_ref, one_ref, ds_ref, ref_ref,
+    side_ref, dens_ref, act_ref, del_ref, one_ref, ds_ref, ref_ref,
 ):
     me_y, me_z = lax.axis_index("gy"), lax.axis_index("gz")
     even = me_y % 2 == 0
-
-    @pl.when(even)
-    def _():
-        msg_ref[0] = rb_ref[...]
-        msg_ref[1] = ra_ref[...]
-
-    @pl.when(jnp.logical_not(even))
-    def _():
-        msg_ref[0] = ra_ref[...]
-        msg_ref[1] = rb_ref[...]
 
     edge = _iota((1, LANES), 1)
     first_lane, last_lane = edge == 0, edge == LANES - 1
@@ -293,20 +319,18 @@
             dst[row0 + 2 * stride : row0 + 2 * stride + rows, at] = right.astype(BF)
 
     keep_y = jnp.where(me_y < count_y - 1, 1.0, 0.0)
-    up = msg_ref[0, :, 0:640].astype(F32)
-    down = msg_ref[1, :, 0:512].astype(F32)
+    first, second = da_ref[...].astype(F32), db_ref[...].astype(F32)
+    up = jnp.where(even, second, first)
+    down = jnp.where(even, first, second)
+    first, second = ca_ref[...].astype(F32), cb_ref[...].astype(F32)
+    side_ref[0] = jnp.where(even, second, first)
+    side_ref[1] = jnp.where(even, first, second)
     shifted(up[:, 0:512], dens_ref, 0, 64, 0)
     shifted(wide_ref[:, 0:128] + up[:, 512:640], dens_ref, 0, 64, 512)
     shifted(wide_ref[:, 128:1024], dens_ref, 0, 64, 640)
     shifted(wide_ref[:, 1024:1152] * keep_y + down[:, 0:128], dens_ref, 0, 64, 1536)
     shifted(down[:, 128:512], dens_ref, 0, 64, 1664)
 
-    eye = _iota((16, 16), 0) == _iota((16, 16), 1)
-
-    def column(bias_ref, count):
-        one = jnp.sum(jnp.where(eye, bias_ref[...], 0.0), axis=1, keepdims=True)
-        return jnp.concatenate([one] * count, axis=0)
-
     def inside_z(rows, halo):
         z = me_z * 8 - halo + (_iota((rows, 1), 0) >> 4)
         return jnp.where((z >= 0) & (z < count_z * 8), 1.0, 0.0)
@@ -315,7 +339,7 @@
         y = me_y * 8 - halo + first + (_iota((1, 256), 1) >> 7)
         return jnp.where((y >= 0) & (y < count_y * 8), 1.0, 0.0)
 
-    bias = column(b1_ref, 14)
+    bias = jnp.concatenate([b1_ref[...]] * 14, axis=0)
     mask_z = inside_z(224, 3)
     for tx in range(3):
         act_ref[tx * 256 + 224 : (tx + 1) * 256, :] = jnp.zeros((32, act_ref.shape[1]), BF)
@@ -331,7 +355,7 @@
             ds_ref[:, (n - 1) * 256 : n * 256] = sig[mid] * (1.0 + pre[mid] - act[mid])
         shifted(act * (mask_z * inside_y(2 * n, 3)), act_ref, 0, 256, n * 256)
 
-    bias = column(b2_ref, 12)
+    bias = jnp.concatenate([b2_ref[...]] * 12, axis=0)
     for n in range(6):
         pre = bias
         for ty in range(3):
@@ -340,14 +364,11 @@
         sig = 0.5 * jnp.tanh(0.5 * pre) + 0.5
         act = pre * sig
         if n == 0 or n == 5:
-            side = 0 if n == 0 else 1
-            cot = jnp.concatenate(
-                [msg_ref[side, :, 640 + 256 * i : 896 + 256 * i] for i in range(3)], axis=0
-            )
+            cot = side_ref[0 if n == 0 else 1]
         else:
-            cot = cotw_ref[:, (n - 1) * 256 : n * 256]
+            cot = cotw_ref[:, (n - 1) * 256 : n * 256].astype(F32)
             ref_ref[:, (n - 1) * 256 : n * 256] = act[32:160].astype(BF)
-        shifted(cot.astype(F32) * (sig * (1.0 + pre - act)), del_ref, 0, 192, n * 256)
+        shifted(cot * (sig * (1.0 + pre - act)), del_ref, 0, 192, n * 256)
 
     mask_z = inside_z(160, 1)
     for n in range(5):
@@ -466,25 +487,38 @@
     lanes = span_y * span_x
     both = ("gy", "gz")
 
+    def along(axis, first, second):
+        count = lax.axis_size(axis)
+        inner = [(i, i ^ 1) for i in range(count)]
+        outer = [(i, i + 1) for i in range(1, count - 1, 2)]
+        outer = outer + [(j, i) for i, j in outer]
+        far = lax.ppermute(second, axis, outer)
+        return far, lax.ppermute(first, axis, inner)
+
     outgoing = _route(offsets, masses, velocities, destination, devices, spans)
     arrived = lax.all_to_all(outgoing, both, split_axis=0, concat_axis=0, tiled=True)
 
-    turned = _call(
-        _turn_kernel, jax.ShapeDtypeStruct((channels * span_z, lanes), BF), flops=10**8, moved=10**6
+    turned, first, second = _call(
+        _turn_kernel,
+        (
+            jax.ShapeDtypeStruct((channels * span_z, lanes), BF),
+            jax.ShapeDtypeStruct((32, lanes), BF),
+            jax.ShapeDtypeStruct((32, lanes), BF),
+        ),
+        flops=10**8,
+        moved=10**6,
     )(cotangent)
-    own, to_next, to_prev = _call(
-        functools.partial(_deposit_kernel, span_y),
+    cot_wide, first, second = _call(
+        _rim_kernel,
         (
-            jax.ShapeDtypeStruct((40, lanes + span_x), F32),
-            jax.ShapeDtypeStruct((64, lanes + span_x), BF),
-            jax.ShapeDtypeStruct((48, lanes + span_x), BF),
+            jax.ShapeDtypeStruct((192, lanes), BF),
+            jax.ShapeDtypeStruct((192, 256), BF),
+            jax.ShapeDtypeStruct((192, 256), BF),
         ),
-        [pltpu.VMEM((40 * (span_y + 1), span_x), F32)],
-        flops=4 * 10**9,
+        flops=10**6,
         moved=10**6,
-    )(arrived, turned)
-    left = lax.ppermute(to_next, "gz", [(i, i + 1) for i in range(count_z - 1)])
-    right = lax.ppermute(to_prev, "gz", [(i + 1, i) for i in range(count_z - 1)])
+    )(turned, *along("gz", first, second))
+    rims = along("gy", first, second)
     k1 = first_weight.transpose(2, 3, 4, 1, 0).reshape(27, 4, 16)
     k2 = second_weight.transpose(2, 3, 4, 0, 1).reshape(27, 16, 16)
     banded = _call(
@@ -494,27 +528,37 @@
             jax.ShapeDtypeStruct((3, 192, 768), BF),
             jax.ShapeDtypeStruct((3, 160, 640), BF),
             jax.ShapeDtypeStruct((3, 32, 512), BF),
+            jax.ShapeDtypeStruct((16, 256), F32),
+            jax.ShapeDtypeStruct((16, 256), F32),
         ),
         [pltpu.VMEM((32, 512), F32)],
         flops=2 * 10**9,
         moved=2 * 10**6,
-    )(k1, k2)
-    wide, cot_wide, first, second = _call(
+    )(k1, k2, first_bias.reshape(1, 16), second_bias.reshape(1, 16))
+
+    earlier = [banded[0]]
+    own, first, second = pl.pallas_call(
+        functools.partial(_deposit_kernel, span_y),
+        out_shape=(
+            jax.ShapeDtypeStruct((40, lanes + span_x), F32),
+            jax.ShapeDtypeStruct((24, lanes + span_x), BF),
+            jax.ShapeDtypeStruct((24, lanes + span_x), BF),
+        ),
+        in_specs=[pl.BlockSpec(memory_space=pltpu.VMEM)] + [pl.BlockSpec(memory_space=pl.ANY)] * len(earlier),
+        scratch_shapes=[pltpu.VMEM((40 * (span_y + 1), span_x), F32)],
+        compiler_params=pltpu.CompilerParams(vmem_limit_bytes=VMEM_LIMIT),
+        cost_estimate=pl.CostEstimate(flops=4 * 10**9, bytes_accessed=10**6, transcendentals=0),
+    )(arrived, *earlier)
+    wide, first, second = _call(
         functools.partial(_merge_kernel, count_z),
         (
             jax.ShapeDtypeStruct((64, lanes + span_x), F32),
-            jax.ShapeDtypeStruct((192, lanes), BF),
-            jax.ShapeDtypeStruct((64, 1408), BF),
-            jax.ShapeDtypeStruct((64, 1408), BF),
+            jax.ShapeDtypeStruct((64, 640), BF),
+            jax.ShapeDtypeStruct((64, 640), BF),
         ),
         flops=10**6,
         moved=10**6,
-    )(own, turned, left, right)
-    inner = [(i, i ^ 1) for i in range(count_y)]
-    outer = [(i, i + 1) for i in range(1, count_y - 1, 2)]
-    outer = outer + [(j, i) for i, j in outer]
-    got_first = lax.ppermute(first, "gy", inner)
-    got_second = lax.ppermute(second, "gy", outer)
+    )(own, *along("gz", first, second))
     refined, grad_field, sums = _call(
         functools.partial(_net_kernel, count_y, count_z),
         (
@@ -523,7 +567,7 @@
             jax.ShapeDtypeStruct((80, LANES), F32),
         ),
         [
-            pltpu.VMEM((2, 64, 1408), BF),
+            pltpu.VMEM((2, 192, 256), F32),
             pltpu.VMEM((192, 2048), BF),
             pltpu.VMEM((768, 1792), BF),
             pltpu.VMEM((576, 1536), BF),
@@ -533,10 +577,7 @@
         ],
         flops=6 * 10**9,
         moved=2 * 10**6,
-    )(
-        wide, cot_wide, got_first, got_second, *banded,
-        first_bias.reshape(1, 16), second_bias.reshape(1, 16),
-    )
+    )(wide, cot_wide, *along("gy", first, second), *rims, *banded)
 
     def swapped(value, bit):
         return lax.ppermute(value, both, [(i, i ^ bit) for i in range(devices)])

time: 83.2 us -> 64.2 us (0.77)
  waiting for transfers between devices: 24.2 us -> 12.2 us
  Pallas kernels: 28.5 us -> 18 us
  starting transfers between devices: 25.3 us -> 32.3 us
  local copies, waits for them, and re-layouts: 4.03 us -> 0.68 us
    pallas_call x3 -> x4, Pallas kernels: 20 us -> 9.4 us  [the longest x1 4.99 us: _route(): pl.pallas_call(functools.partial(_route_kernel, devices, spans), out_shap...]
    ppermute x4 -> x8, starting transfers between devices: 4.85 us -> 14.9 us  [the longest x4 12.1 us: along(): return (far, lax.ppermute(first, axis, inner))]
    all_to_all x1, waiting for transfers between devices: 11.9 us -> 4.28 us  [_local(): lax.all_to_all(outgoing, both, split_axis=0, concat_axis=0, tiled=True)]
    ppermute x4 -> x8, waiting for transfers between devices: 5.4 us -> 0.93 us  [the longest x4 0.92 us: along(): return (far, lax.ppermute(first, axis, inner))]
    unnamed x18 -> x10, local copies, waits for them, and re-layouts: 4.03 us -> 0.68 us
    ppermute x7, starting transfers between devices: 13.1 us -> 10.1 us  [swapped(): return lax.ppermute(value, both, [(i, i ^ bit) for i in range(devices)])]
  transfers between devices with their start and end apart: 12 -> 16, of which waited for: 8 -> 8; matrix products, arithmetic and copies ran while one was open for 0% -> 0% of each run, Pallas kernels for 2% -> 10%
where the time goes in v2:
time: 64.2 us; the launch traced here: 63.9 us
  starting transfers between devices  32.3 us (50%)
  Pallas kernels  18 us (28%)
  waiting for transfers between devices  12.2 us (19%)
  between operations  0.76 us (1%)
  local copies, waits for them, and re-layouts  0.68 us (1%)
    ppermute x4, starting transfers between devices, along(): return (far, lax.ppermute(first, axis, inner))  12.1 us
    ppermute x7, starting transfers between devices, swapped(): return lax.ppermute(value, both, [(i, i ^ bit) for i in range(devices)])  10.1 us
    all_to_all x1, starting transfers between devices, _local(): lax.all_to_all(outgoing, both, split_axis=0, concat_axis=0, tiled=True)  7.31 us
    ppermute x7, waiting for transfers between devices, swapped(): return lax.ppermute(value, both, [(i, i ^ bit) for i in range(devices)])  6.99 us
    pallas_call x1, Pallas kernels, _local(): _call(functools.partial(_net_kernel, count_y, count_z), (jax.ShapeDtypeSt...  5.93 us
    pallas_call x1, Pallas kernels, _route(): pl.pallas_call(functools.partial(_route_kernel, devices, spans), out_shap...  4.99 us
    all_to_all x1, waiting for transfers between devices, _local(): lax.all_to_all(outgoing, both, split_axis=0, concat_axis=0, tiled=True)  4.28 us
    pallas_call x1, Pallas kernels, _local(): pl.pallas_call(functools.partial(_deposit_kernel, span_y), out_shape=(jax...  4.09 us
  transfers between devices with their start and end apart: 16, of which 8 were waited for; matrix products, arithmetic and copies ran while one was open for 0% of the time, Pallas kernels for 10%

profile of v2, /device:TPU:0, one launch (start us, length us, event | category | flops | bytes accessed | tf_op | source)
XLA Modules:
  0.0 63.9 jit_solution(1087293802046908662)
XLA Ops:
  0.6 5.0 %shard_map.136 = bf16[32,40,128]{2,1,0:T(8,128)(2,1)} custom-call(f32[3,8192]{1,0:T(4,128)} %off_hbm.1, f32[1,8192]{1,0:T(1,128)} %bitcast.24, f32[3,8192]{1,0:T(4,128)} %vel_hbm.1, s32[1,8192]{1,0:T(1,128)} %bitcast.25), custom_call_target="tpu_custom_call" | custom-call | flops 4000000000 | bytes 1000000 | tf_op jit(solution)/shard_map/pallas_call | solution.py:131
  5.6 7.3 %all-to-all-start = ((bf16[32,40,128]{2,1,0:T(8,128)(2,1)}), bf16[32,40,128]{2,1,0:T(8,128)(2,1)S(1)}, u32[]{:S(2)}, u32[]{:S(2)}) async-start(bf16[32,40,128]{2,1,0:T(8,128)(2,1)} %shard_map.136), calls=%async_computation | async-start | bytes 655360 | tf_op jit(solution)/shard_map/all_to_all | solution.py:499
  13.9 4.5 %collective-permute-start.3 = (bf16[32,1024]{1,0:T(8,128)(2,1)S(1)}, bf16[32,1024]{1,0:T(8,128)(2,1)S(1)}, u32[]{:S(2)}, u32[]{:S(2)}) collective-permute-start(bf16[32,1024]{1,0:T(8,128)(2,1)S(1)} %get-tuple-element.38), channel_id=1, source_target_pairs={{0,1},{1,0},{2,3},{3,2},{4,5},{5,4},{6,7},{7,6},{8,9},{9,8},{10,11... | collective-permute-start | bytes 196616 | tf_op jit(solution)/shard_map/ppermute | solution.py:496
  19.1 1.7 %shard_map.137 = (bf16[3,224,256]{2,1,0:T(8,128)(2,1)S(1)}, bf16[3,192,768]{2,1,0:T(8,128)(2,1)S(1)}, bf16[3,160,640]{2,1,0:T(8,128)(2,1)S(1)}, bf16[3,32,512]{2...) custom-call(bf16[27,4,16]{2,1,0:T(4,128)(2,1)S(1)} %bitcast.19, bf16[27,16,16]{2,1,0:T(8,128)(2,1)S(1)} %bitcast.18, ...), custom_call_target="tpu_custom_call" | custom-call | flops 2000000000 | bytes 2000000 | tf_op jit(solution)/shard_map/pallas_call | solution.py:524
  20.8 4.3 %all-to-all-done.arrived_ref = bf16[32,40,128]{2,1,0:T(8,128)(2,1)S(1)} async-done(((bf16[32,40,128]{2,1,0:T(8,128)(2,1)}), bf16[32,40,128]{2,1,0:T(8,128)(2,1)S(1)}, u32[]{:S(2)}, u32[]{:S(2)}) %all-to-all-start) | async-done | bytes 327712 | tf_op jit(solution)/shard_map/all_to_all | solution.py:499
  25.1 4.1 %shard_map.138 = (f32[40,1152]{1,0:T(8,128)S(1)}, bf16[24,1152]{1,0:T(8,128)(2,1)S(1)}, bf16[24,1152]{1,0:T(8,128)(2,1)S(1)}) custom-call(bf16[32,40,128]{2,1,0:T(8,128)(2,1)S(1)} %all-to-all-done.arrived_ref, bf16[3,224,256]{2,1,0:T(8,128)(2,1)S(1)} %get-tuple-element.31.refs_0_.w1_ref), custom_call_target="tpu_custom_call" | custom-call | flops 4000000000 | bytes 1000000 | tf_op jit(solution)/shard_map/pallas_call | solution.py:540
  29.9 3.6 %collective-permute-start.1 = (bf16[24,1152]{1,0:T(8,128)(2,1)S(1)}, bf16[24,1152]{1,0:T(8,128)(2,1)S(1)}, u32[]{:S(2)}, u32[]{:S(2)}) collective-permute-start(bf16[24,1152]{1,0:T(8,128)(2,1)S(1)} %get-tuple-element.34), channel_id=1, source_target_pairs={{0,1},{1,0},{2,3},{3,2},{4,5},{5,4},{6,7},{7,6},{8,9},{9,8},{10,11... | collective-permute-start | bytes 165896 | tf_op jit(solution)/shard_map/ppermute | solution.py:496
  34.2 2.0 %collective-permute-start.7 = (bf16[192,256]{1,0:T(8,128)(2,1)S(1)}, bf16[192,256]{1,0:T(8,128)(2,1)S(1)}, u32[]{:S(2)}, u32[]{:S(2)}) collective-permute-start(bf16[192,256]{1,0:T(8,128)(2,1)S(1)} %get-tuple-element.43), channel_id=1, source_target_pairs={{0,8},{8,0},{16,24},{24,16},{1,9},{9,1},{17,25},{25,17},{2,10},{10... | collective-permute-start | bytes 294920 | tf_op jit(solution)/shard_map/ppermute | solution.py:496
  36.3 0.8 %collective-permute-start.4 = (bf16[64,640]{1,0:T(8,128)(2,1)S(1)}, bf16[64,640]{1,0:T(8,128)(2,1)S(1)}, u32[]{:S(2)}, u32[]{:S(2)}) collective-permute-start(bf16[64,640]{1,0:T(8,128)(2,1)S(1)} %get-tuple-element.40), channel_id=1, source_target_pairs={{8,16},{16,8},{9,17},{17,9},{10,18},{18,10},{11,19},{19,11},{12,20... | collective-permute-start | bytes 245768 | tf_op jit(solution)/shard_map/ppermute | solution.py:495
  37.2 2.0 %collective-permute-start.5 = (bf16[64,640]{1,0:T(8,128)(2,1)S(1)}, bf16[64,640]{1,0:T(8,128)(2,1)S(1)}, u32[]{:S(2)}, u32[]{:S(2)}) collective-permute-start(bf16[64,640]{1,0:T(8,128)(2,1)S(1)} %get-tuple-element.41), channel_id=1, source_target_pairs={{0,8},{8,0},{16,24},{24,16},{1,9},{9,1},{17,25},{25,17},{2,10},{10... | collective-permute-start | bytes 245768 | tf_op jit(solution)/shard_map/ppermute | solution.py:496
  39.1 0.9 %collective-permute-done.5.da_ref = bf16[64,640]{1,0:T(8,128)(2,1)S(1)} collective-permute-done((bf16[64,640]{1,0:T(8,128)(2,1)S(1)}, bf16[64,640]{1,0:T(8,128)(2,1)S(1)}, u32[]{:S(2)}, u32[]{:S(2)}) %collective-permute-start.5) | collective-permute-done | bytes 81952 | tf_op jit(solution)/shard_map/ppermute | solution.py:496
  40.0 5.9 %shard_map.142 = (bf16[16,8,8,128]{3,2,1,0:T(8,128)(2,1)}, f32[4,8,8,128]{3,2,1,0:T(8,128)}, f32[80,128]{1,0:T(8,128)S(1)}) custom-call(f32[64,1152]{1,0:T(8,128)S(1)} %get-tuple-element.35.wide_ref, bf16[192,1024]{1,0:T(8,128)(2,1)S(1)} %get-tuple-element.39.cotw_ref, bf16[64,640]{1,0:T(8,128)(2,1)S(1)} %collective-permute-done.4.db_ref, ...), custom_call_target="tpu_custom_call" | custom-call | flops 6000000000 | bytes 2000000 | tf_op jit(solution)/shard_map/pallas_call | solution.py:562
  46.0 2.1 %collective-permute-start.8 = (f32[80,128]{1,0:T(8,128)S(1)}, f32[80,128]{1,0:T(8,128)S(1)}, u32[]{:S(2)}, u32[]{:S(2)}) collective-permute-start(f32[80,128]{1,0:T(8,128)S(1)} %get-tuple-element.51), channel_id=1, source_target_pairs={{0,8},{1,9},{2,10},{3,11},{4,12},{5,13},{6,14},{7,15},{8,0},{9,1},... | collective-permute-start | bytes 122888 | tf_op jit(solution)/shard_map/ppermute | solution.py:583
  48.1 0.9 %collective-permute-done.8 = f32[80,128]{1,0:T(8,128)S(1)} collective-permute-done((f32[80,128]{1,0:T(8,128)S(1)}, f32[80,128]{1,0:T(8,128)S(1)}, u32[]{:S(2)}, u32[]{:S(2)}) %collective-permute-start.8) | collective-permute-done | bytes 40992 | tf_op jit(solution)/shard_map/ppermute | solution.py:583
  49.0 2.3 %collective-permute-start.11 = (f32[80,128]{1,0:T(8,128)S(1)}, f32[80,128]{1,0:T(8,128)S(1)}, u32[]{:S(2)}, u32[]{:S(2)}) collective-permute-start(f32[80,128]{1,0:T(8,128)S(1)} %add.12), channel_id=1, source_target_pairs={{0,17},{1,16},{2,19},{3,18},{4,21},{5,20},{6,23},{7,22},{8,25},{9,... | collective-permute-start | bytes 122888 | tf_op jit(solution)/shard_map/ppermute | solution.py:583
  51.3 1.2 %collective-permute-start.9 = (f32[80,128]{1,0:T(8,128)S(1)}, f32[80,128]{1,0:T(8,128)S(1)}, u32[]{:S(2)}, u32[]{:S(2)}) collective-permute-start(f32[80,128]{1,0:T(8,128)S(1)} %add.12), channel_id=1, source_target_pairs={{0,16},{1,17},{2,18},{3,19},{4,20},{5,21},{6,22},{7,23},{8,24},{9,... | collective-permute-start | bytes 122888 | tf_op jit(solution)/shard_map/ppermute | solution.py:583
  52.5 1.4 %collective-permute-done.11 = f32[80,128]{1,0:T(8,128)S(1)} collective-permute-done((f32[80,128]{1,0:T(8,128)S(1)}, f32[80,128]{1,0:T(8,128)S(1)}, u32[]{:S(2)}, u32[]{:S(2)}) %collective-permute-start.11) | collective-permute-done | bytes 40992 | tf_op jit(solution)/shard_map/ppermute | solution.py:583
  53.9 1.4 %collective-permute-done.10 = f32[80,128]{1,0:T(8,128)S(1)} collective-permute-done((f32[80,128]{1,0:T(8,128)S(1)}, f32[80,128]{1,0:T(8,128)S(1)}, u32[]{:S(2)}, u32[]{:S(2)}) %collective-permute-start.10) | collective-permute-done | bytes 40992 | tf_op jit(solution)/shard_map/ppermute | solution.py:583
  55.3 2.4 %collective-permute-start.14 = (f32[80,128]{1,0:T(8,128)S(1)}, f32[80,128]{1,0:T(8,128)S(1)}, u32[]{:S(2)}, u32[]{:S(2)}) collective-permute-start(f32[80,128]{1,0:T(8,128)S(1)} %add_add_fusion.a_ref), channel_id=1, source_target_pairs={{0,6},{1,7},{2,4},{3,5},{4,2},{5,3},{6,0},{7,1},{8,14},{9,15},{10,... | collective-permute-start | bytes 122888 | tf_op jit(solution)/shard_map/ppermute | solution.py:583
  57.7 1.0 %collective-permute-start.13 = (f32[80,128]{1,0:T(8,128)S(1)}, f32[80,128]{1,0:T(8,128)S(1)}, u32[]{:S(2)}, u32[]{:S(2)}) collective-permute-start(f32[80,128]{1,0:T(8,128)S(1)} %add_add_fusion.a_ref), channel_id=1, source_target_pairs={{0,4},{1,5},{2,6},{3,7},{4,0},{5,1},{6,2},{7,3},{8,12},{9,13},{10,... | collective-permute-start | bytes 122888 | tf_op jit(solution)/shard_map/ppermute | solution.py:583
  58.7 1.0 %collective-permute-start.12 = (f32[80,128]{1,0:T(8,128)S(1)}, f32[80,128]{1,0:T(8,128)S(1)}, u32[]{:S(2)}, u32[]{:S(2)}) collective-permute-start(f32[80,128]{1,0:T(8,128)S(1)} %add_add_fusion.a_ref), channel_id=1, source_target_pairs={{0,2},{1,3},{2,0},{3,1},{4,6},{5,7},{6,4},{7,5},{8,10},{9,11},{10,... | collective-permute-start | bytes 122888 | tf_op jit(solution)/shard_map/ppermute | solution.py:583
  59.8 1.7 %collective-permute-done.14.d_ref = f32[80,128]{1,0:T(8,128)S(1)} collective-permute-done((f32[80,128]{1,0:T(8,128)S(1)}, f32[80,128]{1,0:T(8,128)S(1)}, u32[]{:S(2)}, u32[]{:S(2)}) %collective-permute-start.14) | collective-permute-done | bytes 40992 | tf_op jit(solution)/shard_map/ppermute | solution.py:583
  61.4 1.2 %collective-permute-done.13.c_ref = f32[80,128]{1,0:T(8,128)S(1)} collective-permute-done((f32[80,128]{1,0:T(8,128)S(1)}, f32[80,128]{1,0:T(8,128)S(1)}, u32[]{:S(2)}, u32[]{:S(2)}) %collective-permute-start.13) | collective-permute-done | bytes 40992 | tf_op jit(solution)/shard_map/ppermute | solution.py:583
  63.0 0.9 %shard_map.143 = (f32[27,4,16]{2,1,0:T(4,128)}, f32[1,16]{1,0:T(1,128)}, f32[27,16,16]{2,1,0:T(8,128)}, f32[1,16]{1,0:T(1,128)}) custom-call(f32[80,128]{1,0:T(8,128)S(1)} %add_add_fusion.a_ref, f32[80,128]{1,0:T(8,128)S(1)} %collective-permute-done.12.b_ref, f32[80,128]{1,0:T(8,128)S(1)} %collective-permute-done.13.c_ref, ...), custom_call_target="tpu_custom_call" | custom-call | flops 100000 | bytes 100000 | tf_op jit(solution)/shard_map/pallas_call | solution.py:599
  (28 shorter events, 3.5 us)
Async XLA Ops:
  5.6 7.3 %copy-start = (bf16[16,8,8,128]{3,2,1,0:T(8,128)(2,1)S(1)}, bf16[16,8,8,128]{3,2,1,0:T(8,128)(2,1)}, u32[]{:S(2)}) copy-start(bf16[16,8,8,128]{3,2,1,0:T(8,128)(2,1)} %cot_ref.1) | copy-start | bytes 786436
  5.6 19.5 %all-to-all-start = ((bf16[32,40,128]{2,1,0:T(8,128)(2,1)}), bf16[32,40,128]{2,1,0:T(8,128)(2,1)S(1)}, u32[]{:S(2)}, u32[]{:S(2)}) async-start(bf16[32,40,128]{2,1,0:T(8,128)(2,1)} %shard_map.136), calls=%async_computation | async-start | bytes 655360 | tf_op jit(solution)/shard_map/all_to_all | solution.py:499
  13.0 5.5 %copy-start.1 = (bf16[16,16,3,3,3]{1,0,4,3,2:T(8,128)(2,1)S(1)}, bf16[16,16,3,3,3]{1,0,4,3,2:T(8,128)(2,1)}, u32[]{:S(2)}) copy-start(bf16[16,16,3,3,3]{1,0,4,3,2:T(8,128)(2,1)} %param.15) | copy-start | bytes 41476
  13.0 5.5 %copy-start.2 = (bf16[16,4,3,3,3]{0,1,4,3,2:T(4,128)(2,1)S(1)}, bf16[16,4,3,3,3]{0,1,4,3,2:T(4,128)(2,1)}, u32[]{:S(2)}) copy-start(bf16[16,4,3,3,3]{0,1,4,3,2:T(4,128)(2,1)} %param.13) | copy-start | bytes 10372
  13.2 20.2 %collective-permute-start.2 = (bf16[32,1024]{1,0:T(8,128)(2,1)S(1)}, bf16[32,1024]{1,0:T(8,128)(2,1)S(1)}, u32[]{:S(2)}, u32[]{:S(2)}) collective-permute-start(bf16[32,1024]{1,0:T(8,128)(2,1)S(1)} %get-tuple-element.37), channel_id=1, source_target_pairs={{1,2},{3,4},{5,6},{2,1},{4,3},{6,5},{9,10},{11,12},{13,14},{10,9},... | collective-permute-start | bytes 196616 | tf_op jit(solution)/shard_map/ppermute | solution.py:495
  13.9 19.6 %collective-permute-start.3 = (bf16[32,1024]{1,0:T(8,128)(2,1)S(1)}, bf16[32,1024]{1,0:T(8,128)(2,1)S(1)}, u32[]{:S(2)}, u32[]{:S(2)}) collective-permute-start(bf16[32,1024]{1,0:T(8,128)(2,1)S(1)} %get-tuple-element.38), channel_id=1, source_target_pairs={{0,1},{1,0},{2,3},{3,2},{4,5},{5,4},{6,7},{7,6},{8,9},{9,8},{10,11... | collective-permute-start | bytes 196616 | tf_op jit(solution)/shard_map/ppermute | solution.py:496
  18.4 0.7 %copy-start.3 = (f32[16]{0:T(128)S(1)}, f32[16]{0:T(128)}, u32[]{:S(2)}) copy-start(f32[16]{0:T(128)} %param.14) | copy-start | bytes 196
  18.4 0.7 %copy-start.4 = (f32[16]{0:T(128)S(1)}, f32[16]{0:T(128)}, u32[]{:S(2)}) copy-start(f32[16]{0:T(128)} %param.16) | copy-start | bytes 196
  29.2 7.0 %collective-permute-start = (bf16[24,1152]{1,0:T(8,128)(2,1)S(1)}, bf16[24,1152]{1,0:T(8,128)(2,1)S(1)}, u32[]{:S(2)}, u32[]{:S(2)}) collective-permute-start(bf16[24,1152]{1,0:T(8,128)(2,1)S(1)} %get-tuple-element.33), channel_id=1, source_target_pairs={{1,2},{3,4},{5,6},{2,1},{4,3},{6,5},{9,10},{11,12},{13,14},{10,9},... | collective-permute-start | bytes 165896 | tf_op jit(solution)/shard_map/ppermute | solution.py:495
  29.9 6.4 %collective-permute-start.1 = (bf16[24,1152]{1,0:T(8,128)(2,1)S(1)}, bf16[24,1152]{1,0:T(8,128)(2,1)S(1)}, u32[]{:S(2)}, u32[]{:S(2)}) collective-permute-start(bf16[24,1152]{1,0:T(8,128)(2,1)S(1)} %get-tuple-element.34), channel_id=1, source_target_pairs={{0,1},{1,0},{2,3},{3,2},{4,5},{5,4},{6,7},{7,6},{8,9},{9,8},{10,11... | collective-permute-start | bytes 165896 | tf_op jit(solution)/shard_map/ppermute | solution.py:496
  33.6 5.6 %collective-permute-start.6 = (bf16[192,256]{1,0:T(8,128)(2,1)S(1)}, bf16[192,256]{1,0:T(8,128)(2,1)S(1)}, u32[]{:S(2)}, u32[]{:S(2)}) collective-permute-start(bf16[192,256]{1,0:T(8,128)(2,1)S(1)} %get-tuple-element.42), channel_id=1, source_target_pairs={{8,16},{16,8},{9,17},{17,9},{10,18},{18,10},{11,19},{19,11},{12,20... | collective-permute-start | bytes 294920 | tf_op jit(solution)/shard_map/ppermute | solution.py:495
  34.2 4.9 %collective-permute-start.7 = (bf16[192,256]{1,0:T(8,128)(2,1)S(1)}, bf16[192,256]{1,0:T(8,128)(2,1)S(1)}, u32[]{:S(2)}, u32[]{:S(2)}) collective-permute-start(bf16[192,256]{1,0:T(8,128)(2,1)S(1)} %get-tuple-element.43), channel_id=1, source_target_pairs={{0,8},{8,0},{16,24},{24,16},{1,9},{9,1},{17,25},{25,17},{2,10},{10... | collective-permute-start | bytes 294920 | tf_op jit(solution)/shard_map/ppermute | solution.py:496
  36.3 2.8 %collective-permute-start.4 = (bf16[64,640]{1,0:T(8,128)(2,1)S(1)}, bf16[64,640]{1,0:T(8,128)(2,1)S(1)}, u32[]{:S(2)}, u32[]{:S(2)}) collective-permute-start(bf16[64,640]{1,0:T(8,128)(2,1)S(1)} %get-tuple-element.40), channel_id=1, source_target_pairs={{8,16},{16,8},{9,17},{17,9},{10,18},{18,10},{11,19},{19,11},{12,20... | collective-permute-start | bytes 245768 | tf_op jit(solution)/shard_map/ppermute | solution.py:495
  37.2 2.9 %collective-permute-start.5 = (bf16[64,640]{1,0:T(8,128)(2,1)S(1)}, bf16[64,640]{1,0:T(8,128)(2,1)S(1)}, u32[]{:S(2)}, u32[]{:S(2)}) collective-permute-start(bf16[64,640]{1,0:T(8,128)(2,1)S(1)} %get-tuple-element.41), channel_id=1, source_target_pairs={{0,8},{8,0},{16,24},{24,16},{1,9},{9,1},{17,25},{25,17},{2,10},{10... | collective-permute-start | bytes 245768 | tf_op jit(solution)/shard_map/ppermute | solution.py:496
  46.0 3.0 %collective-permute-start.8 = (f32[80,128]{1,0:T(8,128)S(1)}, f32[80,128]{1,0:T(8,128)S(1)}, u32[]{:S(2)}, u32[]{:S(2)}) collective-permute-start(f32[80,128]{1,0:T(8,128)S(1)} %get-tuple-element.51), channel_id=1, source_target_pairs={{0,8},{1,9},{2,10},{3,11},{4,12},{5,13},{6,14},{7,15},{8,0},{9,1},... | collective-permute-start | bytes 122888 | tf_op jit(solution)/shard_map/ppermute | solution.py:583
  49.0 4.9 %collective-permute-start.11 = (f32[80,128]{1,0:T(8,128)S(1)}, f32[80,128]{1,0:T(8,128)S(1)}, u32[]{:S(2)}, u32[]{:S(2)}) collective-permute-start(f32[80,128]{1,0:T(8,128)S(1)} %add.12), channel_id=1, source_target_pairs={{0,17},{1,16},{2,19},{3,18},{4,21},{5,20},{6,23},{7,22},{8,25},{9,... | collective-permute-start | bytes 122888 | tf_op jit(solution)/shard_map/ppermute | solution.py:583
  51.3 4.0 %collective-permute-start.10 = (f32[80,128]{1,0:T(8,128)S(1)}, f32[80,128]{1,0:T(8,128)S(1)}, u32[]{:S(2)}, u32[]{:S(2)}) collective-permute-start(f32[80,128]{1,0:T(8,128)S(1)} %add.12), channel_id=1, source_target_pairs={{0,1},{1,0},{2,3},{3,2},{4,5},{5,4},{6,7},{7,6},{8,9},{9,8},{10,11... | collective-permute-start | bytes 122888 | tf_op jit(solution)/shard_map/ppermute | solution.py:583
  51.3 4.0 %collective-permute-start.9 = (f32[80,128]{1,0:T(8,128)S(1)}, f32[80,128]{1,0:T(8,128)S(1)}, u32[]{:S(2)}, u32[]{:S(2)}) collective-permute-start(f32[80,128]{1,0:T(8,128)S(1)} %add.12), channel_id=1, source_target_pairs={{0,16},{1,17},{2,18},{3,19},{4,20},{5,21},{6,22},{7,23},{8,24},{9,... | collective-permute-start | bytes 122888 | tf_op jit(solution)/shard_map/ppermute | solution.py:583
  55.3 6.1 %collective-permute-start.14 = (f32[80,128]{1,0:T(8,128)S(1)}, f32[80,128]{1,0:T(8,128)S(1)}, u32[]{:S(2)}, u32[]{:S(2)}) collective-permute-start(f32[80,128]{1,0:T(8,128)S(1)} %add_add_fusion.a_ref), channel_id=1, source_target_pairs={{0,6},{1,7},{2,4},{3,5},{4,2},{5,3},{6,0},{7,1},{8,14},{9,15},{10,... | collective-permute-start | bytes 122888 | tf_op jit(solution)/shard_map/ppermute | solution.py:583
  57.7 4.9 %collective-permute-start.13 = (f32[80,128]{1,0:T(8,128)S(1)}, f32[80,128]{1,0:T(8,128)S(1)}, u32[]{:S(2)}, u32[]{:S(2)}) collective-permute-start(f32[80,128]{1,0:T(8,128)S(1)} %add_add_fusion.a_ref), channel_id=1, source_target_pairs={{0,4},{1,5},{2,6},{3,7},{4,0},{5,1},{6,2},{7,3},{8,12},{9,13},{10,... | collective-permute-start | bytes 122888 | tf_op jit(solution)/shard_map/ppermute | solution.py:583
  58.7 4.3 %collective-permute-start.12 = (f32[80,128]{1,0:T(8,128)S(1)}, f32[80,128]{1,0:T(8,128)S(1)}, u32[]{:S(2)}, u32[]{:S(2)}) collective-permute-start(f32[80,128]{1,0:T(8,128)S(1)} %add_add_fusion.a_ref), channel_id=1, source_target_pairs={{0,2},{1,3},{2,0},{3,1},{4,6},{5,7},{6,4},{7,5},{8,10},{9,11},{10,... | collective-permute-start | bytes 122888 | tf_op jit(solution)/shard_map/ppermute | solution.py:583

commit v3 on v2

--- a/solution.py
+++ b/solution.py
@@ -10,8 +10,13 @@
 
 BF = jnp.bfloat16
 F32 = jnp.float32
+I32 = jnp.int32
+I16 = jnp.int16
+MASS_TOP, SPEED_TOP = 4.0, 5.0
+STEPS = 32767.0
 LANES = 128
-VALUES = 10
+PARTS = 10
+VALUES = 8
 VMEM_LIMIT = 48 * 1024 * 1024
 ROUTE_VMEM_LIMIT = 60 * 1024 * 1024
 ROUTE_WIDTH = 512
@@ -40,7 +45,7 @@
 
 
 def _route_kernel(
-    devices, spans, off_hbm, mass_hbm, vel_hbm, dest_hbm, out_ref,
+    devices, off_hbm, mass_hbm, vel_hbm, dest_hbm, out_ref,
     off_ref, mass_ref, vel_ref, dest_ref, acc_ref, rank_ref, sems,
 ):
     loads = [
@@ -94,10 +99,10 @@
             lo = rank + jnp.where(upper, LANES, 0)
         rows = []
         for axis in range(3):
-            position = off_ref[axis : axis + 1, lanes] * spans[axis]
-            coarse = position.astype(BF)
-            rows.append(coarse)
-            rows.append((position - coarse.astype(F32)).astype(BF))
+            position = jnp.floor(off_ref[axis : axis + 1, lanes] * (2.0 * STEPS + 1.0) + 0.5)
+            coarse = jnp.floor(position * (1.0 / 256.0))
+            rows.append(coarse.astype(BF))
+            rows.append((position - 256.0 * coarse).astype(BF))
         mass = mass_ref[:, lanes]
         rows.append(mass.astype(BF))
         for axis in range(3):
@@ -116,28 +121,40 @@
     halves = []
     for half in range(2):
         part = acc_ref[:, half * LANES : (half + 1) * LANES]
+
+        def value(i):
+            return part[i * hi_count : (i + 1) * hi_count]
+
+        sent = [256.0 * value(2 * i) + value(2 * i + 1) - (STEPS + 1.0) for i in range(3)]
+        sent.append(value(6) * (STEPS / MASS_TOP))
+        for i in range(7, 10):
+            root = jnp.sqrt(jnp.abs(value(i)) * (1.0 / (MASS_TOP * SPEED_TOP))) * STEPS
+            sent.append(jnp.where(value(i) < 0.0, -root, root))
+        sent = [jnp.floor(x + 0.5) for x in sent]
+        sent.append(jnp.zeros_like(sent[0]))
+        part = jnp.concatenate(sent, axis=0)
         if pieces >= 2:
             halves.append(part.reshape(VALUES * pieces // 2, devices, LANES))
         else:
             halves.append(part.reshape(VALUES, devices // 2, LANES))
     whole = jnp.concatenate(halves, axis=0 if pieces >= 2 else 1)
-    out_ref[...] = jnp.transpose(whole, (1, 0, 2)).astype(BF)
-
-
-def _route(offsets, masses, velocities, destination, devices, spans):
+    out_ref[...] = jnp.transpose(whole, (1, 0, 2)).astype(I32).astype(I16)
+
+
+def _route(offsets, masses, velocities, destination, devices):
     particles = masses.shape[0]
     capacity = 2 * particles // devices
     rows = VALUES * capacity // LANES
     return pl.pallas_call(
-        functools.partial(_route_kernel, devices, spans),
-        out_shape=jax.ShapeDtypeStruct((devices, rows, LANES), BF),
+        functools.partial(_route_kernel, devices),
+        out_shape=jax.ShapeDtypeStruct((devices, rows, LANES), I16),
         in_specs=[pl.BlockSpec(memory_space=pltpu.HBM)] * 4,
         scratch_shapes=[
             pltpu.VMEM((3, particles), F32),
             pltpu.VMEM((1, particles), F32),
             pltpu.VMEM((3, particles), F32),
             pltpu.VMEM((1, particles), jnp.int32),
-            pltpu.VMEM((VALUES * 2 * particles // 256, 256), F32),
+            pltpu.VMEM((PARTS * 2 * particles // 256, 256), F32),
             pltpu.VMEM((1, particles), jnp.int32),
             pltpu.SemaphoreType.DMA((4,)),
         ],
@@ -146,7 +163,7 @@
     )(offsets, masses.reshape(1, particles), velocities, destination.reshape(1, particles))
 
 
-def _deposit_kernel(span_y, arrived_ref, *refs):
+def _deposit_kernel(span_y, span_z, arrived_ref, *refs):
     own_ref, first_ref, second_ref, acc_ref = refs[-4:]
     sources, height, _ = arrived_ref.shape
     pieces = height // VALUES
@@ -168,11 +185,17 @@
         return jnp.concatenate(parts, axis=1)
 
     def step(i, carry):
-        blocks = [arrived_ref[i * group + g].astype(F32) for g in range(group)]
-        pos_y = value_rows(blocks, 0) + value_rows(blocks, 1)
-        pos_z = value_rows(blocks, 2) + value_rows(blocks, 3)
-        pos_x = value_rows(blocks, 4) + value_rows(blocks, 5)
-        charges = jnp.concatenate([value_rows(blocks, 6 + c) for c in range(4)] * 2, axis=0)
+        blocks = [arrived_ref[i * group + g].astype(I32).astype(F32) for g in range(group)]
+
+        def position(axis, span):
+            return (value_rows(blocks, axis) + (STEPS + 1.0)) * (span / (2.0 * STEPS + 1.0))
+
+        pos_y, pos_z, pos_x = position(0, span_y), position(1, span_z), position(2, span_x)
+        charges = [value_rows(blocks, 3) * (MASS_TOP / STEPS)]
+        for c in range(4, 7):
+            root = value_rows(blocks, c) * (1.0 / STEPS)
+            charges.append(root * jnp.abs(root) * (MASS_TOP * SPEED_TOP))
+        charges = jnp.concatenate(charges * 2, axis=0)
         cell_x = _iota((span_x, width), 0).astype(F32)
         hat_x = jnp.maximum(1.0 - jnp.abs(cell_x - pos_x), 0.0).astype(BF)
         cell_z = (_iota((40, width), 0) >> 2).astype(F32)
@@ -197,8 +220,9 @@
     even = lax.axis_index("gy") % 2 == 0
     even_z = lax.axis_index("gz") % 2 == 0
     first, second = fa_ref[...].astype(F32), fb_ref[...].astype(F32)
-    left = jnp.where(even_z, second, first)
-    right = jnp.where(even_z, first, second)
+    me_z = lax.axis_index("gz")
+    left = jnp.where(me_z > 0, jnp.where(even_z, second, first), 0.0)
+    right = jnp.where(me_z < count_z - 1, jnp.where(even_z, first, second), 0.0)
     own = own_ref[...]
     wide = jnp.concatenate(
         [
@@ -235,13 +259,16 @@
     second_ref[...] = jnp.where(even, to_prev, to_next).astype(BF)
 
 
-def _rim_kernel(cot_ref, fb_ref, fa_ref, wide_ref, first_ref, second_ref):
+def _rim_kernel(count_z, cot_ref, fb_ref, fa_ref, wide_ref, first_ref, second_ref):
     even = lax.axis_index("gy") % 2 == 0
     even_z = lax.axis_index("gz") % 2 == 0
     first, second = fa_ref[...].astype(F32), fb_ref[...].astype(F32)
-    wide_ref[0:32, :] = jnp.where(even_z, second, first).astype(BF)
+    me_z = lax.axis_index("gz")
+    left = jnp.where(me_z > 0, jnp.where(even_z, second, first), 0.0)
+    right = jnp.where(me_z < count_z - 1, jnp.where(even_z, first, second), 0.0)
+    wide_ref[0:32, :] = left.astype(BF)
     wide_ref[32:160, :] = cot_ref[...]
-    wide_ref[160:192, :] = jnp.where(even_z, first, second).astype(BF)
+    wide_ref[160:192, :] = right.astype(BF)
     cells = wide_ref.shape[1]
     to_next = wide_ref[:, cells - 256 : cells].astype(F32)
     to_prev = wide_ref[:, 0:256].astype(F32)
@@ -319,12 +346,15 @@
             dst[row0 + 2 * stride : row0 + 2 * stride + rows, at] = right.astype(BF)
 
     keep_y = jnp.where(me_y < count_y - 1, 1.0, 0.0)
-    first, second = da_ref[...].astype(F32), db_ref[...].astype(F32)
-    up = jnp.where(even, second, first)
-    down = jnp.where(even, first, second)
-    first, second = ca_ref[...].astype(F32), cb_ref[...].astype(F32)
-    side_ref[0] = jnp.where(even, second, first)
-    side_ref[1] = jnp.where(even, first, second)
+    has_up, has_down = me_y > 0, me_y < count_y - 1
+
+    def sides(a_ref, b_ref):
+        first, second = a_ref[...].astype(F32), b_ref[...].astype(F32)
+        up = jnp.where(has_up, jnp.where(even, second, first), 0.0)
+        return up, jnp.where(has_down, jnp.where(even, first, second), 0.0)
+
+    up, down = sides(da_ref, db_ref)
+    side_ref[0], side_ref[1] = sides(ca_ref, cb_ref)
     shifted(up[:, 0:512], dens_ref, 0, 64, 0)
     shifted(wide_ref[:, 0:128] + up[:, 512:640], dens_ref, 0, 64, 512)
     shifted(wide_ref[:, 128:1024], dens_ref, 0, 64, 640)
@@ -483,19 +513,22 @@
     count_z = lax.axis_size("gz")
     devices = count_y * count_z
     channels, span_y, span_z, span_x = cotangent.shape
-    spans = (float(span_y), float(span_z), float(span_x))
     lanes = span_y * span_x
     both = ("gy", "gz")
 
-    def along(axis, first, second):
+    def along(axis, first, second, wrapped):
         count = lax.axis_size(axis)
         inner = [(i, i ^ 1) for i in range(count)]
         outer = [(i, i + 1) for i in range(1, count - 1, 2)]
+        if wrapped == 1:
+            outer.append((count - 1, 0))
         outer = outer + [(j, i) for i, j in outer]
+        if wrapped == 2:
+            outer = outer + [(0, 0), (count - 1, count - 1)]
         far = lax.ppermute(second, axis, outer)
         return far, lax.ppermute(first, axis, inner)
 
-    outgoing = _route(offsets, masses, velocities, destination, devices, spans)
+    outgoing = _route(offsets, masses, velocities, destination, devices)
     arrived = lax.all_to_all(outgoing, both, split_axis=0, concat_axis=0, tiled=True)
 
     turned, first, second = _call(
@@ -509,7 +542,7 @@
         moved=10**6,
     )(cotangent)
     cot_wide, first, second = _call(
-        _rim_kernel,
+        functools.partial(_rim_kernel, count_z),
         (
             jax.ShapeDtypeStruct((192, lanes), BF),
             jax.ShapeDtypeStruct((192, 256), BF),
@@ -517,8 +550,8 @@
         ),
         flops=10**6,
         moved=10**6,
-    )(turned, *along("gz", first, second))
-    rims = along("gy", first, second)
+    )(turned, *along("gz", first, second, 0))
+    rims = along("gy", first, second, 1)
     k1 = first_weight.transpose(2, 3, 4, 1, 0).reshape(27, 4, 16)
     k2 = second_weight.transpose(2, 3, 4, 0, 1).reshape(27, 16, 16)
     banded = _call(
@@ -538,7 +571,7 @@
 
     earlier = [banded[0]]
     own, first, second = pl.pallas_call(
-        functools.partial(_deposit_kernel, span_y),
+        functools.partial(_deposit_kernel, span_y, span_z),
         out_shape=(
             jax.ShapeDtypeStruct((40, lanes + span_x), F32),
             jax.ShapeDtypeStruct((24, lanes + span_x), BF),
@@ -558,7 +591,7 @@
         ),
         flops=10**6,
         moved=10**6,
-    )(own, *along("gz", first, second))
+    )(own, *along("gz", first, second, 1))
     refined, grad_field, sums = _call(
         functools.partial(_net_kernel, count_y, count_z),
         (
@@ -577,7 +610,7 @@
         ],
         flops=6 * 10**9,
         moved=2 * 10**6,
-    )(wide, cot_wide, *along("gy", first, second), *rims, *banded)
+    )(wide, cot_wide, *along("gy", first, second, 1), *rims, *banded)
 
     def swapped(value, bit):
         return lax.ppermute(value, both, [(i, i ^ bit) for i in range(devices)])

time: 64.2 us -> 60.9 us (0.949)
  starting transfers between devices: 32.3 us -> 25 us
  waiting for transfers between devices: 12.2 us -> 16.1 us
    ppermute x4, waiting for transfers between devices: 0.01 us -> 6.72 us  [along(): far = lax.ppermute(second, axis, outer)]
    ppermute x4, starting transfers between devices: 12.1 us -> 6.71 us  [along(): return (far, lax.ppermute(first, axis, inner))]
    ppermute x7, starting transfers between devices: 10.1 us -> 8 us  [swapped(): return lax.ppermute(value, both, [(i, i ^ bit) for i in range(devices)])]
    all_to_all x1, waiting for transfers between devices: 4.28 us -> 2.6 us  [_local(): lax.all_to_all(outgoing, both, split_axis=0, concat_axis=0, tiled=True)]
    ppermute x4, waiting for transfers between devices: 0.92 us -> 0.01 us  [along(): return (far, lax.ppermute(first, axis, inner))]
  transfers between devices with their start and end apart: 16 -> 16, of which waited for: 8 -> 9; matrix products, arithmetic and copies ran while one was open for 0% -> 0% of each run, Pallas kernels for 10% -> 10%
where the time goes in v3:
time: 60.9 us; the launch traced here: 60.7 us
  starting transfers between devices  25 us (41%)
  Pallas kernels  18.2 us (30%)
  waiting for transfers between devices  16.1 us (26%)
  between operations  0.76 us (1%)
  local copies, waits for them, and re-layouts  0.68 us (1%)
    ppermute x7, starting transfers between devices, swapped(): return lax.ppermute(value, both, [(i, i ^ bit) for i in range(devices)])  8 us
    all_to_all x1, starting transfers between devices, _local(): lax.all_to_all(outgoing, both, split_axis=0, concat_axis=0, tiled=True)  7.31 us
    ppermute x7, waiting for transfers between devices, swapped(): return lax.ppermute(value, both, [(i, i ^ bit) for i in range(devices)])  6.74 us
    ppermute x4, waiting for transfers between devices, along(): far = lax.ppermute(second, axis, outer)  6.72 us
    ppermute x4, starting transfers between devices, along(): return (far, lax.ppermute(first, axis, inner))  6.71 us
    pallas_call x1, Pallas kernels, _local(): _call(functools.partial(_net_kernel, count_y, count_z), (jax.ShapeDtypeSt...  5.93 us
    pallas_call x1, Pallas kernels, _route(): pl.pallas_call(functools.partial(_route_kernel, devices), out_shape=jax.S...  5.09 us
    pallas_call x1, Pallas kernels, _local(): pl.pallas_call(functools.partial(_deposit_kernel, span_y, span_z), out_sh...  4.16 us
  transfers between devices with their start and end apart: 16, of which 9 were waited for; matrix products, arithmetic and copies ran while one was open for 0% of the time, Pallas kernels for 10%

profile of v3, /device:TPU:0, one launch (start us, length us, event | category | flops | bytes accessed | tf_op | source)
XLA Modules:
  0.0 60.7 jit_solution(15918848182353307071)
XLA Ops:
  0.6 5.1 %shard_map.136 = s16[32,32,128]{2,1,0:T(8,128)(2,1)} custom-call(f32[3,8192]{1,0:T(4,128)} %off_hbm.1, f32[1,8192]{1,0:T(1,128)} %bitcast.24, f32[3,8192]{1,0:T(4,128)} %vel_hbm.1, s32[1,8192]{1,0:T(1,128)} %bitcast.25), custom_call_target="tpu_custom_call" | custom-call | flops 4000000000 | bytes 1000000 | tf_op jit(solution)/shard_map/pallas_call | solution.py:148
  5.7 7.3 %all-to-all-start = ((s16[32,32,128]{2,1,0:T(8,128)(2,1)}), s16[32,32,128]{2,1,0:T(8,128)(2,1)S(1)}, u32[]{:S(2)}, u32[]{:S(2)}) async-start(s16[32,32,128]{2,1,0:T(8,128)(2,1)} %shard_map.136), calls=%async_computation | async-start | bytes 524288 | tf_op jit(solution)/shard_map/all_to_all | solution.py:532
  13.3 0.8 %collective-permute-start.2 = (bf16[32,1024]{1,0:T(8,128)(2,1)S(1)}, bf16[32,1024]{1,0:T(8,128)(2,1)S(1)}, u32[]{:S(2)}, u32[]{:S(2)}) collective-permute-start(bf16[32,1024]{1,0:T(8,128)(2,1)S(1)} %get-tuple-element.37), channel_id=1, source_target_pairs={{1,2},{3,4},{5,6},{2,1},{4,3},{6,5},{9,10},{11,12},{13,14},{10,9},... | collective-permute-start | bytes 196616 | tf_op jit(solution)/shard_map/ppermute | solution.py:528
  14.2 4.5 %collective-permute-start.3 = (bf16[32,1024]{1,0:T(8,128)(2,1)S(1)}, bf16[32,1024]{1,0:T(8,128)(2,1)S(1)}, u32[]{:S(2)}, u32[]{:S(2)}) collective-permute-start(bf16[32,1024]{1,0:T(8,128)(2,1)S(1)} %get-tuple-element.38), channel_id=1, source_target_pairs={{0,1},{1,0},{2,3},{3,2},{4,5},{5,4},{6,7},{7,6},{8,9},{9,8},{10,11... | collective-permute-start | bytes 196616 | tf_op jit(solution)/shard_map/ppermute | solution.py:529
  19.4 1.7 %shard_map.137 = (bf16[3,224,256]{2,1,0:T(8,128)(2,1)S(1)}, bf16[3,192,768]{2,1,0:T(8,128)(2,1)S(1)}, bf16[3,160,640]{2,1,0:T(8,128)(2,1)S(1)}, bf16[3,32,512]{2...) custom-call(bf16[27,4,16]{2,1,0:T(4,128)(2,1)S(1)} %bitcast.19, bf16[27,16,16]{2,1,0:T(8,128)(2,1)S(1)} %bitcast.18, ...), custom_call_target="tpu_custom_call" | custom-call | flops 2000000000 | bytes 2000000 | tf_op jit(solution)/shard_map/pallas_call | solution.py:557
  21.1 2.6 %all-to-all-done.arrived_ref = s16[32,32,128]{2,1,0:T(8,128)(2,1)S(1)} async-done(((s16[32,32,128]{2,1,0:T(8,128)(2,1)}), s16[32,32,128]{2,1,0:T(8,128)(2,1)S(1)}, u32[]{:S(2)}, u32[]{:S(2)}) %all-to-all-start) | async-done | bytes 262176 | tf_op jit(solution)/shard_map/all_to_all | solution.py:532
  23.7 4.2 %shard_map.138 = (f32[40,1152]{1,0:T(8,128)S(1)}, bf16[24,1152]{1,0:T(8,128)(2,1)S(1)}, bf16[24,1152]{1,0:T(8,128)(2,1)S(1)}) custom-call(s16[32,32,128]{2,1,0:T(8,128)(2,1)S(1)} %all-to-all-done.arrived_ref, bf16[3,224,256]{2,1,0:T(8,128)(2,1)S(1)} %get-tuple-element.31.refs_0_.w1_ref), custom_call_target="tpu_custom_call" | custom-call | flops 4000000000 | bytes 1000000 | tf_op jit(solution)/shard_map/pallas_call | solution.py:573
  27.9 2.0 %collective-permute-start = (bf16[24,1152]{1,0:T(8,128)(2,1)S(1)}, bf16[24,1152]{1,0:T(8,128)(2,1)S(1)}, u32[]{:S(2)}, u32[]{:S(2)}) collective-permute-start(bf16[24,1152]{1,0:T(8,128)(2,1)S(1)} %get-tuple-element.33), channel_id=1, source_target_pairs={{1,2},{3,4},{5,6},{7,0},{2,1},{4,3},{6,5},{0,7},{9,10},{11,12},{13... | collective-permute-start | bytes 165896 | tf_op jit(solution)/shard_map/ppermute | solution.py:528
  30.6 0.7 %collective-permute-start.7 = (bf16[192,256]{1,0:T(8,128)(2,1)S(1)}, bf16[192,256]{1,0:T(8,128)(2,1)S(1)}, u32[]{:S(2)}, u32[]{:S(2)}) collective-permute-start(bf16[192,256]{1,0:T(8,128)(2,1)S(1)} %get-tuple-element.43), channel_id=1, source_target_pairs={{0,8},{8,0},{16,24},{24,16},{1,9},{9,1},{17,25},{25,17},{2,10},{10... | collective-permute-start | bytes 294920 | tf_op jit(solution)/shard_map/ppermute | solution.py:529
  31.3 3.5 %collective-permute-done.fb_ref = bf16[24,1152]{1,0:T(8,128)(2,1)S(1)} collective-permute-done((bf16[24,1152]{1,0:T(8,128)(2,1)S(1)}, bf16[24,1152]{1,0:T(8,128)(2,1)S(1)}, u32[]{:S(2)}, u32[]{:S(2)}) %collective-permute-start) | collective-permute-done | bytes 55328 | tf_op jit(solution)/shard_map/ppermute | solution.py:528
  34.9 1.0 %collective-permute-start.5 = (bf16[64,640]{1,0:T(8,128)(2,1)S(1)}, bf16[64,640]{1,0:T(8,128)(2,1)S(1)}, u32[]{:S(2)}, u32[]{:S(2)}) collective-permute-start(bf16[64,640]{1,0:T(8,128)(2,1)S(1)} %get-tuple-element.41), channel_id=1, source_target_pairs={{0,8},{8,0},{16,24},{24,16},{1,9},{9,1},{17,25},{25,17},{2,10},{10... | collective-permute-start | bytes 245768 | tf_op jit(solution)/shard_map/ppermute | solution.py:529
  35.9 3.2 %collective-permute-done.4.db_ref = bf16[64,640]{1,0:T(8,128)(2,1)S(1)} collective-permute-done((bf16[64,640]{1,0:T(8,128)(2,1)S(1)}, bf16[64,640]{1,0:T(8,128)(2,1)S(1)}, u32[]{:S(2)}, u32[]{:S(2)}) %collective-permute-start.4) | collective-permute-done | bytes 81952 | tf_op jit(solution)/shard_map/ppermute | solution.py:528
  39.1 5.9 %shard_map.142 = (bf16[16,8,8,128]{3,2,1,0:T(8,128)(2,1)}, f32[4,8,8,128]{3,2,1,0:T(8,128)}, f32[80,128]{1,0:T(8,128)S(1)}) custom-call(f32[64,1152]{1,0:T(8,128)S(1)} %get-tuple-element.35.wide_ref, bf16[192,1024]{1,0:T(8,128)(2,1)S(1)} %get-tuple-element.39.cotw_ref, bf16[64,640]{1,0:T(8,128)(2,1)S(1)} %collective-permute-done.4.db_ref, ...), custom_call_target="tpu_custom_call" | custom-call | flops 6000000000 | bytes 2000000 | tf_op jit(solution)/shard_map/pallas_call | solution.py:595
  45.1 1.2 %collective-permute-done.8 = f32[80,128]{1,0:T(8,128)S(1)} collective-permute-done((f32[80,128]{1,0:T(8,128)S(1)}, f32[80,128]{1,0:T(8,128)S(1)}, u32[]{:S(2)}, u32[]{:S(2)}) %collective-permute-start.8) | collective-permute-done | bytes 40992 | tf_op jit(solution)/shard_map/ppermute | solution.py:616
  46.3 0.9 %collective-permute-start.11 = (f32[80,128]{1,0:T(8,128)S(1)}, f32[80,128]{1,0:T(8,128)S(1)}, u32[]{:S(2)}, u32[]{:S(2)}) collective-permute-start(f32[80,128]{1,0:T(8,128)S(1)} %add.12), channel_id=1, source_target_pairs={{0,17},{1,16},{2,19},{3,18},{4,21},{5,20},{6,23},{7,22},{8,25},{9,... | collective-permute-start | bytes 122888 | tf_op jit(solution)/shard_map/ppermute | solution.py:616
  47.2 1.7 %collective-permute-start.10 = (f32[80,128]{1,0:T(8,128)S(1)}, f32[80,128]{1,0:T(8,128)S(1)}, u32[]{:S(2)}, u32[]{:S(2)}) collective-permute-start(f32[80,128]{1,0:T(8,128)S(1)} %add.12), channel_id=1, source_target_pairs={{0,1},{1,0},{2,3},{3,2},{4,5},{5,4},{6,7},{7,6},{8,9},{9,8},{10,11... | collective-permute-start | bytes 122888 | tf_op jit(solution)/shard_map/ppermute | solution.py:616
  48.9 0.9 %collective-permute-start.9 = (f32[80,128]{1,0:T(8,128)S(1)}, f32[80,128]{1,0:T(8,128)S(1)}, u32[]{:S(2)}, u32[]{:S(2)}) collective-permute-start(f32[80,128]{1,0:T(8,128)S(1)} %add.12), channel_id=1, source_target_pairs={{0,16},{1,17},{2,18},{3,19},{4,20},{5,21},{6,22},{7,23},{8,24},{9,... | collective-permute-start | bytes 122888 | tf_op jit(solution)/shard_map/ppermute | solution.py:616
  49.8 1.8 %collective-permute-done.11 = f32[80,128]{1,0:T(8,128)S(1)} collective-permute-done((f32[80,128]{1,0:T(8,128)S(1)}, f32[80,128]{1,0:T(8,128)S(1)}, u32[]{:S(2)}, u32[]{:S(2)}) %collective-permute-start.11) | collective-permute-done | bytes 40992 | tf_op jit(solution)/shard_map/ppermute | solution.py:616
  51.7 1.3 %collective-permute-done.9 = f32[80,128]{1,0:T(8,128)S(1)} collective-permute-done((f32[80,128]{1,0:T(8,128)S(1)}, f32[80,128]{1,0:T(8,128)S(1)}, u32[]{:S(2)}, u32[]{:S(2)}) %collective-permute-start.9) | collective-permute-done | bytes 40992 | tf_op jit(solution)/shard_map/ppermute | solution.py:616
  53.0 1.2 %collective-permute-start.14 = (f32[80,128]{1,0:T(8,128)S(1)}, f32[80,128]{1,0:T(8,128)S(1)}, u32[]{:S(2)}, u32[]{:S(2)}) collective-permute-start(f32[80,128]{1,0:T(8,128)S(1)} %add_add_fusion.a_ref), channel_id=1, source_target_pairs={{0,6},{1,7},{2,4},{3,5},{4,2},{5,3},{6,0},{7,1},{8,14},{9,15},{10,... | collective-permute-start | bytes 122888 | tf_op jit(solution)/shard_map/ppermute | solution.py:616
  54.7 2.7 %collective-permute-start.12 = (f32[80,128]{1,0:T(8,128)S(1)}, f32[80,128]{1,0:T(8,128)S(1)}, u32[]{:S(2)}, u32[]{:S(2)}) collective-permute-start(f32[80,128]{1,0:T(8,128)S(1)} %add_add_fusion.a_ref), channel_id=1, source_target_pairs={{0,2},{1,3},{2,0},{3,1},{4,6},{5,7},{6,4},{7,5},{8,10},{9,11},{10,... | collective-permute-start | bytes 122888 | tf_op jit(solution)/shard_map/ppermute | solution.py:616
  57.4 1.4 %collective-permute-done.14.d_ref = f32[80,128]{1,0:T(8,128)S(1)} collective-permute-done((f32[80,128]{1,0:T(8,128)S(1)}, f32[80,128]{1,0:T(8,128)S(1)}, u32[]{:S(2)}, u32[]{:S(2)}) %collective-permute-start.14) | collective-permute-done | bytes 40992 | tf_op jit(solution)/shard_map/ppermute | solution.py:616
  58.8 1.0 %collective-permute-done.13.c_ref = f32[80,128]{1,0:T(8,128)S(1)} collective-permute-done((f32[80,128]{1,0:T(8,128)S(1)}, f32[80,128]{1,0:T(8,128)S(1)}, u32[]{:S(2)}, u32[]{:S(2)}) %collective-permute-start.13) | collective-permute-done | bytes 40992 | tf_op jit(solution)/shard_map/ppermute | solution.py:616
  59.8 0.9 %shard_map.143 = (f32[27,4,16]{2,1,0:T(4,128)}, f32[1,16]{1,0:T(1,128)}, f32[27,16,16]{2,1,0:T(8,128)}, f32[1,16]{1,0:T(1,128)}) custom-call(f32[80,128]{1,0:T(8,128)S(1)} %add_add_fusion.a_ref, f32[80,128]{1,0:T(8,128)S(1)} %collective-permute-done.12.b_ref, f32[80,128]{1,0:T(8,128)S(1)} %collective-permute-done.13.c_ref, ...), custom_call_target="tpu_custom_call" | custom-call | flops 100000 | bytes 100000 | tf_op jit(solution)/shard_map/pallas_call | solution.py:632
  (28 shorter events, 2.5 us)
Async XLA Ops:
  5.7 7.3 %copy-start = (bf16[16,8,8,128]{3,2,1,0:T(8,128)(2,1)S(1)}, bf16[16,8,8,128]{3,2,1,0:T(8,128)(2,1)}, u32[]{:S(2)}) copy-start(bf16[16,8,8,128]{3,2,1,0:T(8,128)(2,1)} %cot_ref.1) | copy-start | bytes 786436
  5.7 18.0 %all-to-all-start = ((s16[32,32,128]{2,1,0:T(8,128)(2,1)}), s16[32,32,128]{2,1,0:T(8,128)(2,1)S(1)}, u32[]{:S(2)}, u32[]{:S(2)}) async-start(s16[32,32,128]{2,1,0:T(8,128)(2,1)} %shard_map.136), calls=%async_computation | async-start | bytes 524288 | tf_op jit(solution)/shard_map/all_to_all | solution.py:532
  13.1 5.7 %copy-start.1 = (bf16[16,16,3,3,3]{1,0,4,3,2:T(8,128)(2,1)S(1)}, bf16[16,16,3,3,3]{1,0,4,3,2:T(8,128)(2,1)}, u32[]{:S(2)}) copy-start(bf16[16,16,3,3,3]{1,0,4,3,2:T(8,128)(2,1)} %param.15) | copy-start | bytes 41476
  13.1 5.6 %copy-start.2 = (bf16[16,4,3,3,3]{0,1,4,3,2:T(4,128)(2,1)S(1)}, bf16[16,4,3,3,3]{0,1,4,3,2:T(4,128)(2,1)}, u32[]{:S(2)}) copy-start(bf16[16,4,3,3,3]{0,1,4,3,2:T(4,128)(2,1)} %param.13) | copy-start | bytes 10372
  13.3 17.1 %collective-permute-start.2 = (bf16[32,1024]{1,0:T(8,128)(2,1)S(1)}, bf16[32,1024]{1,0:T(8,128)(2,1)S(1)}, u32[]{:S(2)}, u32[]{:S(2)}) collective-permute-start(bf16[32,1024]{1,0:T(8,128)(2,1)S(1)} %get-tuple-element.37), channel_id=1, source_target_pairs={{1,2},{3,4},{5,6},{2,1},{4,3},{6,5},{9,10},{11,12},{13,14},{10,9},... | collective-permute-start | bytes 196616 | tf_op jit(solution)/shard_map/ppermute | solution.py:528
  14.2 16.2 %collective-permute-start.3 = (bf16[32,1024]{1,0:T(8,128)(2,1)S(1)}, bf16[32,1024]{1,0:T(8,128)(2,1)S(1)}, u32[]{:S(2)}, u32[]{:S(2)}) collective-permute-start(bf16[32,1024]{1,0:T(8,128)(2,1)S(1)} %get-tuple-element.38), channel_id=1, source_target_pairs={{0,1},{1,0},{2,3},{3,2},{4,5},{5,4},{6,7},{7,6},{8,9},{9,8},{10,11... | collective-permute-start | bytes 196616 | tf_op jit(solution)/shard_map/ppermute | solution.py:529
  18.7 0.7 %copy-start.3 = (f32[16]{0:T(128)S(1)}, f32[16]{0:T(128)}, u32[]{:S(2)}) copy-start(f32[16]{0:T(128)} %param.14) | copy-start | bytes 196
  18.7 0.7 %copy-start.4 = (f32[16]{0:T(128)S(1)}, f32[16]{0:T(128)}, u32[]{:S(2)}) copy-start(f32[16]{0:T(128)} %param.16) | copy-start | bytes 196
  27.9 6.9 %collective-permute-start = (bf16[24,1152]{1,0:T(8,128)(2,1)S(1)}, bf16[24,1152]{1,0:T(8,128)(2,1)S(1)}, u32[]{:S(2)}, u32[]{:S(2)}) collective-permute-start(bf16[24,1152]{1,0:T(8,128)(2,1)S(1)} %get-tuple-element.33), channel_id=1, source_target_pairs={{1,2},{3,4},{5,6},{7,0},{2,1},{4,3},{6,5},{0,7},{9,10},{11,12},{13... | collective-permute-start | bytes 165896 | tf_op jit(solution)/shard_map/ppermute | solution.py:528
  29.8 5.0 %collective-permute-start.1 = (bf16[24,1152]{1,0:T(8,128)(2,1)S(1)}, bf16[24,1152]{1,0:T(8,128)(2,1)S(1)}, u32[]{:S(2)}, u32[]{:S(2)}) collective-permute-start(bf16[24,1152]{1,0:T(8,128)(2,1)S(1)} %get-tuple-element.34), channel_id=1, source_target_pairs={{0,1},{1,0},{2,3},{3,2},{4,5},{5,4},{6,7},{7,6},{8,9},{9,8},{10,11... | collective-permute-start | bytes 165896 | tf_op jit(solution)/shard_map/ppermute | solution.py:529
  30.5 5.4 %collective-permute-start.6 = (bf16[192,256]{1,0:T(8,128)(2,1)S(1)}, bf16[192,256]{1,0:T(8,128)(2,1)S(1)}, u32[]{:S(2)}, u32[]{:S(2)}) collective-permute-start(bf16[192,256]{1,0:T(8,128)(2,1)S(1)} %get-tuple-element.42), channel_id=1, source_target_pairs={{8,16},{24,0},{16,8},{0,24},{9,17},{25,1},{17,9},{1,25},{10,18},{2... | collective-permute-start | bytes 294920 | tf_op jit(solution)/shard_map/ppermute | solution.py:528
  30.6 5.3 %collective-permute-start.7 = (bf16[192,256]{1,0:T(8,128)(2,1)S(1)}, bf16[192,256]{1,0:T(8,128)(2,1)S(1)}, u32[]{:S(2)}, u32[]{:S(2)}) collective-permute-start(bf16[192,256]{1,0:T(8,128)(2,1)S(1)} %get-tuple-element.43), channel_id=1, source_target_pairs={{0,8},{8,0},{16,24},{24,16},{1,9},{9,1},{17,25},{25,17},{2,10},{10... | collective-permute-start | bytes 294920 | tf_op jit(solution)/shard_map/ppermute | solution.py:529
  34.9 4.2 %collective-permute-start.4 = (bf16[64,640]{1,0:T(8,128)(2,1)S(1)}, bf16[64,640]{1,0:T(8,128)(2,1)S(1)}, u32[]{:S(2)}, u32[]{:S(2)}) collective-permute-start(bf16[64,640]{1,0:T(8,128)(2,1)S(1)} %get-tuple-element.40), channel_id=1, source_target_pairs={{8,16},{24,0},{16,8},{0,24},{9,17},{25,1},{17,9},{1,25},{10,18},{2... | collective-permute-start | bytes 245768 | tf_op jit(solution)/shard_map/ppermute | solution.py:528
  34.9 4.1 %collective-permute-start.5 = (bf16[64,640]{1,0:T(8,128)(2,1)S(1)}, bf16[64,640]{1,0:T(8,128)(2,1)S(1)}, u32[]{:S(2)}, u32[]{:S(2)}) collective-permute-start(bf16[64,640]{1,0:T(8,128)(2,1)S(1)} %get-tuple-element.41), channel_id=1, source_target_pairs={{0,8},{8,0},{16,24},{24,16},{1,9},{9,1},{17,25},{25,17},{2,10},{10... | collective-permute-start | bytes 245768 | tf_op jit(solution)/shard_map/ppermute | solution.py:529
  45.0 1.3 %collective-permute-start.8 = (f32[80,128]{1,0:T(8,128)S(1)}, f32[80,128]{1,0:T(8,128)S(1)}, u32[]{:S(2)}, u32[]{:S(2)}) collective-permute-start(f32[80,128]{1,0:T(8,128)S(1)} %get-tuple-element.51), channel_id=1, source_target_pairs={{0,8},{1,9},{2,10},{3,11},{4,12},{5,13},{6,14},{7,15},{8,0},{9,1},... | collective-permute-start | bytes 122888 | tf_op jit(solution)/shard_map/ppermute | solution.py:616
  46.3 5.2 %collective-permute-start.11 = (f32[80,128]{1,0:T(8,128)S(1)}, f32[80,128]{1,0:T(8,128)S(1)}, u32[]{:S(2)}, u32[]{:S(2)}) collective-permute-start(f32[80,128]{1,0:T(8,128)S(1)} %add.12), channel_id=1, source_target_pairs={{0,17},{1,16},{2,19},{3,18},{4,21},{5,20},{6,23},{7,22},{8,25},{9,... | collective-permute-start | bytes 122888 | tf_op jit(solution)/shard_map/ppermute | solution.py:616
  47.2 4.4 %collective-permute-start.10 = (f32[80,128]{1,0:T(8,128)S(1)}, f32[80,128]{1,0:T(8,128)S(1)}, u32[]{:S(2)}, u32[]{:S(2)}) collective-permute-start(f32[80,128]{1,0:T(8,128)S(1)} %add.12), channel_id=1, source_target_pairs={{0,1},{1,0},{2,3},{3,2},{4,5},{5,4},{6,7},{7,6},{8,9},{9,8},{10,11... | collective-permute-start | bytes 122888 | tf_op jit(solution)/shard_map/ppermute | solution.py:616
  48.9 4.0 %collective-permute-start.9 = (f32[80,128]{1,0:T(8,128)S(1)}, f32[80,128]{1,0:T(8,128)S(1)}, u32[]{:S(2)}, u32[]{:S(2)}) collective-permute-start(f32[80,128]{1,0:T(8,128)S(1)} %add.12), channel_id=1, source_target_pairs={{0,16},{1,17},{2,18},{3,19},{4,20},{5,21},{6,22},{7,23},{8,24},{9,... | collective-permute-start | bytes 122888 | tf_op jit(solution)/shard_map/ppermute | solution.py:616
  53.0 5.9 %collective-permute-start.14 = (f32[80,128]{1,0:T(8,128)S(1)}, f32[80,128]{1,0:T(8,128)S(1)}, u32[]{:S(2)}, u32[]{:S(2)}) collective-permute-start(f32[80,128]{1,0:T(8,128)S(1)} %add_add_fusion.a_ref), channel_id=1, source_target_pairs={{0,6},{1,7},{2,4},{3,5},{4,2},{5,3},{6,0},{7,1},{8,14},{9,15},{10,... | collective-permute-start | bytes 122888 | tf_op jit(solution)/shard_map/ppermute | solution.py:616
  54.1 5.7 %collective-permute-start.13 = (f32[80,128]{1,0:T(8,128)S(1)}, f32[80,128]{1,0:T(8,128)S(1)}, u32[]{:S(2)}, u32[]{:S(2)}) collective-permute-start(f32[80,128]{1,0:T(8,128)S(1)} %add_add_fusion.a_ref), channel_id=1, source_target_pairs={{0,4},{1,5},{2,6},{3,7},{4,0},{5,1},{6,2},{7,3},{8,12},{9,13},{10,... | collective-permute-start | bytes 122888 | tf_op jit(solution)/shard_map/ppermute | solution.py:616
  54.7 5.1 %collective-permute-start.12 = (f32[80,128]{1,0:T(8,128)S(1)}, f32[80,128]{1,0:T(8,128)S(1)}, u32[]{:S(2)}, u32[]{:S(2)}) collective-permute-start(f32[80,128]{1,0:T(8,128)S(1)} %add_add_fusion.a_ref), channel_id=1, source_target_pairs={{0,2},{1,3},{2,0},{3,1},{4,6},{5,7},{6,4},{7,5},{8,10},{9,11},{10,... | collective-permute-start | bytes 122888 | tf_op jit(solution)/shard_map/ppermute | solution.py:616

commit v4 on v3

--- a/solution.py
+++ b/solution.py
@@ -125,18 +125,18 @@
         def value(i):
             return part[i * hi_count : (i + 1) * hi_count]
 
-        sent = [256.0 * value(2 * i) + value(2 * i + 1) - (STEPS + 1.0) for i in range(3)]
-        sent.append(value(6) * (STEPS / MASS_TOP))
+        sent = [value(6) * (STEPS / MASS_TOP)]
         for i in range(7, 10):
             root = jnp.sqrt(jnp.abs(value(i)) * (1.0 / (MASS_TOP * SPEED_TOP))) * STEPS
             sent.append(jnp.where(value(i) < 0.0, -root, root))
+        sent += [256.0 * value(2 * i) + value(2 * i + 1) - (STEPS + 1.0) for i in range(3)]
         sent = [jnp.floor(x + 0.5) for x in sent]
         sent.append(jnp.zeros_like(sent[0]))
-        part = jnp.concatenate(sent, axis=0)
         if pieces >= 2:
-            halves.append(part.reshape(VALUES * pieces // 2, devices, LANES))
+            steps = [x[h * devices : (h + 1) * devices] for h in range(pieces // 2) for x in sent]
+            halves.append(jnp.concatenate(steps, axis=0).reshape(-1, devices, LANES))
         else:
-            halves.append(part.reshape(VALUES, devices // 2, LANES))
+            halves.append(jnp.concatenate(sent, axis=0).reshape(VALUES, devices // 2, LANES))
     whole = jnp.concatenate(halves, axis=0 if pieces >= 2 else 1)
     out_ref[...] = jnp.transpose(whole, (1, 0, 2)).astype(I32).astype(I16)
 
@@ -172,32 +172,25 @@
     span_x = LANES
     acc_ref[...] = jnp.zeros_like(acc_ref)
 
-    def value_rows(blocks, value):
-        parts = []
-        for block in blocks:
-            for piece in range(pieces):
-                if pieces >= 2:
-                    half = pieces // 2
-                    at = (piece % 2) * VALUES * half + value * half + piece // 2
-                else:
-                    at = value
-                parts.append(block[at : at + 1, :])
-        return jnp.concatenate(parts, axis=1)
+    row = _iota((VALUES, width), 0)
+    span = jnp.where(row == 4, float(span_y), jnp.where(row == 5, float(span_z), float(span_x)))
+    factor = jnp.where(row == 0, MASS_TOP / STEPS, span / (2.0 * STEPS + 1.0))
+    offset = jnp.where(row == 0, 0.0, STEPS + 1.0)
+    momentum = (row >= 1) & (row <= 3)
 
     def step(i, carry):
         blocks = [arrived_ref[i * group + g].astype(I32).astype(F32) for g in range(group)]
-
-        def position(axis, span):
-            return (value_rows(blocks, axis) + (STEPS + 1.0)) * (span / (2.0 * STEPS + 1.0))
-
-        pos_y, pos_z, pos_x = position(0, span_y), position(1, span_z), position(2, span_x)
-        charges = [value_rows(blocks, 3) * (MASS_TOP / STEPS)]
-        for c in range(4, 7):
-            root = value_rows(blocks, c) * (1.0 / STEPS)
-            charges.append(root * jnp.abs(root) * (MASS_TOP * SPEED_TOP))
-        charges = jnp.concatenate(charges * 2, axis=0)
+        parts = [b[VALUES * k : VALUES * (k + 1)] for b in blocks for k in range(pieces)]
+        coded = jnp.concatenate(parts, axis=1)
+        values = jnp.where(
+            momentum,
+            coded * jnp.abs(coded) * (MASS_TOP * SPEED_TOP / (STEPS * STEPS)),
+            (coded + offset) * factor,
+        )
+        charges = jnp.where(row < 4, values, pltpu.roll(values, 4, 0))
+        pos_y, pos_z, pos_x = values[4:5], values[5:6], values[6:7]
         cell_x = _iota((span_x, width), 0).astype(F32)
-        hat_x = jnp.maximum(1.0 - jnp.abs(cell_x - pos_x), 0.0).astype(BF)
+        hat_x = jnp.maximum((1.0 - jnp.abs(cell_x - pos_x)).astype(BF), 0.0)
         cell_z = (_iota((40, width), 0) >> 2).astype(F32)
         hat_z = jnp.maximum(1.0 - jnp.abs(cell_z - pos_z), 0.0)
         planes = hat_z * jnp.concatenate([charges] * 5, axis=0)
@@ -429,8 +422,8 @@
                 refined_ref[o, 2 * n + y] = turned[o * 8 : (o + 1) * 8, y * LANES : (y + 1) * LANES]
 
     lane_z = _iota((1, LANES), 1) >> 4
-    own_two = del_ref[224:352, 256:1280]
-    own_one = one_ref[176:304, 128:1152]
+    own_two = jnp.swapaxes(del_ref[224:352, 256:1280].astype(F32), 0, 1).astype(BF)
+    own_one = jnp.swapaxes(one_ref[176:304, 128:1152].astype(F32), 0, 1).astype(BF)
 
     def folded(value):
         for step in (64, 32, 16):
@@ -450,24 +443,25 @@
     for ty in range(3):
         for tx in range(3):
             lanes = slice((2 + ty) * LANES, (2 + ty) * LANES + 1024)
-            pairs = _dot_lanes(act_ref[tx * 256 + 32 : tx * 256 + 192, lanes], own_two)
+            pairs = _dot(act_ref[tx * 256 + 32 : tx * 256 + 192, lanes], own_two)
             for tz in range(3):
                 total = jnp.zeros((16, LANES), F32)
                 for z in range(tz, tz + 8):
                     total = total + jnp.where(lane_z == z - tz, pairs[z * 16 : (z + 1) * 16], 0.0)
                 taps[(ty * 3 + tz) * 3 + tx] = folded(total)
     ones = jnp.ones((16, 1024), BF)
-    taps.append(folded(_dot_lanes(ones, own_two)))
-    taps.append(folded(_dot_lanes(ones, own_one)))
+    taps.append(folded(_dot(ones, own_two)))
+    taps.append(folded(_dot(ones, own_one)))
     for g, group in enumerate(packed(taps, 16)):
         sums_ref[g * 16 : (g + 1) * 16, :] = group
 
     taps = [None] * 27
     row_z = (_iota((64, LANES), 0) >> 2) - (_iota((64, LANES), 1) >> 4) - 3
     for ty in range(3):
+        lanes = slice((3 + ty) * LANES, (3 + ty) * LANES + 1024)
+        every = _dot(dens_ref[:, lanes], own_one)
         for tx in range(3):
-            lanes = slice((3 + ty) * LANES, (3 + ty) * LANES + 1024)
-            pairs = _dot_lanes(dens_ref[tx * 64 : (tx + 1) * 64, lanes], own_one)
+            pairs = every[tx * 64 : (tx + 1) * 64]
             for tz in range(3):
                 chosen = jnp.where(row_z == tz, pairs, 0.0)
                 total = chosen[0:8]
@@ -516,17 +510,28 @@
     lanes = span_y * span_x
     both = ("gy", "gz")
 
-    def along(axis, first, second, wrapped):
-        count = lax.axis_size(axis)
-        inner = [(i, i ^ 1) for i in range(count)]
-        outer = [(i, i + 1) for i in range(1, count - 1, 2)]
-        if wrapped == 1:
-            outer.append((count - 1, 0))
-        outer = outer + [(j, i) for i, j in outer]
-        if wrapped == 2:
-            outer = outer + [(0, 0), (count - 1, count - 1)]
-        far = lax.ppermute(second, axis, outer)
-        return far, lax.ppermute(first, axis, inner)
+    def swaps(axis, lower):
+        pairs = []
+        for y in range(count_y):
+            for z in range(count_z):
+                place, count = (y, count_y) if axis == "gy" else (z, count_z)
+                other = place ^ 1 if not lower else place + 1 if place % 2 else place - 1
+                if axis == "gy":
+                    partner = (other % count, z)
+                elif 0 <= other < count:
+                    partner = (y, other)
+                else:
+                    partner = (y ^ 1, z)
+                pairs.append((y * count_z + z, partner[0] * count_z + partner[1]))
+        return pairs
+
+    def partial_z(first, second):
+        pairs = [(i, j) for i, j in swaps("gz", True) if i // count_z == j // count_z]
+        return lax.ppermute(second, both, pairs), lax.ppermute(first, both, swaps("gz", False))
+
+    def along(axis, first, second):
+        far = lax.ppermute(second, both, swaps(axis, True))
+        return far, lax.ppermute(first, both, swaps(axis, False))
 
     outgoing = _route(offsets, masses, velocities, destination, devices)
     arrived = lax.all_to_all(outgoing, both, split_axis=0, concat_axis=0, tiled=True)
@@ -550,8 +555,8 @@
         ),
         flops=10**6,
         moved=10**6,
-    )(turned, *along("gz", first, second, 0))
-    rims = along("gy", first, second, 1)
+    )(turned, *partial_z(first, second))
+    rims = along("gy", first, second)
     k1 = first_weight.transpose(2, 3, 4, 1, 0).reshape(27, 4, 16)
     k2 = second_weight.transpose(2, 3, 4, 0, 1).reshape(27, 16, 16)
     banded = _call(
@@ -591,7 +596,7 @@
         ),
         flops=10**6,
         moved=10**6,
-    )(own, *along("gz", first, second, 1))
+    )(own, *along("gz", first, second))
     refined, grad_field, sums = _call(
         functools.partial(_net_kernel, count_y, count_z),
         (
@@ -610,7 +615,7 @@
         ],
         flops=6 * 10**9,
         moved=2 * 10**6,
-    )(wide, cot_wide, *along("gy", first, second, 1), *rims, *banded)
+    )(wide, cot_wide, *along("gy", first, second), *rims, *banded)
 
     def swapped(value, bit):
         return lax.ppermute(value, both, [(i, i ^ bit) for i in range(devices)])

time: 60.9 us -> 58.8 us (0.966)
  waiting for transfers between devices: 16.1 us -> 14.5 us
  Pallas kernels: 18.2 us -> 17.2 us
    ppermute x8, waiting for transfers between devices: 6.74 us -> 5.09 us  [the longest x3 3.66 us: along(): far = lax.ppermute(second, both, swaps(axis, True))]
    ppermute x7, starting transfers between devices: 8 us -> 8.73 us  [swapped(): return lax.ppermute(value, both, [(i, i ^ bit) for i in range(devices)])]
    pallas_call x1, Pallas kernels: 4.16 us -> 3.53 us  [_local(): pl.pallas_call(functools.partial(_deposit_kernel, span_y, span_z), out_sh...]
  transfers between devices with their start and end apart: 16 -> 16, of which waited for: 9 -> 10; matrix products, arithmetic and copies ran while one was open for 0% -> 0% of each run, Pallas kernels for 10% -> 10%
where the time goes in v4:
time: 58.8 us; the launch traced here: 58.6 us
  starting transfers between devices  25.4 us (43%)
  Pallas kernels  17.2 us (29%)
  waiting for transfers between devices  14.5 us (25%)
  between operations  0.77 us (1%)
  local copies, waits for them, and re-layouts  0.68 us (1%)
    ppermute x7, starting transfers between devices, swapped(): return lax.ppermute(value, both, [(i, i ^ bit) for i in range(devices)])  8.73 us
    all_to_all x1, starting transfers between devices, _local(): lax.all_to_all(outgoing, both, split_axis=0, concat_axis=0, tiled=True)  7.31 us
    ppermute x7, waiting for transfers between devices, swapped(): return lax.ppermute(value, both, [(i, i ^ bit) for i in range(devices)])  6.82 us
    pallas_call x1, Pallas kernels, _local(): _call(functools.partial(_net_kernel, count_y, count_z), (jax.ShapeDtypeSt...  5.6 us
    pallas_call x1, Pallas kernels, _route(): pl.pallas_call(functools.partial(_route_kernel, devices), out_shape=jax.S...  5.1 us
    ppermute x1, starting transfers between devices, partial_z(): lax.ppermute(first, both, swaps('gz', False))  4.54 us
    ppermute x3, starting transfers between devices, along(): return (far, lax.ppermute(first, both, swaps(axis, False)))  3.74 us
    ppermute x3, waiting for transfers between devices, along(): far = lax.ppermute(second, both, swaps(axis, True))  3.66 us
  transfers between devices with their start and end apart: 16, of which 10 were waited for; matrix products, arithmetic and copies ran while one was open for 0% of the time, Pallas kernels for 10%

profile of v4, /device:TPU:0, one launch (start us, length us, event | category | flops | bytes accessed | tf_op | source)
XLA Modules:
  0.0 58.6 jit_solution(3944767678327342053)
XLA Ops:
  0.6 5.1 %shard_map.136 = s16[32,32,128]{2,1,0:T(8,128)(2,1)} custom-call(f32[3,8192]{1,0:T(4,128)} %off_hbm.1, f32[1,8192]{1,0:T(1,128)} %bitcast.24, f32[3,8192]{1,0:T(4,128)} %vel_hbm.1, s32[1,8192]{1,0:T(1,128)} %bitcast.25), custom_call_target="tpu_custom_call" | custom-call | flops 4000000000 | bytes 1000000 | tf_op jit(solution)/shard_map/pallas_call | solution.py:148
  5.8 7.3 %all-to-all-start = ((s16[32,32,128]{2,1,0:T(8,128)(2,1)}), s16[32,32,128]{2,1,0:T(8,128)(2,1)S(1)}, u32[]{:S(2)}, u32[]{:S(2)}) async-start(s16[32,32,128]{2,1,0:T(8,128)(2,1)} %shard_map.136), calls=%async_computation | async-start | bytes 524288 | tf_op jit(solution)/shard_map/all_to_all | solution.py:537
  13.3 0.8 %collective-permute-start.2 = (bf16[32,1024]{1,0:T(8,128)(2,1)S(1)}, bf16[32,1024]{1,0:T(8,128)(2,1)S(1)}, u32[]{:S(2)}, u32[]{:S(2)}) collective-permute-start(bf16[32,1024]{1,0:T(8,128)(2,1)S(1)} %get-tuple-element.37), channel_id=1, source_target_pairs={{1,2},{2,1},{3,4},{4,3},{5,6},{6,5},{9,10},{10,9},{11,12},{12,11},... | collective-permute-start | bytes 196616 | tf_op jit(solution)/shard_map/ppermute | solution.py:530
  14.2 4.5 %collective-permute-start.3 = (bf16[32,1024]{1,0:T(8,128)(2,1)S(1)}, bf16[32,1024]{1,0:T(8,128)(2,1)S(1)}, u32[]{:S(2)}, u32[]{:S(2)}) collective-permute-start(bf16[32,1024]{1,0:T(8,128)(2,1)S(1)} %get-tuple-element.38), channel_id=1, source_target_pairs={{0,1},{1,0},{2,3},{3,2},{4,5},{5,4},{6,7},{7,6},{8,9},{9,8},{10,11... | collective-permute-start | bytes 196616 | tf_op jit(solution)/shard_map/ppermute | solution.py:530
  19.4 1.7 %shard_map.137 = (bf16[3,224,256]{2,1,0:T(8,128)(2,1)S(1)}, bf16[3,192,768]{2,1,0:T(8,128)(2,1)S(1)}, bf16[3,160,640]{2,1,0:T(8,128)(2,1)S(1)}, bf16[3,32,512]{2...) custom-call(bf16[27,4,16]{2,1,0:T(4,128)(2,1)S(1)} %bitcast.19, bf16[27,16,16]{2,1,0:T(8,128)(2,1)S(1)} %bitcast.18, ...), custom_call_target="tpu_custom_call" | custom-call | flops 2000000000 | bytes 2000000 | tf_op jit(solution)/shard_map/pallas_call | solution.py:562
  21.1 2.6 %all-to-all-done.arrived_ref = s16[32,32,128]{2,1,0:T(8,128)(2,1)S(1)} async-done(((s16[32,32,128]{2,1,0:T(8,128)(2,1)}), s16[32,32,128]{2,1,0:T(8,128)(2,1)S(1)}, u32[]{:S(2)}, u32[]{:S(2)}) %all-to-all-start) | async-done | bytes 262176 | tf_op jit(solution)/shard_map/all_to_all | solution.py:537
  23.7 3.5 %shard_map.138 = (f32[40,1152]{1,0:T(8,128)S(1)}, bf16[24,1152]{1,0:T(8,128)(2,1)S(1)}, bf16[24,1152]{1,0:T(8,128)(2,1)S(1)}) custom-call(s16[32,32,128]{2,1,0:T(8,128)(2,1)S(1)} %all-to-all-done.arrived_ref, bf16[3,224,256]{2,1,0:T(8,128)(2,1)S(1)} %get-tuple-element.31.refs_0_.w1_ref), custom_call_target="tpu_custom_call" | custom-call | flops 4000000000 | bytes 1000000 | tf_op jit(solution)/shard_map/pallas_call | solution.py:578
  27.3 2.4 %collective-permute-start.1 = (bf16[24,1152]{1,0:T(8,128)(2,1)S(1)}, bf16[24,1152]{1,0:T(8,128)(2,1)S(1)}, u32[]{:S(2)}, u32[]{:S(2)}) collective-permute-start(bf16[24,1152]{1,0:T(8,128)(2,1)S(1)} %get-tuple-element.34), channel_id=1, source_target_pairs={{0,1},{1,0},{2,3},{3,2},{4,5},{5,4},{6,7},{7,6},{8,9},{9,8},{10,11... | collective-permute-start | bytes 165896 | tf_op jit(solution)/shard_map/ppermute | solution.py:534
  30.0 0.7 %collective-permute-start.7 = (bf16[192,256]{1,0:T(8,128)(2,1)S(1)}, bf16[192,256]{1,0:T(8,128)(2,1)S(1)}, u32[]{:S(2)}, u32[]{:S(2)}) collective-permute-start(bf16[192,256]{1,0:T(8,128)(2,1)S(1)} %get-tuple-element.43), channel_id=1, source_target_pairs={{0,8},{1,9},{2,10},{3,11},{4,12},{5,13},{6,14},{7,15},{8,0},{9,1},... | collective-permute-start | bytes 294920 | tf_op jit(solution)/shard_map/ppermute | solution.py:534
  30.6 1.4 %collective-permute-done.1.fa_ref = bf16[24,1152]{1,0:T(8,128)(2,1)S(1)} collective-permute-done((bf16[24,1152]{1,0:T(8,128)(2,1)S(1)}, bf16[24,1152]{1,0:T(8,128)(2,1)S(1)}, u32[]{:S(2)}, u32[]{:S(2)}) %collective-permute-start.1) | collective-permute-done | bytes 55328 | tf_op jit(solution)/shard_map/ppermute | solution.py:534
  32.9 2.2 %collective-permute-done.6.cb_ref = bf16[192,256]{1,0:T(8,128)(2,1)S(1)} collective-permute-done((bf16[192,256]{1,0:T(8,128)(2,1)S(1)}, bf16[192,256]{1,0:T(8,128)(2,1)S(1)}, u32[]{:S(2)}, u32[]{:S(2)}) %collective-permute-start.6) | collective-permute-done | bytes 98336 | tf_op jit(solution)/shard_map/ppermute | solution.py:533
  35.0 1.5 %collective-permute-done.4.db_ref = bf16[64,640]{1,0:T(8,128)(2,1)S(1)} collective-permute-done((bf16[64,640]{1,0:T(8,128)(2,1)S(1)}, bf16[64,640]{1,0:T(8,128)(2,1)S(1)}, u32[]{:S(2)}, u32[]{:S(2)}) %collective-permute-start.4) | collective-permute-done | bytes 81952 | tf_op jit(solution)/shard_map/ppermute | solution.py:533
  36.5 5.6 %shard_map.142 = (bf16[16,8,8,128]{3,2,1,0:T(8,128)(2,1)}, f32[4,8,8,128]{3,2,1,0:T(8,128)}, f32[80,128]{1,0:T(8,128)S(1)}) custom-call(f32[64,1152]{1,0:T(8,128)S(1)} %get-tuple-element.35.wide_ref, bf16[192,1024]{1,0:T(8,128)(2,1)S(1)} %get-tuple-element.39.cotw_ref, bf16[64,640]{1,0:T(8,128)(2,1)S(1)} %collective-permute-done.4.db_ref, ...), custom_call_target="tpu_custom_call" | custom-call | flops 6000000000 | bytes 2000000 | tf_op jit(solution)/shard_map/pallas_call | solution.py:600
  42.2 1.2 %collective-permute-done.8 = f32[80,128]{1,0:T(8,128)S(1)} collective-permute-done((f32[80,128]{1,0:T(8,128)S(1)}, f32[80,128]{1,0:T(8,128)S(1)}, u32[]{:S(2)}, u32[]{:S(2)}) %collective-permute-start.8) | collective-permute-done | bytes 40992 | tf_op jit(solution)/shard_map/ppermute | solution.py:621
  43.4 2.8 %collective-permute-start.11 = (f32[80,128]{1,0:T(8,128)S(1)}, f32[80,128]{1,0:T(8,128)S(1)}, u32[]{:S(2)}, u32[]{:S(2)}) collective-permute-start(f32[80,128]{1,0:T(8,128)S(1)} %add.12), channel_id=1, source_target_pairs={{0,17},{1,16},{2,19},{3,18},{4,21},{5,20},{6,23},{7,22},{8,25},{9,... | collective-permute-start | bytes 122888 | tf_op jit(solution)/shard_map/ppermute | solution.py:621
  46.3 1.4 %collective-permute-start.9 = (f32[80,128]{1,0:T(8,128)S(1)}, f32[80,128]{1,0:T(8,128)S(1)}, u32[]{:S(2)}, u32[]{:S(2)}) collective-permute-start(f32[80,128]{1,0:T(8,128)S(1)} %add.12), channel_id=1, source_target_pairs={{0,16},{1,17},{2,18},{3,19},{4,20},{5,21},{6,22},{7,23},{8,24},{9,... | collective-permute-start | bytes 122888 | tf_op jit(solution)/shard_map/ppermute | solution.py:621
  47.6 0.7 %collective-permute-done.11 = f32[80,128]{1,0:T(8,128)S(1)} collective-permute-done((f32[80,128]{1,0:T(8,128)S(1)}, f32[80,128]{1,0:T(8,128)S(1)}, u32[]{:S(2)}, u32[]{:S(2)}) %collective-permute-start.11) | collective-permute-done | bytes 40992 | tf_op jit(solution)/shard_map/ppermute | solution.py:621
  48.3 1.9 %collective-permute-done.10 = f32[80,128]{1,0:T(8,128)S(1)} collective-permute-done((f32[80,128]{1,0:T(8,128)S(1)}, f32[80,128]{1,0:T(8,128)S(1)}, u32[]{:S(2)}, u32[]{:S(2)}) %collective-permute-start.10) | collective-permute-done | bytes 40992 | tf_op jit(solution)/shard_map/ppermute | solution.py:621
  50.3 1.9 %collective-permute-start.14 = (f32[80,128]{1,0:T(8,128)S(1)}, f32[80,128]{1,0:T(8,128)S(1)}, u32[]{:S(2)}, u32[]{:S(2)}) collective-permute-start(f32[80,128]{1,0:T(8,128)S(1)} %add_add_fusion.a_ref), channel_id=1, source_target_pairs={{0,6},{1,7},{2,4},{3,5},{4,2},{5,3},{6,0},{7,1},{8,14},{9,15},{10,... | collective-permute-start | bytes 122888 | tf_op jit(solution)/shard_map/ppermute | solution.py:621
  52.2 1.5 %collective-permute-start.13 = (f32[80,128]{1,0:T(8,128)S(1)}, f32[80,128]{1,0:T(8,128)S(1)}, u32[]{:S(2)}, u32[]{:S(2)}) collective-permute-start(f32[80,128]{1,0:T(8,128)S(1)} %add_add_fusion.a_ref), channel_id=1, source_target_pairs={{0,4},{1,5},{2,6},{3,7},{4,0},{5,1},{6,2},{7,3},{8,12},{9,13},{10,... | collective-permute-start | bytes 122888 | tf_op jit(solution)/shard_map/ppermute | solution.py:621
  53.7 1.0 %collective-permute-start.12 = (f32[80,128]{1,0:T(8,128)S(1)}, f32[80,128]{1,0:T(8,128)S(1)}, u32[]{:S(2)}, u32[]{:S(2)}) collective-permute-start(f32[80,128]{1,0:T(8,128)S(1)} %add_add_fusion.a_ref), channel_id=1, source_target_pairs={{0,2},{1,3},{2,0},{3,1},{4,6},{5,7},{6,4},{7,5},{8,10},{9,11},{10,... | collective-permute-start | bytes 122888 | tf_op jit(solution)/shard_map/ppermute | solution.py:621
  54.7 1.5 %collective-permute-done.14.d_ref = f32[80,128]{1,0:T(8,128)S(1)} collective-permute-done((f32[80,128]{1,0:T(8,128)S(1)}, f32[80,128]{1,0:T(8,128)S(1)}, u32[]{:S(2)}, u32[]{:S(2)}) %collective-permute-start.14) | collective-permute-done | bytes 40992 | tf_op jit(solution)/shard_map/ppermute | solution.py:621
  56.2 0.9 %collective-permute-done.13.c_ref = f32[80,128]{1,0:T(8,128)S(1)} collective-permute-done((f32[80,128]{1,0:T(8,128)S(1)}, f32[80,128]{1,0:T(8,128)S(1)}, u32[]{:S(2)}, u32[]{:S(2)}) %collective-permute-start.13) | collective-permute-done | bytes 40992 | tf_op jit(solution)/shard_map/ppermute | solution.py:621
  57.7 0.9 %shard_map.143 = (f32[27,4,16]{2,1,0:T(4,128)}, f32[1,16]{1,0:T(1,128)}, f32[27,16,16]{2,1,0:T(8,128)}, f32[1,16]{1,0:T(1,128)}) custom-call(f32[80,128]{1,0:T(8,128)S(1)} %add_add_fusion.a_ref, f32[80,128]{1,0:T(8,128)S(1)} %collective-permute-done.12.b_ref, f32[80,128]{1,0:T(8,128)S(1)} %collective-permute-done.13.c_ref, ...), custom_call_target="tpu_custom_call" | custom-call | flops 100000 | bytes 100000 | tf_op jit(solution)/shard_map/pallas_call | solution.py:637
  (28 shorter events, 2.7 us)
Async XLA Ops:
  5.7 7.3 %copy-start = (bf16[16,8,8,128]{3,2,1,0:T(8,128)(2,1)S(1)}, bf16[16,8,8,128]{3,2,1,0:T(8,128)(2,1)}, u32[]{:S(2)}) copy-start(bf16[16,8,8,128]{3,2,1,0:T(8,128)(2,1)} %cot_ref.1) | copy-start | bytes 786436
  5.8 18.0 %all-to-all-start = ((s16[32,32,128]{2,1,0:T(8,128)(2,1)}), s16[32,32,128]{2,1,0:T(8,128)(2,1)S(1)}, u32[]{:S(2)}, u32[]{:S(2)}) async-start(s16[32,32,128]{2,1,0:T(8,128)(2,1)} %shard_map.136), calls=%async_computation | async-start | bytes 524288 | tf_op jit(solution)/shard_map/all_to_all | solution.py:537
  13.1 5.7 %copy-start.1 = (bf16[16,16,3,3,3]{1,0,4,3,2:T(8,128)(2,1)S(1)}, bf16[16,16,3,3,3]{1,0,4,3,2:T(8,128)(2,1)}, u32[]{:S(2)}) copy-start(bf16[16,16,3,3,3]{1,0,4,3,2:T(8,128)(2,1)} %param.15) | copy-start | bytes 41476
  13.1 5.6 %copy-start.2 = (bf16[16,4,3,3,3]{0,1,4,3,2:T(4,128)(2,1)S(1)}, bf16[16,4,3,3,3]{0,1,4,3,2:T(4,128)(2,1)}, u32[]{:S(2)}) copy-start(bf16[16,4,3,3,3]{0,1,4,3,2:T(4,128)(2,1)} %param.13) | copy-start | bytes 10372
  13.3 16.4 %collective-permute-start.2 = (bf16[32,1024]{1,0:T(8,128)(2,1)S(1)}, bf16[32,1024]{1,0:T(8,128)(2,1)S(1)}, u32[]{:S(2)}, u32[]{:S(2)}) collective-permute-start(bf16[32,1024]{1,0:T(8,128)(2,1)S(1)} %get-tuple-element.37), channel_id=1, source_target_pairs={{1,2},{2,1},{3,4},{4,3},{5,6},{6,5},{9,10},{10,9},{11,12},{12,11},... | collective-permute-start | bytes 196616 | tf_op jit(solution)/shard_map/ppermute | solution.py:530
  14.2 15.6 %collective-permute-start.3 = (bf16[32,1024]{1,0:T(8,128)(2,1)S(1)}, bf16[32,1024]{1,0:T(8,128)(2,1)S(1)}, u32[]{:S(2)}, u32[]{:S(2)}) collective-permute-start(bf16[32,1024]{1,0:T(8,128)(2,1)S(1)} %get-tuple-element.38), channel_id=1, source_target_pairs={{0,1},{1,0},{2,3},{3,2},{4,5},{5,4},{6,7},{7,6},{8,9},{9,8},{10,11... | collective-permute-start | bytes 196616 | tf_op jit(solution)/shard_map/ppermute | solution.py:530
  18.7 0.7 %copy-start.3 = (f32[16]{0:T(128)S(1)}, f32[16]{0:T(128)}, u32[]{:S(2)}) copy-start(f32[16]{0:T(128)} %param.14) | copy-start | bytes 196
  18.7 0.7 %copy-start.4 = (f32[16]{0:T(128)S(1)}, f32[16]{0:T(128)}, u32[]{:S(2)}) copy-start(f32[16]{0:T(128)} %param.16) | copy-start | bytes 196
  27.3 3.4 %collective-permute-start = (bf16[24,1152]{1,0:T(8,128)(2,1)S(1)}, bf16[24,1152]{1,0:T(8,128)(2,1)S(1)}, u32[]{:S(2)}, u32[]{:S(2)}) collective-permute-start(bf16[24,1152]{1,0:T(8,128)(2,1)S(1)} %get-tuple-element.33), channel_id=1, source_target_pairs={{0,8},{1,2},{2,1},{3,4},{4,3},{5,6},{6,5},{7,15},{8,0},{9,10},{10,... | collective-permute-start | bytes 165896 | tf_op jit(solution)/shard_map/ppermute | solution.py:533
  27.3 4.7 %collective-permute-start.1 = (bf16[24,1152]{1,0:T(8,128)(2,1)S(1)}, bf16[24,1152]{1,0:T(8,128)(2,1)S(1)}, u32[]{:S(2)}, u32[]{:S(2)}) collective-permute-start(bf16[24,1152]{1,0:T(8,128)(2,1)S(1)} %get-tuple-element.34), channel_id=1, source_target_pairs={{0,1},{1,0},{2,3},{3,2},{4,5},{5,4},{6,7},{7,6},{8,9},{9,8},{10,11... | collective-permute-start | bytes 165896 | tf_op jit(solution)/shard_map/ppermute | solution.py:534
  29.9 5.2 %collective-permute-start.6 = (bf16[192,256]{1,0:T(8,128)(2,1)S(1)}, bf16[192,256]{1,0:T(8,128)(2,1)S(1)}, u32[]{:S(2)}, u32[]{:S(2)}) collective-permute-start(bf16[192,256]{1,0:T(8,128)(2,1)S(1)} %get-tuple-element.42), channel_id=1, source_target_pairs={{0,24},{1,25},{2,26},{3,27},{4,28},{5,29},{6,30},{7,31},{8,16},{9,... | collective-permute-start | bytes 294920 | tf_op jit(solution)/shard_map/ppermute | solution.py:533
  30.0 5.1 %collective-permute-start.7 = (bf16[192,256]{1,0:T(8,128)(2,1)S(1)}, bf16[192,256]{1,0:T(8,128)(2,1)S(1)}, u32[]{:S(2)}, u32[]{:S(2)}) collective-permute-start(bf16[192,256]{1,0:T(8,128)(2,1)S(1)} %get-tuple-element.43), channel_id=1, source_target_pairs={{0,8},{1,9},{2,10},{3,11},{4,12},{5,13},{6,14},{7,15},{8,0},{9,1},... | collective-permute-start | bytes 294920 | tf_op jit(solution)/shard_map/ppermute | solution.py:534
  32.1 4.4 %collective-permute-start.4 = (bf16[64,640]{1,0:T(8,128)(2,1)S(1)}, bf16[64,640]{1,0:T(8,128)(2,1)S(1)}, u32[]{:S(2)}, u32[]{:S(2)}) collective-permute-start(bf16[64,640]{1,0:T(8,128)(2,1)S(1)} %get-tuple-element.40), channel_id=1, source_target_pairs={{0,24},{1,25},{2,26},{3,27},{4,28},{5,29},{6,30},{7,31},{8,16},{9,... | collective-permute-start | bytes 245768 | tf_op jit(solution)/shard_map/ppermute | solution.py:533
  32.2 4.3 %collective-permute-start.5 = (bf16[64,640]{1,0:T(8,128)(2,1)S(1)}, bf16[64,640]{1,0:T(8,128)(2,1)S(1)}, u32[]{:S(2)}, u32[]{:S(2)}) collective-permute-start(bf16[64,640]{1,0:T(8,128)(2,1)S(1)} %get-tuple-element.41), channel_id=1, source_target_pairs={{0,8},{1,9},{2,10},{3,11},{4,12},{5,13},{6,14},{7,15},{8,0},{9,1},... | collective-permute-start | bytes 245768 | tf_op jit(solution)/shard_map/ppermute | solution.py:534
  42.1 1.3 %collective-permute-start.8 = (f32[80,128]{1,0:T(8,128)S(1)}, f32[80,128]{1,0:T(8,128)S(1)}, u32[]{:S(2)}, u32[]{:S(2)}) collective-permute-start(f32[80,128]{1,0:T(8,128)S(1)} %get-tuple-element.51), channel_id=1, source_target_pairs={{0,8},{1,9},{2,10},{3,11},{4,12},{5,13},{6,14},{7,15},{8,0},{9,1},... | collective-permute-start | bytes 122888 | tf_op jit(solution)/shard_map/ppermute | solution.py:621
  43.4 4.9 %collective-permute-start.11 = (f32[80,128]{1,0:T(8,128)S(1)}, f32[80,128]{1,0:T(8,128)S(1)}, u32[]{:S(2)}, u32[]{:S(2)}) collective-permute-start(f32[80,128]{1,0:T(8,128)S(1)} %add.12), channel_id=1, source_target_pairs={{0,17},{1,16},{2,19},{3,18},{4,21},{5,20},{6,23},{7,22},{8,25},{9,... | collective-permute-start | bytes 122888 | tf_op jit(solution)/shard_map/ppermute | solution.py:621
  46.3 4.0 %collective-permute-start.10 = (f32[80,128]{1,0:T(8,128)S(1)}, f32[80,128]{1,0:T(8,128)S(1)}, u32[]{:S(2)}, u32[]{:S(2)}) collective-permute-start(f32[80,128]{1,0:T(8,128)S(1)} %add.12), channel_id=1, source_target_pairs={{0,1},{1,0},{2,3},{3,2},{4,5},{5,4},{6,7},{7,6},{8,9},{9,8},{10,11... | collective-permute-start | bytes 122888 | tf_op jit(solution)/shard_map/ppermute | solution.py:621
  46.3 4.0 %collective-permute-start.9 = (f32[80,128]{1,0:T(8,128)S(1)}, f32[80,128]{1,0:T(8,128)S(1)}, u32[]{:S(2)}, u32[]{:S(2)}) collective-permute-start(f32[80,128]{1,0:T(8,128)S(1)} %add.12), channel_id=1, source_target_pairs={{0,16},{1,17},{2,18},{3,19},{4,20},{5,21},{6,22},{7,23},{8,24},{9,... | collective-permute-start | bytes 122888 | tf_op jit(solution)/shard_map/ppermute | solution.py:621
  50.3 5.9 %collective-permute-start.14 = (f32[80,128]{1,0:T(8,128)S(1)}, f32[80,128]{1,0:T(8,128)S(1)}, u32[]{:S(2)}, u32[]{:S(2)}) collective-permute-start(f32[80,128]{1,0:T(8,128)S(1)} %add_add_fusion.a_ref), channel_id=1, source_target_pairs={{0,6},{1,7},{2,4},{3,5},{4,2},{5,3},{6,0},{7,1},{8,14},{9,15},{10,... | collective-permute-start | bytes 122888 | tf_op jit(solution)/shard_map/ppermute | solution.py:621
  52.2 4.9 %collective-permute-start.13 = (f32[80,128]{1,0:T(8,128)S(1)}, f32[80,128]{1,0:T(8,128)S(1)}, u32[]{:S(2)}, u32[]{:S(2)}) collective-permute-start(f32[80,128]{1,0:T(8,128)S(1)} %add_add_fusion.a_ref), channel_id=1, source_target_pairs={{0,4},{1,5},{2,6},{3,7},{4,0},{5,1},{6,2},{7,3},{8,12},{9,13},{10,... | collective-permute-start | bytes 122888 | tf_op jit(solution)/shard_map/ppermute | solution.py:621
  53.7 4.0 %collective-permute-start.12 = (f32[80,128]{1,0:T(8,128)S(1)}, f32[80,128]{1,0:T(8,128)S(1)}, u32[]{:S(2)}, u32[]{:S(2)}) collective-permute-start(f32[80,128]{1,0:T(8,128)S(1)} %add_add_fusion.a_ref), channel_id=1, source_target_pairs={{0,2},{1,3},{2,0},{3,1},{4,6},{5,7},{6,4},{7,5},{8,10},{9,11},{10,... | collective-permute-start | bytes 122888 | tf_op jit(solution)/shard_map/ppermute | solution.py:621

commit v5 on v4

--- a/solution.py
+++ b/solution.py
@@ -317,26 +317,27 @@
 
 
 def _net_kernel(
-    count_y, count_z, wide_ref, cotw_ref, db_ref, da_ref, cb_ref, ca_ref, w1_ref, w2_ref, wb_ref, wf_ref,
-    b1_ref, b2_ref, refined_ref, field_ref, sums_ref,
-    side_ref, dens_ref, act_ref, del_ref, one_ref, ds_ref, ref_ref,
+    count_y, count_z, wide_ref, cotw_ref, db_ref, da_ref, cb_ref, ca_ref, w1_ref, w2_ref, wb_ref,
+    b1_ref, b2_ref, one_ref, ref_ref, sums_ref,
+    side_ref, dens_ref, act_ref, del_ref, ds_ref,
 ):
     me_y, me_z = lax.axis_index("gy"), lax.axis_index("gz")
     even = me_y % 2 == 0
 
-    edge = _iota((1, LANES), 1)
-    first_lane, last_lane = edge == 0, edge == LANES - 1
+    edge = _iota((16, LANES), 1)
+    not_first = jnp.where(edge == 0, 0.0, 1.0).astype(BF)
+    not_last = jnp.where(edge == LANES - 1, 0.0, 1.0).astype(BF)
 
     def shifted(value, dst, row0, stride, lane0):
         rows, lanes = value.shape
         for y in range(lanes // LANES):
-            block = value[:, y * LANES : (y + 1) * LANES]
+            block = value[:, y * LANES : (y + 1) * LANES].astype(BF)
             at = slice(lane0 + y * LANES, lane0 + (y + 1) * LANES)
-            left = jnp.where(first_lane, 0.0, pltpu.roll(block, 1, 1))
-            right = jnp.where(last_lane, 0.0, pltpu.roll(block, LANES - 1, 1))
-            dst[row0 : row0 + rows, at] = left.astype(BF)
-            dst[row0 + stride : row0 + stride + rows, at] = block.astype(BF)
-            dst[row0 + 2 * stride : row0 + 2 * stride + rows, at] = right.astype(BF)
+            left = pltpu.roll(block, 1, 1) * jnp.concatenate([not_first] * (rows // 16), axis=0)
+            right = pltpu.roll(block, LANES - 1, 1) * jnp.concatenate([not_last] * (rows // 16), axis=0)
+            dst[row0 : row0 + rows, at] = left
+            dst[row0 + stride : row0 + stride + rows, at] = block
+            dst[row0 + 2 * stride : row0 + 2 * stride + rows, at] = right
 
     keep_y = jnp.where(me_y < count_y - 1, 1.0, 0.0)
     has_up, has_down = me_y > 0, me_y < count_y - 1
@@ -402,24 +403,6 @@
             back = term if back is None else back + term
         back = back * ds_ref[:, n * 256 : (n + 1) * 256] * (mask_z * inside_y(2 * n, 1))
         shifted(back, one_ref, 0, 160, n * 256)
-
-    for n in range(4):
-        grad = None
-        for ty in range(3):
-            at = (2 * n + ty) * LANES
-            term = _dot(wf_ref[ty, :, 0:480], one_ref[:, at : at + 256])
-            grad = term if grad is None else grad + term
-        for y in range(2):
-            for c in range(4):
-                field_ref[c, 2 * n + y] = grad[c * 8 : (c + 1) * 8, y * LANES : (y + 1) * LANES]
-
-    row, col = _iota((128, 128), 0), _iota((128, 128), 1)
-    order = jnp.where(col == (row % 8) * 16 + row // 8, 1.0, 0.0).astype(BF)
-    for n in range(4):
-        turned = _dot(order, ref_ref[:, n * 256 : (n + 1) * 256]).astype(BF)
-        for y in range(2):
-            for o in range(16):
-                refined_ref[o, 2 * n + y] = turned[o * 8 : (o + 1) * 8, y * LANES : (y + 1) * LANES]
 
     lane_z = _iota((1, LANES), 1) >> 4
     own_two = jnp.swapaxes(del_ref[224:352, 256:1280].astype(F32), 0, 1).astype(BF)
@@ -475,6 +458,26 @@
     sums_ref[72:80, :] = jnp.where(upper, groups[2], groups[3])
 
 
+def _outputs_kernel(one_ref, rows_ref, wf_ref, refined_ref, field_ref):
+    for n in range(4):
+        grad = None
+        for ty in range(3):
+            at = (2 * n + ty) * LANES
+            term = _dot(wf_ref[ty, :, 0:480], one_ref[:, at : at + 256])
+            grad = term if grad is None else grad + term
+        for y in range(2):
+            for c in range(4):
+                field_ref[c, 2 * n + y] = grad[c * 8 : (c + 1) * 8, y * LANES : (y + 1) * LANES]
+
+    row, col = _iota((128, 128), 0), _iota((128, 128), 1)
+    order = jnp.where(col == (row % 8) * 16 + row // 8, 1.0, 0.0).astype(BF)
+    for n in range(4):
+        turned = _dot(order, rows_ref[:, n * 256 : (n + 1) * 256]).astype(BF)
+        for y in range(2):
+            for o in range(16):
+                refined_ref[o, 2 * n + y] = turned[o * 8 : (o + 1) * 8, y * LANES : (y + 1) * LANES]
+
+
 def _finish_kernel(scale, a_ref, b_ref, c_ref, d_ref, k1_ref, b1_ref, k2_ref, b2_ref):
     total = ((a_ref[...] + b_ref[...]) + (c_ref[...] + d_ref[...])) * scale
     for g in range(4):
@@ -516,12 +519,10 @@
             for z in range(count_z):
                 place, count = (y, count_y) if axis == "gy" else (z, count_z)
                 other = place ^ 1 if not lower else place + 1 if place % 2 else place - 1
-                if axis == "gy":
-                    partner = (other % count, z)
-                elif 0 <= other < count:
-                    partner = (y, other)
+                if 0 <= other < count:
+                    partner = (other, z) if axis == "gy" else (y, other)
                 else:
-                    partner = (y ^ 1, z)
+                    partner = (y, z ^ 1) if axis == "gy" else (y ^ 1, z)
                 pairs.append((y * count_z + z, partner[0] * count_z + partner[1]))
         return pairs
 
@@ -597,11 +598,12 @@
         flops=10**6,
         moved=10**6,
     )(own, *along("gz", first, second))
-    refined, grad_field, sums = _call(
+    w1, w2, wb, wf, b1, b2 = banded
+    delta_one, rows, sums = _call(
         functools.partial(_net_kernel, count_y, count_z),
         (
-            jax.ShapeDtypeStruct(cotangent.shape, BF),
-            jax.ShapeDtypeStruct((4,) + cotangent.shape[1:], F32),
+            jax.ShapeDtypeStruct((480, 1280), BF),
+            jax.ShapeDtypeStruct((128, 1024), BF),
             jax.ShapeDtypeStruct((80, LANES), F32),
         ),
         [
@@ -609,13 +611,20 @@
             pltpu.VMEM((192, 2048), BF),
             pltpu.VMEM((768, 1792), BF),
             pltpu.VMEM((576, 1536), BF),
-            pltpu.VMEM((480, 1280), BF),
             pltpu.VMEM((160, 1280), F32),
-            pltpu.VMEM((128, 1024), BF),
         ],
         flops=6 * 10**9,
         moved=2 * 10**6,
-    )(wide, cot_wide, *along("gy", first, second), *rims, *banded)
+    )(wide, cot_wide, *along("gy", first, second), *rims, w1, w2, wb, b1, b2)
+    refined, grad_field = _call(
+        _outputs_kernel,
+        (
+            jax.ShapeDtypeStruct(cotangent.shape, BF),
+            jax.ShapeDtypeStruct((4,) + cotangent.shape[1:], F32),
+        ),
+        flops=10**9,
+        moved=10**6,
+    )(delta_one, rows, wf)
 
     def swapped(value, bit):
         return lax.ppermute(value, both, [(i, i ^ bit) for i in range(devices)])

time: 58.8 us -> 58.4 us (level)
  waiting for transfers between devices: 14.5 us -> 12.6 us
  starting transfers between devices: 25.4 us -> 26.5 us
  Pallas kernels: 17.2 us -> 18.2 us
  local copies, waits for them, and re-layouts: 0.68 us -> 0.02 us
    ppermute x3, starting transfers between devices: 0.21 us -> 2.69 us  [along(): far = lax.ppermute(second, both, swaps(axis, True))]
    pallas_call x0 -> x1, Pallas kernels: none -> 1.43 us  [_local(): _call(_outputs_kernel, (jax.ShapeDtypeStruct(cotangent.shape, BF), jax.Sh...]
    ppermute x7, waiting for transfers between devices: 6.82 us -> 5.48 us  [swapped(): return lax.ppermute(value, both, [(i, i ^ bit) for i in range(devices)])]
    ppermute x3, waiting for transfers between devices: 3.66 us -> 2.41 us  [along(): far = lax.ppermute(second, both, swaps(axis, True))]
    ppermute x7, starting transfers between devices: 8.73 us -> 8.01 us  [swapped(): return lax.ppermute(value, both, [(i, i ^ bit) for i in range(devices)])]
    all_to_all x1, waiting for transfers between devices: 2.6 us -> 3.28 us  [_local(): lax.all_to_all(outgoing, both, split_axis=0, concat_axis=0, tiled=True)]
    unnamed x10, local copies, waits for them, and re-layouts: 0.68 us -> 0.02 us
    ppermute x3, starting transfers between devices: 3.74 us -> 3.09 us  [along(): return (far, lax.ppermute(first, both, swaps(axis, False)))]
  transfers between devices with their start and end apart: 16 -> 16, of which waited for: 10 -> 10; matrix products, arithmetic and copies ran while one was open for 0% -> 0% of each run, Pallas kernels for 10% -> 12%
where the time goes in v5:
time: 58.4 us; the launch traced here: 58.1 us
  starting transfers between devices  26.5 us (45%)
  Pallas kernels  18.2 us (31%)
  waiting for transfers between devices  12.6 us (22%)
  between operations  0.78 us (1%)
    ppermute x7, starting transfers between devices, swapped(): return lax.ppermute(value, both, [(i, i ^ bit) for i in range(devices)])  8.01 us
    all_to_all x1, starting transfers between devices, _local(): lax.all_to_all(outgoing, both, split_axis=0, concat_axis=0, tiled=True)  7.3 us
    ppermute x7, waiting for transfers between devices, swapped(): return lax.ppermute(value, both, [(i, i ^ bit) for i in range(devices)])  5.48 us
    pallas_call x1, Pallas kernels, _route(): pl.pallas_call(functools.partial(_route_kernel, devices), out_shape=jax.S...  5.14 us
    pallas_call x1, Pallas kernels, _local(): _call(functools.partial(_net_kernel, count_y, count_z), (jax.ShapeDtypeSt...  5.13 us
    ppermute x1, starting transfers between devices, partial_z(): lax.ppermute(first, both, swaps('gz', False))  4.54 us
    pallas_call x1, Pallas kernels, _local(): pl.pallas_call(functools.partial(_deposit_kernel, span_y, span_z), out_sh...  3.53 us
    all_to_all x1, waiting for transfers between devices, _local(): lax.all_to_all(outgoing, both, split_axis=0, concat_axis=0, tiled=True)  3.28 us
  transfers between devices with their start and end apart: 16, of which 10 were waited for; matrix products, arithmetic and copies ran while one was open for 0% of the time, Pallas kernels for 12%

profile of v5, /device:TPU:0, one launch (start us, length us, event | category | flops | bytes accessed | tf_op | source)
XLA Modules:
  0.0 58.1 jit_solution(6046489507775908683)
XLA Ops:
  0.7 5.1 %shard_map.136 = s16[32,32,128]{2,1,0:T(8,128)(2,1)} custom-call(f32[3,8192]{1,0:T(4,128)} %off_hbm.1, f32[1,8192]{1,0:T(1,128)} %bitcast.24, f32[3,8192]{1,0:T(4,128)} %vel_hbm.1, s32[1,8192]{1,0:T(1,128)} %bitcast.25), custom_call_target="tpu_custom_call" | custom-call | flops 4000000000 | bytes 1000000 | tf_op jit(solution)/shard_map/pallas_call | solution.py:148
  5.8 7.3 %all-to-all-start = ((s16[32,32,128]{2,1,0:T(8,128)(2,1)}), s16[32,32,128]{2,1,0:T(8,128)(2,1)S(1)}, u32[]{:S(2)}, u32[]{:S(2)}) async-start(s16[32,32,128]{2,1,0:T(8,128)(2,1)} %shard_map.136), calls=%async_computation | async-start | bytes 524288 | tf_op jit(solution)/shard_map/all_to_all | solution.py:538
  13.4 0.8 %collective-permute-start.2 = (bf16[32,1024]{1,0:T(8,128)(2,1)S(1)}, bf16[32,1024]{1,0:T(8,128)(2,1)S(1)}, u32[]{:S(2)}, u32[]{:S(2)}) collective-permute-start(bf16[32,1024]{1,0:T(8,128)(2,1)S(1)} %get-tuple-element.39), channel_id=1, source_target_pairs={{1,2},{2,1},{3,4},{4,3},{5,6},{6,5},{9,10},{10,9},{11,12},{12,11},... | collective-permute-start | bytes 196616 | tf_op jit(solution)/shard_map/ppermute | solution.py:531
  14.2 4.5 %collective-permute-start.3 = (bf16[32,1024]{1,0:T(8,128)(2,1)S(1)}, bf16[32,1024]{1,0:T(8,128)(2,1)S(1)}, u32[]{:S(2)}, u32[]{:S(2)}) collective-permute-start(bf16[32,1024]{1,0:T(8,128)(2,1)S(1)} %get-tuple-element.40), channel_id=1, source_target_pairs={{0,1},{1,0},{2,3},{3,2},{4,5},{5,4},{6,7},{7,6},{8,9},{9,8},{10,11... | collective-permute-start | bytes 196616 | tf_op jit(solution)/shard_map/ppermute | solution.py:531
  18.8 1.7 %shard_map.137 = (bf16[3,224,256]{2,1,0:T(8,128)(2,1)S(1)}, bf16[3,192,768]{2,1,0:T(8,128)(2,1)S(1)}, bf16[3,160,640]{2,1,0:T(8,128)(2,1)S(1)}, bf16[3,32,512]{2...) custom-call(bf16[27,4,16]{2,1,0:T(4,128)(2,1)S(1)} %bitcast.19, bf16[27,16,16]{2,1,0:T(8,128)(2,1)S(1)} %bitcast.18, ...), custom_call_target="tpu_custom_call" | custom-call | flops 2000000000 | bytes 2000000 | tf_op jit(solution)/shard_map/pallas_call | solution.py:563
  20.5 3.3 %all-to-all-done.arrived_ref = s16[32,32,128]{2,1,0:T(8,128)(2,1)S(1)} async-done(((s16[32,32,128]{2,1,0:T(8,128)(2,1)}), s16[32,32,128]{2,1,0:T(8,128)(2,1)S(1)}, u32[]{:S(2)}, u32[]{:S(2)}) %all-to-all-start) | async-done | bytes 262176 | tf_op jit(solution)/shard_map/all_to_all | solution.py:538
  23.8 3.5 %shard_map.138 = (f32[40,1152]{1,0:T(8,128)S(1)}, bf16[24,1152]{1,0:T(8,128)(2,1)S(1)}, bf16[24,1152]{1,0:T(8,128)(2,1)S(1)}) custom-call(s16[32,32,128]{2,1,0:T(8,128)(2,1)S(1)} %all-to-all-done.arrived_ref, bf16[3,224,256]{2,1,0:T(8,128)(2,1)S(1)} %get-tuple-element.33.refs_0_.w1_ref), custom_call_target="tpu_custom_call" | custom-call | flops 4000000000 | bytes 1000000 | tf_op jit(solution)/shard_map/pallas_call | solution.py:579
  27.4 2.4 %collective-permute-start.1 = (bf16[24,1152]{1,0:T(8,128)(2,1)S(1)}, bf16[24,1152]{1,0:T(8,128)(2,1)S(1)}, u32[]{:S(2)}, u32[]{:S(2)}) collective-permute-start(bf16[24,1152]{1,0:T(8,128)(2,1)S(1)} %get-tuple-element.36), channel_id=1, source_target_pairs={{0,1},{1,0},{2,3},{3,2},{4,5},{5,4},{6,7},{7,6},{8,9},{9,8},{10,11... | collective-permute-start | bytes 165896 | tf_op jit(solution)/shard_map/ppermute | solution.py:535
  30.0 0.7 %collective-permute-start.7 = (bf16[192,256]{1,0:T(8,128)(2,1)S(1)}, bf16[192,256]{1,0:T(8,128)(2,1)S(1)}, u32[]{:S(2)}, u32[]{:S(2)}) collective-permute-start(bf16[192,256]{1,0:T(8,128)(2,1)S(1)} %get-tuple-element.45), channel_id=1, source_target_pairs={{0,8},{1,9},{2,10},{3,11},{4,12},{5,13},{6,14},{7,15},{8,0},{9,1},... | collective-permute-start | bytes 294920 | tf_op jit(solution)/shard_map/ppermute | solution.py:535
  30.7 1.4 %collective-permute-done.1.fa_ref = bf16[24,1152]{1,0:T(8,128)(2,1)S(1)} collective-permute-done((bf16[24,1152]{1,0:T(8,128)(2,1)S(1)}, bf16[24,1152]{1,0:T(8,128)(2,1)S(1)}, u32[]{:S(2)}, u32[]{:S(2)}) %collective-permute-start.1) | collective-permute-done | bytes 55328 | tf_op jit(solution)/shard_map/ppermute | solution.py:535
  32.2 2.5 %collective-permute-start.4 = (bf16[64,640]{1,0:T(8,128)(2,1)S(1)}, bf16[64,640]{1,0:T(8,128)(2,1)S(1)}, u32[]{:S(2)}, u32[]{:S(2)}) collective-permute-start(bf16[64,640]{1,0:T(8,128)(2,1)S(1)} %get-tuple-element.42), channel_id=1, source_target_pairs={{0,1},{1,0},{2,3},{3,2},{4,5},{5,4},{6,7},{7,6},{8,16},{9,17},{10,... | collective-permute-start | bytes 245768 | tf_op jit(solution)/shard_map/ppermute | solution.py:534
  34.8 2.4 %collective-permute-done.4.db_ref = bf16[64,640]{1,0:T(8,128)(2,1)S(1)} collective-permute-done((bf16[64,640]{1,0:T(8,128)(2,1)S(1)}, bf16[64,640]{1,0:T(8,128)(2,1)S(1)}, u32[]{:S(2)}, u32[]{:S(2)}) %collective-permute-start.4) | collective-permute-done | bytes 81952 | tf_op jit(solution)/shard_map/ppermute | solution.py:534
  37.2 5.1 %shard_map.142 = (bf16[480,1280]{1,0:T(8,128)(2,1)S(1)}, bf16[128,1024]{1,0:T(8,128)(2,1)S(1)}, f32[80,128]{1,0:T(8,128)S(1)}) custom-call(f32[64,1152]{1,0:T(8,128)S(1)} %get-tuple-element.37.wide_ref, bf16[192,1024]{1,0:T(8,128)(2,1)S(1)} %get-tuple-element.41.cotw_ref, bf16[64,640]{1,0:T(8,128)(2,1)S(1)} %collective-permute-done.4.db_ref, ...), custom_call_target="tpu_custom_call" | custom-call | flops 6000000000 | bytes 2000000 | tf_op jit(solution)/shard_map/pallas_call | solution.py:602
  42.4 1.2 %collective-permute-done.8 = f32[80,128]{1,0:T(8,128)S(1)} collective-permute-done((f32[80,128]{1,0:T(8,128)S(1)}, f32[80,128]{1,0:T(8,128)S(1)}, u32[]{:S(2)}, u32[]{:S(2)}) %collective-permute-start.8) | collective-permute-done | bytes 40992 | tf_op jit(solution)/shard_map/ppermute | solution.py:630
  43.6 1.9 %collective-permute-start.11 = (f32[80,128]{1,0:T(8,128)S(1)}, f32[80,128]{1,0:T(8,128)S(1)}, u32[]{:S(2)}, u32[]{:S(2)}) collective-permute-start(f32[80,128]{1,0:T(8,128)S(1)} %add.12), channel_id=1, source_target_pairs={{0,17},{1,16},{2,19},{3,18},{4,21},{5,20},{6,23},{7,22},{8,25},{9,... | collective-permute-start | bytes 122888 | tf_op jit(solution)/shard_map/ppermute | solution.py:630
  45.7 1.4 %collective-permute-start.9 = (f32[80,128]{1,0:T(8,128)S(1)}, f32[80,128]{1,0:T(8,128)S(1)}, u32[]{:S(2)}, u32[]{:S(2)}) collective-permute-start(f32[80,128]{1,0:T(8,128)S(1)} %add.12), channel_id=1, source_target_pairs={{0,16},{1,17},{2,18},{3,19},{4,20},{5,21},{6,22},{7,23},{8,24},{9,... | collective-permute-start | bytes 122888 | tf_op jit(solution)/shard_map/ppermute | solution.py:630
  47.1 1.5 %collective-permute-done.11 = f32[80,128]{1,0:T(8,128)S(1)} collective-permute-done((f32[80,128]{1,0:T(8,128)S(1)}, f32[80,128]{1,0:T(8,128)S(1)}, u32[]{:S(2)}, u32[]{:S(2)}) %collective-permute-start.11) | collective-permute-done | bytes 40992 | tf_op jit(solution)/shard_map/ppermute | solution.py:630
  48.6 0.9 %collective-permute-done.10 = f32[80,128]{1,0:T(8,128)S(1)} collective-permute-done((f32[80,128]{1,0:T(8,128)S(1)}, f32[80,128]{1,0:T(8,128)S(1)}, u32[]{:S(2)}, u32[]{:S(2)}) %collective-permute-start.10) | collective-permute-done | bytes 40992 | tf_op jit(solution)/shard_map/ppermute | solution.py:630
  49.7 2.2 %collective-permute-start.14 = (f32[80,128]{1,0:T(8,128)S(1)}, f32[80,128]{1,0:T(8,128)S(1)}, u32[]{:S(2)}, u32[]{:S(2)}) collective-permute-start(f32[80,128]{1,0:T(8,128)S(1)} %add_add_fusion.a_ref), channel_id=1, source_target_pairs={{0,6},{1,7},{2,4},{3,5},{4,2},{5,3},{6,0},{7,1},{8,14},{9,15},{10,... | collective-permute-start | bytes 122888 | tf_op jit(solution)/shard_map/ppermute | solution.py:630
  51.9 1.1 %collective-permute-start.13 = (f32[80,128]{1,0:T(8,128)S(1)}, f32[80,128]{1,0:T(8,128)S(1)}, u32[]{:S(2)}, u32[]{:S(2)}) collective-permute-start(f32[80,128]{1,0:T(8,128)S(1)} %add_add_fusion.a_ref), channel_id=1, source_target_pairs={{0,4},{1,5},{2,6},{3,7},{4,0},{5,1},{6,2},{7,3},{8,12},{9,13},{10,... | collective-permute-start | bytes 122888 | tf_op jit(solution)/shard_map/ppermute | solution.py:630
  53.0 1.1 %collective-permute-start.12 = (f32[80,128]{1,0:T(8,128)S(1)}, f32[80,128]{1,0:T(8,128)S(1)}, u32[]{:S(2)}, u32[]{:S(2)}) collective-permute-start(f32[80,128]{1,0:T(8,128)S(1)} %add_add_fusion.a_ref), channel_id=1, source_target_pairs={{0,2},{1,3},{2,0},{3,1},{4,6},{5,7},{6,4},{7,5},{8,10},{9,11},{10,... | collective-permute-start | bytes 122888 | tf_op jit(solution)/shard_map/ppermute | solution.py:630
  54.2 1.4 %shard_map.143 = (bf16[16,8,8,128]{3,2,1,0:T(8,128)(2,1)}, f32[4,8,8,128]{3,2,1,0:T(8,128)}) custom-call(bf16[480,1280]{1,0:T(8,128)(2,1)S(1)} %get-tuple-element.50.one_ref, bf16[128,1024]{1,0:T(8,128)(2,1)S(1)} %get-tuple-element.51.rows_ref, bf16[3,32,512]{2,1,0:T(8,128)(2,1)S(1)} %get-tuple-element.52.wf_ref), custom_call_target="tpu_custom_call" | custom-call | flops 1000000000 | bytes 1000000 | tf_op jit(solution)/shard_map/pallas_call | solution.py:619
  55.9 0.9 %collective-permute-done.13.c_ref = f32[80,128]{1,0:T(8,128)S(1)} collective-permute-done((f32[80,128]{1,0:T(8,128)S(1)}, f32[80,128]{1,0:T(8,128)S(1)}, u32[]{:S(2)}, u32[]{:S(2)}) %collective-permute-start.13) | collective-permute-done | bytes 40992 | tf_op jit(solution)/shard_map/ppermute | solution.py:630
  57.3 0.9 %shard_map.144 = (f32[27,4,16]{2,1,0:T(4,128)}, f32[1,16]{1,0:T(1,128)}, f32[27,16,16]{2,1,0:T(8,128)}, f32[1,16]{1,0:T(1,128)}) custom-call(f32[80,128]{1,0:T(8,128)S(1)} %add_add_fusion.a_ref, f32[80,128]{1,0:T(8,128)S(1)} %collective-permute-done.12.b_ref, f32[80,128]{1,0:T(8,128)S(1)} %collective-permute-done.13.c_ref, ...), custom_call_target="tpu_custom_call" | custom-call | flops 100000 | bytes 100000 | tf_op jit(solution)/shard_map/pallas_call | solution.py:646
  (29 shorter events, 1.8 us)
Async XLA Ops:
  0.6 12.5 %copy-start = (bf16[16,8,8,128]{3,2,1,0:T(8,128)(2,1)S(1)}, bf16[16,8,8,128]{3,2,1,0:T(8,128)(2,1)}, u32[]{:S(2)}) copy-start(bf16[16,8,8,128]{3,2,1,0:T(8,128)(2,1)} %cot_ref.1) | copy-start | bytes 786436
  0.6 18.1 %copy-start.1 = (bf16[16,16,3,3,3]{1,0,4,3,2:T(8,128)(2,1)S(1)}, bf16[16,16,3,3,3]{1,0,4,3,2:T(8,128)(2,1)}, u32[]{:S(2)}) copy-start(bf16[16,16,3,3,3]{1,0,4,3,2:T(8,128)(2,1)} %param.15) | copy-start | bytes 41476
  0.7 18.1 %copy-start.2 = (bf16[16,4,3,3,3]{0,1,4,3,2:T(4,128)(2,1)S(1)}, bf16[16,4,3,3,3]{0,1,4,3,2:T(4,128)(2,1)}, u32[]{:S(2)}) copy-start(bf16[16,4,3,3,3]{0,1,4,3,2:T(4,128)(2,1)} %param.13) | copy-start | bytes 10372
  0.7 18.1 %copy-start.3 = (f32[16]{0:T(128)S(1)}, f32[16]{0:T(128)}, u32[]{:S(2)}) copy-start(f32[16]{0:T(128)} %param.14) | copy-start | bytes 196
  0.7 18.1 %copy-start.4 = (f32[16]{0:T(128)S(1)}, f32[16]{0:T(128)}, u32[]{:S(2)}) copy-start(f32[16]{0:T(128)} %param.16) | copy-start | bytes 196
  5.8 18.0 %all-to-all-start = ((s16[32,32,128]{2,1,0:T(8,128)(2,1)}), s16[32,32,128]{2,1,0:T(8,128)(2,1)S(1)}, u32[]{:S(2)}, u32[]{:S(2)}) async-start(s16[32,32,128]{2,1,0:T(8,128)(2,1)} %shard_map.136), calls=%async_computation | async-start | bytes 524288 | tf_op jit(solution)/shard_map/all_to_all | solution.py:538
  13.4 16.4 %collective-permute-start.2 = (bf16[32,1024]{1,0:T(8,128)(2,1)S(1)}, bf16[32,1024]{1,0:T(8,128)(2,1)S(1)}, u32[]{:S(2)}, u32[]{:S(2)}) collective-permute-start(bf16[32,1024]{1,0:T(8,128)(2,1)S(1)} %get-tuple-element.39), channel_id=1, source_target_pairs={{1,2},{2,1},{3,4},{4,3},{5,6},{6,5},{9,10},{10,9},{11,12},{12,11},... | collective-permute-start | bytes 196616 | tf_op jit(solution)/shard_map/ppermute | solution.py:531
  14.2 15.6 %collective-permute-start.3 = (bf16[32,1024]{1,0:T(8,128)(2,1)S(1)}, bf16[32,1024]{1,0:T(8,128)(2,1)S(1)}, u32[]{:S(2)}, u32[]{:S(2)}) collective-permute-start(bf16[32,1024]{1,0:T(8,128)(2,1)S(1)} %get-tuple-element.40), channel_id=1, source_target_pairs={{0,1},{1,0},{2,3},{3,2},{4,5},{5,4},{6,7},{7,6},{8,9},{9,8},{10,11... | collective-permute-start | bytes 196616 | tf_op jit(solution)/shard_map/ppermute | solution.py:531
  27.3 3.4 %collective-permute-start = (bf16[24,1152]{1,0:T(8,128)(2,1)S(1)}, bf16[24,1152]{1,0:T(8,128)(2,1)S(1)}, u32[]{:S(2)}, u32[]{:S(2)}) collective-permute-start(bf16[24,1152]{1,0:T(8,128)(2,1)S(1)} %get-tuple-element.35), channel_id=1, source_target_pairs={{0,8},{1,2},{2,1},{3,4},{4,3},{5,6},{6,5},{7,15},{8,0},{9,10},{10,... | collective-permute-start | bytes 165896 | tf_op jit(solution)/shard_map/ppermute | solution.py:534
  27.4 4.7 %collective-permute-start.1 = (bf16[24,1152]{1,0:T(8,128)(2,1)S(1)}, bf16[24,1152]{1,0:T(8,128)(2,1)S(1)}, u32[]{:S(2)}, u32[]{:S(2)}) collective-permute-start(bf16[24,1152]{1,0:T(8,128)(2,1)S(1)} %get-tuple-element.36), channel_id=1, source_target_pairs={{0,1},{1,0},{2,3},{3,2},{4,5},{5,4},{6,7},{7,6},{8,9},{9,8},{10,11... | collective-permute-start | bytes 165896 | tf_op jit(solution)/shard_map/ppermute | solution.py:535
  30.0 4.8 %collective-permute-start.6 = (bf16[192,256]{1,0:T(8,128)(2,1)S(1)}, bf16[192,256]{1,0:T(8,128)(2,1)S(1)}, u32[]{:S(2)}, u32[]{:S(2)}) collective-permute-start(bf16[192,256]{1,0:T(8,128)(2,1)S(1)} %get-tuple-element.44), channel_id=1, source_target_pairs={{0,1},{1,0},{2,3},{3,2},{4,5},{5,4},{6,7},{7,6},{8,16},{9,17},{10,... | collective-permute-start | bytes 294920 | tf_op jit(solution)/shard_map/ppermute | solution.py:534
  30.0 4.7 %collective-permute-start.7 = (bf16[192,256]{1,0:T(8,128)(2,1)S(1)}, bf16[192,256]{1,0:T(8,128)(2,1)S(1)}, u32[]{:S(2)}, u32[]{:S(2)}) collective-permute-start(bf16[192,256]{1,0:T(8,128)(2,1)S(1)} %get-tuple-element.45), channel_id=1, source_target_pairs={{0,8},{1,9},{2,10},{3,11},{4,12},{5,13},{6,14},{7,15},{8,0},{9,1},... | collective-permute-start | bytes 294920 | tf_op jit(solution)/shard_map/ppermute | solution.py:535
  32.2 5.0 %collective-permute-start.4 = (bf16[64,640]{1,0:T(8,128)(2,1)S(1)}, bf16[64,640]{1,0:T(8,128)(2,1)S(1)}, u32[]{:S(2)}, u32[]{:S(2)}) collective-permute-start(bf16[64,640]{1,0:T(8,128)(2,1)S(1)} %get-tuple-element.42), channel_id=1, source_target_pairs={{0,1},{1,0},{2,3},{3,2},{4,5},{5,4},{6,7},{7,6},{8,16},{9,17},{10,... | collective-permute-start | bytes 245768 | tf_op jit(solution)/shard_map/ppermute | solution.py:534
  34.7 2.4 %collective-permute-start.5 = (bf16[64,640]{1,0:T(8,128)(2,1)S(1)}, bf16[64,640]{1,0:T(8,128)(2,1)S(1)}, u32[]{:S(2)}, u32[]{:S(2)}) collective-permute-start(bf16[64,640]{1,0:T(8,128)(2,1)S(1)} %get-tuple-element.43), channel_id=1, source_target_pairs={{0,8},{1,9},{2,10},{3,11},{4,12},{5,13},{6,14},{7,15},{8,0},{9,1},... | collective-permute-start | bytes 245768 | tf_op jit(solution)/shard_map/ppermute | solution.py:535
  42.3 1.3 %collective-permute-start.8 = (f32[80,128]{1,0:T(8,128)S(1)}, f32[80,128]{1,0:T(8,128)S(1)}, u32[]{:S(2)}, u32[]{:S(2)}) collective-permute-start(f32[80,128]{1,0:T(8,128)S(1)} %get-tuple-element.55), channel_id=1, source_target_pairs={{0,8},{1,9},{2,10},{3,11},{4,12},{5,13},{6,14},{7,15},{8,0},{9,1},... | collective-permute-start | bytes 122888 | tf_op jit(solution)/shard_map/ppermute | solution.py:630
  43.6 5.0 %collective-permute-start.11 = (f32[80,128]{1,0:T(8,128)S(1)}, f32[80,128]{1,0:T(8,128)S(1)}, u32[]{:S(2)}, u32[]{:S(2)}) collective-permute-start(f32[80,128]{1,0:T(8,128)S(1)} %add.12), channel_id=1, source_target_pairs={{0,17},{1,16},{2,19},{3,18},{4,21},{5,20},{6,23},{7,22},{8,25},{9,... | collective-permute-start | bytes 122888 | tf_op jit(solution)/shard_map/ppermute | solution.py:630
  45.5 4.0 %collective-permute-start.10 = (f32[80,128]{1,0:T(8,128)S(1)}, f32[80,128]{1,0:T(8,128)S(1)}, u32[]{:S(2)}, u32[]{:S(2)}) collective-permute-start(f32[80,128]{1,0:T(8,128)S(1)} %add.12), channel_id=1, source_target_pairs={{0,1},{1,0},{2,3},{3,2},{4,5},{5,4},{6,7},{7,6},{8,9},{9,8},{10,11... | collective-permute-start | bytes 122888 | tf_op jit(solution)/shard_map/ppermute | solution.py:630
  45.7 4.0 %collective-permute-start.9 = (f32[80,128]{1,0:T(8,128)S(1)}, f32[80,128]{1,0:T(8,128)S(1)}, u32[]{:S(2)}, u32[]{:S(2)}) collective-permute-start(f32[80,128]{1,0:T(8,128)S(1)} %add.12), channel_id=1, source_target_pairs={{0,16},{1,17},{2,18},{3,19},{4,20},{5,21},{6,22},{7,23},{8,24},{9,... | collective-permute-start | bytes 122888 | tf_op jit(solution)/shard_map/ppermute | solution.py:630
  49.7 6.2 %collective-permute-start.14 = (f32[80,128]{1,0:T(8,128)S(1)}, f32[80,128]{1,0:T(8,128)S(1)}, u32[]{:S(2)}, u32[]{:S(2)}) collective-permute-start(f32[80,128]{1,0:T(8,128)S(1)} %add_add_fusion.a_ref), channel_id=1, source_target_pairs={{0,6},{1,7},{2,4},{3,5},{4,2},{5,3},{6,0},{7,1},{8,14},{9,15},{10,... | collective-permute-start | bytes 122888 | tf_op jit(solution)/shard_map/ppermute | solution.py:630
  51.9 4.9 %collective-permute-start.13 = (f32[80,128]{1,0:T(8,128)S(1)}, f32[80,128]{1,0:T(8,128)S(1)}, u32[]{:S(2)}, u32[]{:S(2)}) collective-permute-start(f32[80,128]{1,0:T(8,128)S(1)} %add_add_fusion.a_ref), channel_id=1, source_target_pairs={{0,4},{1,5},{2,6},{3,7},{4,0},{5,1},{6,2},{7,3},{8,12},{9,13},{10,... | collective-permute-start | bytes 122888 | tf_op jit(solution)/shard_map/ppermute | solution.py:630
  53.0 4.2 %collective-permute-start.12 = (f32[80,128]{1,0:T(8,128)S(1)}, f32[80,128]{1,0:T(8,128)S(1)}, u32[]{:S(2)}, u32[]{:S(2)}) collective-permute-start(f32[80,128]{1,0:T(8,128)S(1)} %add_add_fusion.a_ref), channel_id=1, source_target_pairs={{0,2},{1,3},{2,0},{3,1},{4,6},{5,7},{6,4},{7,5},{8,10},{9,11},{10,... | collective-permute-start | bytes 122888 | tf_op jit(solution)/shard_map/ppermute | solution.py:630

commit v6 on v5

--- a/solution.py
+++ b/solution.py
@@ -458,7 +458,8 @@
     sums_ref[72:80, :] = jnp.where(upper, groups[2], groups[3])
 
 
-def _outputs_kernel(one_ref, rows_ref, wf_ref, refined_ref, field_ref):
+def _outputs_kernel(one_ref, rows_ref, wf_ref, refined_ref, field_ref, done_ref):
+    done_ref[...] = jnp.zeros_like(done_ref)
     for n in range(4):
         grad = None
         for ty in range(3):
@@ -478,8 +479,8 @@
                 refined_ref[o, 2 * n + y] = turned[o * 8 : (o + 1) * 8, y * LANES : (y + 1) * LANES]
 
 
-def _finish_kernel(scale, a_ref, b_ref, c_ref, d_ref, k1_ref, b1_ref, k2_ref, b2_ref):
-    total = ((a_ref[...] + b_ref[...]) + (c_ref[...] + d_ref[...])) * scale
+def _finish_kernel(scale, a_ref, b_ref, k1_ref, b1_ref, k2_ref, b2_ref):
+    total = (a_ref[...] + b_ref[...]) * scale
     for g in range(4):
         block = jnp.swapaxes(total[g * 16 : (g + 1) * 16, :], 0, 1)
         for j in range(8):
@@ -616,11 +617,12 @@
         flops=6 * 10**9,
         moved=2 * 10**6,
     )(wide, cot_wide, *along("gy", first, second), *rims, w1, w2, wb, b1, b2)
-    refined, grad_field = _call(
+    refined, grad_field, done = _call(
         _outputs_kernel,
         (
             jax.ShapeDtypeStruct(cotangent.shape, BF),
             jax.ShapeDtypeStruct((4,) + cotangent.shape[1:], F32),
+            jax.ShapeDtypeStruct((80, LANES), F32),
         ),
         flops=10**9,
         moved=10**6,
@@ -629,19 +631,24 @@
     def swapped(value, bit):
         return lax.ppermute(value, both, [(i, i ^ bit) for i in range(devices)])
 
+    def by_core(value, even_bit, odd_bit):
+        pairs = [(i, i ^ (odd_bit if i & inner_bit else even_bit)) for i in range(devices)]
+        return lax.ppermute(value, both, pairs)
+
+    inner_bit = count_z
     bits = [1 << i for i in range((devices - 1).bit_length())]
-    inner_bit = count_z
     rest = [b for b in bits if b != inner_bit]
     total = sums + swapped(sums, inner_bit)
     while len(rest) > 2:
-        a = rest.pop()
-        if len(rest) > 2:
-            b = rest.pop(0)
-            total = (total + swapped(total, a)) + (swapped(total, b) + swapped(total, a ^ b))
-        else:
-            total = total + swapped(total, a)
-    a, b = rest
-    parts = (total, swapped(total, a), swapped(total, b), swapped(total, a ^ b))
+        a, b = rest.pop(), rest.pop(0)
+        total = (total + swapped(total, a)) + (swapped(total, b) + swapped(total, a ^ b))
+    low, high = rest
+    total = total + done
+    even = lax.axis_index("gy") % 2 == 0
+    one = by_core(total, high, low)
+    two = by_core(total, bits[0], low ^ high)
+    part = one + jnp.where(even, total, two)
+    parts = (part, swapped(part, inner_bit))
     scale = 1.0 / math.sqrt(span_y * span_z * span_x * devices)
     g1, gb1, g2, gb2 = _call(
         functools.partial(_finish_kernel, scale),

time: 58.4 us -> 57.9 us (level)
  starting transfers between devices: 26.5 us -> 24.5 us
  waiting for transfers between devices: 12.6 us -> 14.1 us
    ppermute x7 -> x5, starting transfers between devices: 8.01 us -> 3.7 us  [swapped(): return lax.ppermute(value, both, [(i, i ^ bit) for i in range(devices)])]
    ppermute x0 -> x2, waiting for transfers between devices: none -> 2.64 us  [by_core(): return lax.ppermute(value, both, pairs)]
    ppermute x0 -> x2, starting transfers between devices: none -> 2.34 us  [by_core(): return lax.ppermute(value, both, pairs)]
    ppermute x7 -> x5, waiting for transfers between devices: 5.48 us -> 4.35 us  [swapped(): return lax.ppermute(value, both, [(i, i ^ bit) for i in range(devices)])]
  transfers between devices with their start and end apart: 16 -> 16, of which waited for: 10 -> 7; matrix products, arithmetic and copies ran while one was open for 0% -> 0% of each run, Pallas kernels for 12% -> 12%
where the time goes in v6:
time: 57.9 us; the launch traced here: 57.7 us
  starting transfers between devices  24.5 us (42%)
  Pallas kernels  18.2 us (31%)
  waiting for transfers between devices  14.1 us (24%)
  between operations  0.79 us (1%)
    all_to_all x1, starting transfers between devices, _local(): lax.all_to_all(outgoing, both, split_axis=0, concat_axis=0, tiled=True)  7.3 us
    pallas_call x1, Pallas kernels, _route(): pl.pallas_call(functools.partial(_route_kernel, devices), out_shape=jax.S...  5.14 us
    pallas_call x1, Pallas kernels, _local(): _call(functools.partial(_net_kernel, count_y, count_z), (jax.ShapeDtypeSt...  5.1 us
    ppermute x1, starting transfers between devices, partial_z(): lax.ppermute(first, both, swaps('gz', False))  4.54 us
    ppermute x5, waiting for transfers between devices, swapped(): return lax.ppermute(value, both, [(i, i ^ bit) for i in range(devices)])  4.35 us
    ppermute x5, starting transfers between devices, swapped(): return lax.ppermute(value, both, [(i, i ^ bit) for i in range(devices)])  3.7 us
    pallas_call x1, Pallas kernels, _local(): pl.pallas_call(functools.partial(_deposit_kernel, span_y, span_z), out_sh...  3.53 us
    all_to_all x1, waiting for transfers between devices, _local(): lax.all_to_all(outgoing, both, split_axis=0, concat_axis=0, tiled=True)  3.28 us
  transfers between devices with their start and end apart: 16, of which 7 were waited for; matrix products, arithmetic and copies ran while one was open for 0% of the time, Pallas kernels for 12%

profile of v6, /device:TPU:0, one launch (start us, length us, event | category | flops | bytes accessed | tf_op | source)
XLA Modules:
  0.0 57.7 jit_solution(14959253878474327872)
XLA Ops:
  0.7 5.1 %shard_map.136 = s16[32,32,128]{2,1,0:T(8,128)(2,1)} custom-call(f32[3,8192]{1,0:T(4,128)} %off_hbm.1, f32[1,8192]{1,0:T(1,128)} %bitcast.24, f32[3,8192]{1,0:T(4,128)} %vel_hbm.1, s32[1,8192]{1,0:T(1,128)} %bitcast.25), custom_call_target="tpu_custom_call" | custom-call | flops 4000000000 | bytes 1000000 | tf_op jit(solution)/shard_map/pallas_call | solution.py:148
  5.8 7.3 %all-to-all-start = ((s16[32,32,128]{2,1,0:T(8,128)(2,1)}), s16[32,32,128]{2,1,0:T(8,128)(2,1)S(1)}, u32[]{:S(2)}, u32[]{:S(2)}) async-start(s16[32,32,128]{2,1,0:T(8,128)(2,1)} %shard_map.136), calls=%async_computation | async-start | bytes 524288 | tf_op jit(solution)/shard_map/all_to_all | solution.py:539
  13.2 0.2 shard_map.140
  13.4 0.8 %collective-permute-start.2 = (bf16[32,1024]{1,0:T(8,128)(2,1)S(1)}, bf16[32,1024]{1,0:T(8,128)(2,1)S(1)}, u32[]{:S(2)}, u32[]{:S(2)}) collective-permute-start(bf16[32,1024]{1,0:T(8,128)(2,1)S(1)} %get-tuple-element.40), channel_id=1, source_target_pairs={{1,2},{2,1},{3,4},{4,3},{5,6},{6,5},{9,10},{10,9},{11,12},{12,11},... | collective-permute-start | bytes 196616 | tf_op jit(solution)/shard_map/ppermute | solution.py:532
  14.2 4.5 %collective-permute-start.3 = (bf16[32,1024]{1,0:T(8,128)(2,1)S(1)}, bf16[32,1024]{1,0:T(8,128)(2,1)S(1)}, u32[]{:S(2)}, u32[]{:S(2)}) collective-permute-start(bf16[32,1024]{1,0:T(8,128)(2,1)S(1)} %get-tuple-element.41), channel_id=1, source_target_pairs={{0,1},{1,0},{2,3},{3,2},{4,5},{5,4},{6,7},{7,6},{8,9},{9,8},{10,11... | collective-permute-start | bytes 196616 | tf_op jit(solution)/shard_map/ppermute | solution.py:532
  18.8 1.7 %shard_map.137 = (bf16[3,224,256]{2,1,0:T(8,128)(2,1)S(1)}, bf16[3,192,768]{2,1,0:T(8,128)(2,1)S(1)}, bf16[3,160,640]{2,1,0:T(8,128)(2,1)S(1)}, bf16[3,32,512]{2...) custom-call(bf16[27,4,16]{2,1,0:T(4,128)(2,1)S(1)} %bitcast.19, bf16[27,16,16]{2,1,0:T(8,128)(2,1)S(1)} %bitcast.18, ...), custom_call_target="tpu_custom_call" | custom-call | flops 2000000000 | bytes 2000000 | tf_op jit(solution)/shard_map/pallas_call | solution.py:564
  20.5 3.3 %all-to-all-done.arrived_ref = s16[32,32,128]{2,1,0:T(8,128)(2,1)S(1)} async-done(((s16[32,32,128]{2,1,0:T(8,128)(2,1)}), s16[32,32,128]{2,1,0:T(8,128)(2,1)S(1)}, u32[]{:S(2)}, u32[]{:S(2)}) %all-to-all-start) | async-done | bytes 262176 | tf_op jit(solution)/shard_map/all_to_all | solution.py:539
  23.8 3.5 %shard_map.138 = (f32[40,1152]{1,0:T(8,128)S(1)}, bf16[24,1152]{1,0:T(8,128)(2,1)S(1)}, bf16[24,1152]{1,0:T(8,128)(2,1)S(1)}) custom-call(s16[32,32,128]{2,1,0:T(8,128)(2,1)S(1)} %all-to-all-done.arrived_ref, bf16[3,224,256]{2,1,0:T(8,128)(2,1)S(1)} %get-tuple-element.34.refs_0_.w1_ref), custom_call_target="tpu_custom_call" | custom-call | flops 4000000000 | bytes 1000000 | tf_op jit(solution)/shard_map/pallas_call | solution.py:580
  27.4 2.4 %collective-permute-start.1 = (bf16[24,1152]{1,0:T(8,128)(2,1)S(1)}, bf16[24,1152]{1,0:T(8,128)(2,1)S(1)}, u32[]{:S(2)}, u32[]{:S(2)}) collective-permute-start(bf16[24,1152]{1,0:T(8,128)(2,1)S(1)} %get-tuple-element.37), channel_id=1, source_target_pairs={{0,1},{1,0},{2,3},{3,2},{4,5},{5,4},{6,7},{7,6},{8,9},{9,8},{10,11... | collective-permute-start | bytes 165896 | tf_op jit(solution)/shard_map/ppermute | solution.py:536
  30.0 0.7 %collective-permute-start.7 = (bf16[192,256]{1,0:T(8,128)(2,1)S(1)}, bf16[192,256]{1,0:T(8,128)(2,1)S(1)}, u32[]{:S(2)}, u32[]{:S(2)}) collective-permute-start(bf16[192,256]{1,0:T(8,128)(2,1)S(1)} %get-tuple-element.46), channel_id=1, source_target_pairs={{0,8},{1,9},{2,10},{3,11},{4,12},{5,13},{6,14},{7,15},{8,0},{9,1},... | collective-permute-start | bytes 294920 | tf_op jit(solution)/shard_map/ppermute | solution.py:536
  30.7 1.4 %collective-permute-done.1.fa_ref = bf16[24,1152]{1,0:T(8,128)(2,1)S(1)} collective-permute-done((bf16[24,1152]{1,0:T(8,128)(2,1)S(1)}, bf16[24,1152]{1,0:T(8,128)(2,1)S(1)}, u32[]{:S(2)}, u32[]{:S(2)}) %collective-permute-start.1) | collective-permute-done | bytes 55328 | tf_op jit(solution)/shard_map/ppermute | solution.py:536
  32.2 2.5 %collective-permute-start.4 = (bf16[64,640]{1,0:T(8,128)(2,1)S(1)}, bf16[64,640]{1,0:T(8,128)(2,1)S(1)}, u32[]{:S(2)}, u32[]{:S(2)}) collective-permute-start(bf16[64,640]{1,0:T(8,128)(2,1)S(1)} %get-tuple-element.43), channel_id=1, source_target_pairs={{0,1},{1,0},{2,3},{3,2},{4,5},{5,4},{6,7},{7,6},{8,16},{9,17},{10,... | collective-permute-start | bytes 245768 | tf_op jit(solution)/shard_map/ppermute | solution.py:535
  34.8 2.4 %collective-permute-done.4.db_ref = bf16[64,640]{1,0:T(8,128)(2,1)S(1)} collective-permute-done((bf16[64,640]{1,0:T(8,128)(2,1)S(1)}, bf16[64,640]{1,0:T(8,128)(2,1)S(1)}, u32[]{:S(2)}, u32[]{:S(2)}) %collective-permute-start.4) | collective-permute-done | bytes 81952 | tf_op jit(solution)/shard_map/ppermute | solution.py:535
  37.2 5.1 %shard_map.142 = (bf16[480,1280]{1,0:T(8,128)(2,1)S(1)}, bf16[128,1024]{1,0:T(8,128)(2,1)S(1)}, f32[80,128]{1,0:T(8,128)S(1)}) custom-call(f32[64,1152]{1,0:T(8,128)S(1)} %get-tuple-element.38.wide_ref, bf16[192,1024]{1,0:T(8,128)(2,1)S(1)} %get-tuple-element.42.cotw_ref, bf16[64,640]{1,0:T(8,128)(2,1)S(1)} %collective-permute-done.4.db_ref, ...), custom_call_target="tpu_custom_call" | custom-call | flops 6000000000 | bytes 2000000 | tf_op jit(solution)/shard_map/pallas_call | solution.py:603
  42.4 1.2 %collective-permute-done.8 = f32[80,128]{1,0:T(8,128)S(1)} collective-permute-done((f32[80,128]{1,0:T(8,128)S(1)}, f32[80,128]{1,0:T(8,128)S(1)}, u32[]{:S(2)}, u32[]{:S(2)}) %collective-permute-start.8) | collective-permute-done | bytes 40992 | tf_op jit(solution)/shard_map/ppermute | solution.py:632
  43.6 2.0 %collective-permute-start.10 = (f32[80,128]{1,0:T(8,128)S(1)}, f32[80,128]{1,0:T(8,128)S(1)}, u32[]{:S(2)}, u32[]{:S(2)}) collective-permute-start(f32[80,128]{1,0:T(8,128)S(1)} %add.22), channel_id=1, source_target_pairs={{0,1},{1,0},{2,3},{3,2},{4,5},{5,4},{6,7},{7,6},{8,9},{9,8},{10,11... | collective-permute-start | bytes 122888 | tf_op jit(solution)/shard_map/ppermute | solution.py:632
  45.6 1.5 %collective-permute-start.9 = (f32[80,128]{1,0:T(8,128)S(1)}, f32[80,128]{1,0:T(8,128)S(1)}, u32[]{:S(2)}, u32[]{:S(2)}) collective-permute-start(f32[80,128]{1,0:T(8,128)S(1)} %add.22), channel_id=1, source_target_pairs={{0,16},{1,17},{2,18},{3,19},{4,20},{5,21},{6,22},{7,23},{8,24},{9,... | collective-permute-start | bytes 122888 | tf_op jit(solution)/shard_map/ppermute | solution.py:632
  47.1 1.4 %shard_map.143 = (bf16[16,8,8,128]{3,2,1,0:T(8,128)(2,1)}, f32[4,8,8,128]{3,2,1,0:T(8,128)}, f32[80,128]{1,0:T(8,128)S(1)}) custom-call(bf16[480,1280]{1,0:T(8,128)(2,1)S(1)} %get-tuple-element.51.one_ref, bf16[128,1024]{1,0:T(8,128)(2,1)S(1)} %get-tuple-element.52.rows_ref, bf16[3,32,512]{2,1,0:T(8,128)(2,1)S(1)} %get-tuple-element.53.wf_ref), custom_call_target="tpu_custom_call" | custom-call | flops 1000000000 | bytes 1000000 | tf_op jit(solution)/shard_map/pallas_call | solution.py:620
  48.6 1.9 %collective-permute-done.11 = f32[80,128]{1,0:T(8,128)S(1)} collective-permute-done((f32[80,128]{1,0:T(8,128)S(1)}, f32[80,128]{1,0:T(8,128)S(1)}, u32[]{:S(2)}, u32[]{:S(2)}) %collective-permute-start.11) | collective-permute-done | bytes 40992 | tf_op jit(solution)/shard_map/ppermute | solution.py:632
  50.5 0.8 %collective-permute-start.12 = (f32[80,128]{1,0:T(8,128)S(1)}, f32[80,128]{1,0:T(8,128)S(1)}, u32[]{:S(2)}, u32[]{:S(2)}) collective-permute-start(f32[80,128]{1,0:T(8,128)S(1)} %add_add_fusion), channel_id=1, source_target_pairs={{0,4},{1,5},{2,6},{3,7},{4,0},{5,1},{6,2},{7,3},{8,10},{9,11},{10,... | collective-permute-start | bytes 122888 | tf_op jit(solution)/shard_map/ppermute | solution.py:636
  51.4 1.5 %collective-permute-start.13 = (f32[80,128]{1,0:T(8,128)S(1)}, f32[80,128]{1,0:T(8,128)S(1)}, u32[]{:S(2)}, u32[]{:S(2)}) collective-permute-start(f32[80,128]{1,0:T(8,128)S(1)} %add_add_fusion), channel_id=1, source_target_pairs={{0,1},{1,0},{2,3},{3,2},{4,5},{5,4},{6,7},{7,6},{8,14},{9,15},{10,... | collective-permute-start | bytes 122888 | tf_op jit(solution)/shard_map/ppermute | solution.py:636
  52.9 2.6 %collective-permute-done.12 = f32[80,128]{1,0:T(8,128)S(1)} collective-permute-done((f32[80,128]{1,0:T(8,128)S(1)}, f32[80,128]{1,0:T(8,128)S(1)}, u32[]{:S(2)}, u32[]{:S(2)}) %collective-permute-start.12) | collective-permute-done | bytes 40992 | tf_op jit(solution)/shard_map/ppermute | solution.py:636
  55.6 1.2 %collective-permute-done.14.b_ref = f32[80,128]{1,0:T(8,128)S(1)} collective-permute-done((f32[80,128]{1,0:T(8,128)S(1)}, f32[80,128]{1,0:T(8,128)S(1)}, u32[]{:S(2)}, u32[]{:S(2)}) %collective-permute-start.14) | collective-permute-done | bytes 40992 | tf_op jit(solution)/shard_map/ppermute | solution.py:632
  56.8 0.9 %shard_map.144 = (f32[27,4,16]{2,1,0:T(4,128)}, f32[1,16]{1,0:T(1,128)}, f32[27,16,16]{2,1,0:T(8,128)}, f32[1,16]{1,0:T(1,128)}) custom-call(f32[80,128]{1,0:T(8,128)S(1)} %select_add_fusion.a_ref, f32[80,128]{1,0:T(8,128)S(1)} %collective-permute-done.14.b_ref), custom_call_target="tpu_custom_call" | custom-call | flops 100000 | bytes 100000 | tf_op jit(solution)/shard_map/pallas_call | solution.py:653
  (30 shorter events, 0.5 us)
Async XLA Ops:
  0.6 12.5 %copy-start = (bf16[16,8,8,128]{3,2,1,0:T(8,128)(2,1)S(1)}, bf16[16,8,8,128]{3,2,1,0:T(8,128)(2,1)}, u32[]{:S(2)}) copy-start(bf16[16,8,8,128]{3,2,1,0:T(8,128)(2,1)} %cot_ref.1) | copy-start | bytes 786436
  0.6 18.1 %copy-start.1 = (bf16[16,16,3,3,3]{1,0,4,3,2:T(8,128)(2,1)S(1)}, bf16[16,16,3,3,3]{1,0,4,3,2:T(8,128)(2,1)}, u32[]{:S(2)}) copy-start(bf16[16,16,3,3,3]{1,0,4,3,2:T(8,128)(2,1)} %param.15) | copy-start | bytes 41476
  0.7 18.1 %copy-start.2 = (bf16[16,4,3,3,3]{0,1,4,3,2:T(4,128)(2,1)S(1)}, bf16[16,4,3,3,3]{0,1,4,3,2:T(4,128)(2,1)}, u32[]{:S(2)}) copy-start(bf16[16,4,3,3,3]{0,1,4,3,2:T(4,128)(2,1)} %param.13) | copy-start | bytes 10372
  0.7 18.1 %copy-start.3 = (f32[16]{0:T(128)S(1)}, f32[16]{0:T(128)}, u32[]{:S(2)}) copy-start(f32[16]{0:T(128)} %param.14) | copy-start | bytes 196
  0.7 18.1 %copy-start.4 = (f32[16]{0:T(128)S(1)}, f32[16]{0:T(128)}, u32[]{:S(2)}) copy-start(f32[16]{0:T(128)} %param.16) | copy-start | bytes 196
  5.8 18.0 %all-to-all-start = ((s16[32,32,128]{2,1,0:T(8,128)(2,1)}), s16[32,32,128]{2,1,0:T(8,128)(2,1)S(1)}, u32[]{:S(2)}, u32[]{:S(2)}) async-start(s16[32,32,128]{2,1,0:T(8,128)(2,1)} %shard_map.136), calls=%async_computation | async-start | bytes 524288 | tf_op jit(solution)/shard_map/all_to_all | solution.py:539
  13.4 16.5 %collective-permute-start.2 = (bf16[32,1024]{1,0:T(8,128)(2,1)S(1)}, bf16[32,1024]{1,0:T(8,128)(2,1)S(1)}, u32[]{:S(2)}, u32[]{:S(2)}) collective-permute-start(bf16[32,1024]{1,0:T(8,128)(2,1)S(1)} %get-tuple-element.40), channel_id=1, source_target_pairs={{1,2},{2,1},{3,4},{4,3},{5,6},{6,5},{9,10},{10,9},{11,12},{12,11},... | collective-permute-start | bytes 196616 | tf_op jit(solution)/shard_map/ppermute | solution.py:532
  14.2 15.6 %collective-permute-start.3 = (bf16[32,1024]{1,0:T(8,128)(2,1)S(1)}, bf16[32,1024]{1,0:T(8,128)(2,1)S(1)}, u32[]{:S(2)}, u32[]{:S(2)}) collective-permute-start(bf16[32,1024]{1,0:T(8,128)(2,1)S(1)} %get-tuple-element.41), channel_id=1, source_target_pairs={{0,1},{1,0},{2,3},{3,2},{4,5},{5,4},{6,7},{7,6},{8,9},{9,8},{10,11... | collective-permute-start | bytes 196616 | tf_op jit(solution)/shard_map/ppermute | solution.py:532
  27.3 3.4 %collective-permute-start = (bf16[24,1152]{1,0:T(8,128)(2,1)S(1)}, bf16[24,1152]{1,0:T(8,128)(2,1)S(1)}, u32[]{:S(2)}, u32[]{:S(2)}) collective-permute-start(bf16[24,1152]{1,0:T(8,128)(2,1)S(1)} %get-tuple-element.36), channel_id=1, source_target_pairs={{0,8},{1,2},{2,1},{3,4},{4,3},{5,6},{6,5},{7,15},{8,0},{9,10},{10,... | collective-permute-start | bytes 165896 | tf_op jit(solution)/shard_map/ppermute | solution.py:535
  27.4 4.7 %collective-permute-start.1 = (bf16[24,1152]{1,0:T(8,128)(2,1)S(1)}, bf16[24,1152]{1,0:T(8,128)(2,1)S(1)}, u32[]{:S(2)}, u32[]{:S(2)}) collective-permute-start(bf16[24,1152]{1,0:T(8,128)(2,1)S(1)} %get-tuple-element.37), channel_id=1, source_target_pairs={{0,1},{1,0},{2,3},{3,2},{4,5},{5,4},{6,7},{7,6},{8,9},{9,8},{10,11... | collective-permute-start | bytes 165896 | tf_op jit(solution)/shard_map/ppermute | solution.py:536
  30.0 4.8 %collective-permute-start.6 = (bf16[192,256]{1,0:T(8,128)(2,1)S(1)}, bf16[192,256]{1,0:T(8,128)(2,1)S(1)}, u32[]{:S(2)}, u32[]{:S(2)}) collective-permute-start(bf16[192,256]{1,0:T(8,128)(2,1)S(1)} %get-tuple-element.45), channel_id=1, source_target_pairs={{0,1},{1,0},{2,3},{3,2},{4,5},{5,4},{6,7},{7,6},{8,16},{9,17},{10,... | collective-permute-start | bytes 294920 | tf_op jit(solution)/shard_map/ppermute | solution.py:535
  30.0 4.7 %collective-permute-start.7 = (bf16[192,256]{1,0:T(8,128)(2,1)S(1)}, bf16[192,256]{1,0:T(8,128)(2,1)S(1)}, u32[]{:S(2)}, u32[]{:S(2)}) collective-permute-start(bf16[192,256]{1,0:T(8,128)(2,1)S(1)} %get-tuple-element.46), channel_id=1, source_target_pairs={{0,8},{1,9},{2,10},{3,11},{4,12},{5,13},{6,14},{7,15},{8,0},{9,1},... | collective-permute-start | bytes 294920 | tf_op jit(solution)/shard_map/ppermute | solution.py:536
  32.2 5.0 %collective-permute-start.4 = (bf16[64,640]{1,0:T(8,128)(2,1)S(1)}, bf16[64,640]{1,0:T(8,128)(2,1)S(1)}, u32[]{:S(2)}, u32[]{:S(2)}) collective-permute-start(bf16[64,640]{1,0:T(8,128)(2,1)S(1)} %get-tuple-element.43), channel_id=1, source_target_pairs={{0,1},{1,0},{2,3},{3,2},{4,5},{5,4},{6,7},{7,6},{8,16},{9,17},{10,... | collective-permute-start | bytes 245768 | tf_op jit(solution)/shard_map/ppermute | solution.py:535
  34.8 2.4 %collective-permute-start.5 = (bf16[64,640]{1,0:T(8,128)(2,1)S(1)}, bf16[64,640]{1,0:T(8,128)(2,1)S(1)}, u32[]{:S(2)}, u32[]{:S(2)}) collective-permute-start(bf16[64,640]{1,0:T(8,128)(2,1)S(1)} %get-tuple-element.44), channel_id=1, source_target_pairs={{0,8},{1,9},{2,10},{3,11},{4,12},{5,13},{6,14},{7,15},{8,0},{9,1},... | collective-permute-start | bytes 245768 | tf_op jit(solution)/shard_map/ppermute | solution.py:536
  42.3 1.3 %collective-permute-start.8 = (f32[80,128]{1,0:T(8,128)S(1)}, f32[80,128]{1,0:T(8,128)S(1)}, u32[]{:S(2)}, u32[]{:S(2)}) collective-permute-start(f32[80,128]{1,0:T(8,128)S(1)} %get-tuple-element.56), channel_id=1, source_target_pairs={{0,8},{1,9},{2,10},{3,11},{4,12},{5,13},{6,14},{7,15},{8,0},{9,1},... | collective-permute-start | bytes 122888 | tf_op jit(solution)/shard_map/ppermute | solution.py:632
  43.6 5.0 %collective-permute-start.10 = (f32[80,128]{1,0:T(8,128)S(1)}, f32[80,128]{1,0:T(8,128)S(1)}, u32[]{:S(2)}, u32[]{:S(2)}) collective-permute-start(f32[80,128]{1,0:T(8,128)S(1)} %add.22), channel_id=1, source_target_pairs={{0,1},{1,0},{2,3},{3,2},{4,5},{5,4},{6,7},{7,6},{8,9},{9,8},{10,11... | collective-permute-start | bytes 122888 | tf_op jit(solution)/shard_map/ppermute | solution.py:632
  45.6 4.9 %collective-permute-start.11 = (f32[80,128]{1,0:T(8,128)S(1)}, f32[80,128]{1,0:T(8,128)S(1)}, u32[]{:S(2)}, u32[]{:S(2)}) collective-permute-start(f32[80,128]{1,0:T(8,128)S(1)} %add.22), channel_id=1, source_target_pairs={{0,17},{1,16},{2,19},{3,18},{4,21},{5,20},{6,23},{7,22},{8,25},{9,... | collective-permute-start | bytes 122888 | tf_op jit(solution)/shard_map/ppermute | solution.py:632
  45.6 4.9 %collective-permute-start.9 = (f32[80,128]{1,0:T(8,128)S(1)}, f32[80,128]{1,0:T(8,128)S(1)}, u32[]{:S(2)}, u32[]{:S(2)}) collective-permute-start(f32[80,128]{1,0:T(8,128)S(1)} %add.22), channel_id=1, source_target_pairs={{0,16},{1,17},{2,18},{3,19},{4,20},{5,21},{6,22},{7,23},{8,24},{9,... | collective-permute-start | bytes 122888 | tf_op jit(solution)/shard_map/ppermute | solution.py:632
  50.5 5.0 %collective-permute-start.12 = (f32[80,128]{1,0:T(8,128)S(1)}, f32[80,128]{1,0:T(8,128)S(1)}, u32[]{:S(2)}, u32[]{:S(2)}) collective-permute-start(f32[80,128]{1,0:T(8,128)S(1)} %add_add_fusion), channel_id=1, source_target_pairs={{0,4},{1,5},{2,6},{3,7},{4,0},{5,1},{6,2},{7,3},{8,10},{9,11},{10,... | collective-permute-start | bytes 122888 | tf_op jit(solution)/shard_map/ppermute | solution.py:636
  51.4 4.2 %collective-permute-start.13 = (f32[80,128]{1,0:T(8,128)S(1)}, f32[80,128]{1,0:T(8,128)S(1)}, u32[]{:S(2)}, u32[]{:S(2)}) collective-permute-start(f32[80,128]{1,0:T(8,128)S(1)} %add_add_fusion), channel_id=1, source_target_pairs={{0,1},{1,0},{2,3},{3,2},{4,5},{5,4},{6,7},{7,6},{8,14},{9,15},{10,... | collective-permute-start | bytes 122888 | tf_op jit(solution)/shard_map/ppermute | solution.py:636
  55.5 1.3 %collective-permute-start.14 = (f32[80,128]{1,0:T(8,128)S(1)}, f32[80,128]{1,0:T(8,128)S(1)}, u32[]{:S(2)}, u32[]{:S(2)}) collective-permute-start(f32[80,128]{1,0:T(8,128)S(1)} %select_add_fusion.a_ref), channel_id=1, source_target_pairs={{0,8},{1,9},{2,10},{3,11},{4,12},{5,13},{6,14},{7,15},{8,0},{9,1},... | collective-permute-start | bytes 122888 | tf_op jit(solution)/shard_map/ppermute | solution.py:632
